TPU v7x, 32 devices: a whole 2x2x4 slice. The times are simulated.
32 devices in a mesh: sp: 2 (over x), dp: 16 (over z, y, core).
Axes of the slice: x: 2, y: 2, z: 4, core: 2. Of those that a mesh axis runs over, the one named last changes fastest.
Arguments:
- inputs: bfloat16 [32, 8, 8, 8, 128], P('dp', 'sp'), may hold values from -6 to 6
- cotangent: bfloat16 [32, 8, 8, 8, 128], P('dp', 'sp'), may hold values from -6 to 6
- w_conv: bfloat16 [3456, 128], replicated, may hold values from -0.109375 to 0.109375
- w_down: bfloat16 [1024, 256], replicated, may hold values from -0.1875 to 0.1875
- w_up: bfloat16 [2048, 128], replicated, may hold values from -0.375 to 0.375
Outputs:
- grad_input: bfloat16 [32, 8, 8, 8, 128], P('dp', 'sp')
- weight_grads: float32 [966656], P('dp')
All inputs are finite; a program needn't handle non-finite values.
Results may differ from a plain program's by a relative error of at most 0.017.
Values may be sent and summed in bfloat16 or wider, within the bound.
No kernel may reach another device: no remote copies, remote signals or barrier semaphores. Data moves between devices by JAX's collectives and lax.ppermute only.
A program may use at most 64 MiB of HBM per device.

v0:
```python
import jax
import jax.numpy as jnp
from jax import lax
from jax.sharding import PartitionSpec as P


def extended(cells, sides, width):
    for axis, dim in sides:
        count = lax.axis_size(axis)
        ends = count - 1
        head = lax.slice_in_dim(cells, 0, width, axis=dim)
        tail = lax.slice_in_dim(cells, cells.shape[dim] - width, cells.shape[dim], axis=dim)
        cells = jnp.concatenate(
            [
                lax.ppermute(tail, axis, [(i, (i + 1) % count) for i in range(ends)]),
                cells,
                lax.ppermute(head, axis, [((i + 1) % count, i) for i in range(ends)]),
            ],
            axis=dim,
        )
    return cells


def silu_slope(pre_act):
    sigmoid_value = jax.nn.sigmoid(pre_act)
    return sigmoid_value * (1.0 + pre_act * (1.0 - sigmoid_value))


def unfold_taps(padded):
    first_size = padded.shape[1] - 2
    second_size = padded.shape[2] - 2
    third_size = padded.shape[3] - 2
    pieces = [
        padded[:, i : i + first_size, j : j + second_size, k : k + third_size, :]
        for i in range(3)
        for j in range(3)
        for k in range(3)
    ]
    stacked = jnp.concatenate(pieces, axis=-1)
    return stacked.reshape(-1, stacked.shape[-1])


def to_blocks(volume):
    shape = volume.shape
    folded = volume.reshape(
        shape[0], shape[1] // 2, 2, shape[2] // 2, 2, shape[3] // 2, 2, shape[4]
    )
    folded = folded.transpose(0, 1, 3, 5, 2, 4, 6, 7)
    return folded.reshape(-1, 8 * shape[4])


def from_blocks(blocked, shape):
    folded = blocked.reshape(
        shape[0], shape[1] // 2, shape[2] // 2, shape[3] // 2, 2, 2, 2, shape[4]
    )
    folded = folded.transpose(0, 1, 4, 2, 5, 3, 6, 7)
    return folded.reshape(shape)


def flip_taps(w_conv):
    width_in = w_conv.shape[1]
    return (
        w_conv.reshape(27, width_in, width_in)[::-1]
        .transpose(0, 2, 1)
        .reshape(27 * width_in, width_in)
    )


def deep_level(hidden, upstream, w_down, w_up):
    width_in = hidden.shape[-1]
    width_deep = w_down.shape[1]
    hid_blocks = to_blocks(hidden)
    up_blocks = to_blocks(upstream)
    pre_deep = jnp.dot(hid_blocks, w_down, preferred_element_type=jnp.float32)
    deep_act = jax.nn.silu(pre_deep).astype(jnp.bfloat16)
    w_up_back = (
        w_up.reshape(8, width_deep, width_in).transpose(0, 2, 1).reshape(8 * width_in, width_deep)
    )
    grad_act = jnp.dot(up_blocks, w_up_back, preferred_element_type=jnp.float32)
    grad_up = lax.dot_general(
        deep_act, up_blocks, (((0,), (0,)), ((), ())), preferred_element_type=jnp.float32
    )
    grad_up = (
        grad_up.reshape(width_deep, 8, width_in)
        .transpose(1, 0, 2)
        .reshape(8 * width_deep, width_in)
    )
    grad_deep = (grad_act * silu_slope(pre_deep)).astype(jnp.bfloat16)
    grad_down = lax.dot_general(
        hid_blocks, grad_deep, (((0,), (0,)), ((), ())), preferred_element_type=jnp.float32
    )
    back_blocks = jnp.dot(grad_deep, w_down.T, preferred_element_type=jnp.float32).astype(
        jnp.bfloat16
    )
    return (grad_down, grad_up, from_blocks(back_blocks, hidden.shape))


def per_device(inputs, cotangent, w_conv, w_down, w_up):
    width_in = w_conv.shape[1]
    edge_pad = ((0, 0), (0, 0), (1, 1), (1, 1), (0, 0))
    slab_in = extended(inputs, (("sp", 1),), 1)
    columns = unfold_taps(jnp.pad(slab_in, edge_pad))
    pre_conv = jnp.dot(columns, w_conv, preferred_element_type=jnp.float32)
    hidden = jax.nn.silu(pre_conv).astype(jnp.bfloat16).reshape(inputs.shape)
    hidden_crops, upstream_crops = (
        lax.all_to_all(hidden, "sp", split_axis=0, concat_axis=1, tiled=True),
        lax.all_to_all(cotangent, "sp", split_axis=0, concat_axis=1, tiled=True),
    )
    grad_down, grad_up, back_down = deep_level(hidden_crops, upstream_crops, w_down, w_up)
    back_slab = lax.all_to_all(back_down, "sp", split_axis=1, concat_axis=0, tiled=True)
    summed = cotangent.astype(jnp.float32).reshape(-1, width_in) + back_slab.astype(
        jnp.float32
    ).reshape(-1, width_in)
    grad_pre = (summed * silu_slope(pre_conv)).astype(jnp.bfloat16)
    grad_conv = lax.dot_general(
        columns, grad_pre, (((0,), (0,)), ((), ())), preferred_element_type=jnp.float32
    )
    padded_grad = extended(grad_pre.reshape(inputs.shape), (("sp", 1),), 1)
    grad_input = jnp.dot(
        unfold_taps(jnp.pad(padded_grad, edge_pad)),
        flip_taps(w_conv),
        preferred_element_type=jnp.float32,
    )
    grad_input = grad_input.astype(jnp.bfloat16).reshape(inputs.shape)
    local_sums = jnp.concatenate(
        [grad_conv.reshape(-1), grad_down.reshape(-1), grad_up.reshape(-1)]
    )
    within_group = lax.psum(local_sums.astype(jnp.bfloat16), "sp").astype(jnp.float32)
    grad_share = lax.psum_scatter(within_group, "dp", scatter_dimension=0, tiled=True)
    edge_cells = inputs.shape[2]
    crop_total = inputs.shape[0] * lax.axis_size("dp")
    norm_factor = 1.0 / jnp.sqrt(jnp.float32(crop_total * edge_cells * edge_cells * edge_cells))
    return (grad_input, grad_share * norm_factor)


def solution(mesh):
    return jax.shard_map(
        per_device,
        mesh=mesh,
        in_specs=(P("dp", "sp", None, None, None), P("dp", "sp", None, None, None), P(), P(), P()),
        out_specs=(P("dp", "sp", None, None, None), P("dp")),
        check_vma=False,
    )
```

profile of v0, /device:TPU:0, one launch (start us, length us, event | category | flops | bytes accessed | tf_op | source)
XLA Modules:
  0.0 214.3 jit_solution(3639191068369615893)
XLA Ops:
  7.2 0.9 fusion.25
  8.1 4.8 %collective-permute-start = (bf16[2,1,8,8,128]{4,3,2,1,0:T(8,128)(2,1)S(1)}, bf16[2,1,8,8,128]{4,3,2,1,0:T(8,128)(2,1)S(1)}, u32[]{:S(2)}, u32[]{:S(2)}) collective-permute-start(bf16[2,1,8,8,128]{4,3,2,1,0:T(8,128)(2,1)S(1)} %get-tuple-element.30), channel_id=1, source_target_pairs={{0,16},{1,17},{2,18},{3,19},{4,20},{5,21},{6,22},{7,23},{8,24},{9,... | collective-permute-start | bytes 98312 | tf_op jit(solution)/shard_map/ppermute | solution.py:15
  12.9 1.3 collective-permute-start.1
  14.2 3.9 %all-to-all-start = ((bf16[2,4,8,8,128]{4,3,2,1,0:T(8,128)(2,1)}), bf16[2,4,8,8,128]{4,3,2,1,0:T(8,128)(2,1)S(1)}, u32[]{:S(2)}, u32[]{:S(2)}) async-start(bf16[2,4,8,8,128]{4,3,2,1,0:T(8,128)(2,1)} %param.6), calls=%async_computation | async-start | bytes 262144 | tf_op jit(solution)/shard_map/all_to_all | solution.py:107
  18.1 0.6 collective-permute-done.1
  18.7 1.1 fusion.13
  20.0 1.0 fusion.19
  22.4 1.7 copy-done.1
  24.2 1.8 multiply_convert_fusion
  26.0 3.5 %all-to-all-start.1 = ((bf16[2,4,8,8,128]{4,3,2,1,0:T(8,128)(2,1)}), bf16[2,4,8,8,128]{4,3,2,1,0:T(8,128)(2,1)S(1)}, u32[]{:S(2)}, u32[]{:S(2)}) async-start(bf16[2,4,8,8,128]{4,3,2,1,0:T(8,128)(2,1)} %bitcast.7), calls=%async_computation.1 | async-start | bytes 262144 | tf_op jit(solution)/shard_map/all_to_all | solution.py:106
  29.6 1.0 copy.18
  30.6 1.3 copy.21
  32.0 0.6 dynamic-slice
  33.4 0.6 all-to-all-done.1
  34.4 0.3 convolution_convert_fusion.1
  34.7 1.2 fusion.2
  36.3 0.8 copy.20
  37.1 3.4 %all-to-all-start.2 = ((bf16[1,8,8,8,128]{4,3,2,0,1:T(8,128)(2,1)}), bf16[1,8,8,8,128]{4,3,2,0,1:T(8,128)(2,1)S(1)}, u32[]{:S(2)}, u32[]{:S(2)}) async-start(bf16[1,8,8,8,128]{4,3,2,0,1:T(8,128)(2,1)} %bitcast.11), calls=%async_computation.2 | async-start | bytes 262144 | tf_op jit(solution)/shard_map/all_to_all | solution.py:110
  40.5 0.3 fusion.1
  40.9 0.4 copy.24
  41.3 3.7 %all-to-all-done.2 = bf16[1,8,8,8,128]{4,3,2,0,1:T(8,128)(2,1)S(1)} async-done(((bf16[1,8,8,8,128]{4,3,2,0,1:T(8,128)(2,1)}), bf16[1,8,8,8,128]{4,3,2,0,1:T(8,128)(2,1)S(1)}, u32[]{:S(2)}, u32[]{:S(2)}) %all-to-all-start.2) | async-done | bytes 131104 | tf_op jit(solution)/shard_map/all_to_all | solution.py:110
  44.9 1.1 fusion.15
  46.0 3.1 %fusion = bf16[442368]{0:T(1024)(128)(2,1)S(1)} fusion(bf16[512,3456]{1,0:T(8,128)(2,1)} %bitcast.88, bf16[512,128]{1,0:T(8,128)(2,1)S(1)} %fusion.15), kind=kOutput, calls=%fused_computation.1 | convolution fusion | flops 453427200 | bytes 4554752 | tf_op jit(solution)/shard_map/dot_general | solution.py:115
  49.2 1.9 collective-permute-start.2
  51.1 1.3 collective-permute-start.3
  52.4 1.4 pad_maximum_fusion
  53.8 3.1 %collective-permute-done.3 = bf16[2,1,8,8,128]{4,3,2,1,0:T(8,128)(2,1)S(1)} collective-permute-done((bf16[2,1,8,8,128]{4,3,2,1,0:T(8,128)(2,1)S(1)}, bf16[2,1,8,8,128]{4,3,2,1,0:T(8,128)(2,1)S(1)}, u32[]{:S(2)}, u32[]{:S(2)}) %collective-permute-start.3) | collective-permute-done | bytes 32800 | tf_op jit(solution)/shard_map/ppermute | solution.py:17
  57.2 0.5 fusion.22
  58.8 1.7 convolution_convert_fusion.3
  60.6 55.1 %all-reduce.6.cloned.1.call-done = bf16[966656]{0:T(1024)(128)(2,1)} async-done(((bf16[966656]{0:T(1024)(128)(2,1)}), bf16[966656]{0:T(1024)(128)(2,1)}) %all-reduce.6.cloned.1.call-update) | async-done | bytes 1933328 | tf_op jit(solution)/shard_map/psum | solution.py:128
  115.7 90.0 %all-reduce.7 = f32[966656]{0:T(1024)} all-reduce(bf16[966656]{0:T(1024)(128)(2,1)} %all-reduce.6.cloned.1.call-done), channel_id=2, replica_groups=mesh['sp'=2,'dp'=16] {'dp'}, use_global_device_ids=true, to_apply=%region_1.2.clone | all-reduce | flops 966656 | bytes 5799936
  205.8 1.7 dynamic-slice_multiply_fusion
  (83 shorter events, 3.8 us)
Async XLA Ops:
  7.2 27.0 %copy-start = (bf16[1024,256]{1,0:T(8,128)(2,1)S(1)}, bf16[1024,256]{1,0:T(8,128)(2,1)}, u32[]{:S(2)}) copy-start(bf16[1024,256]{1,0:T(8,128)(2,1)} %param.8) | copy-start | bytes 1572868
  7.2 14.3 %copy-start.2 = (bf16[2,4,8,8,128]{4,3,2,1,0:T(8,128)(2,1)S(1)}, bf16[2,4,8,8,128]{4,3,2,1,0:T(8,128)(2,1)}, u32[]{:S(2)}) copy-start(bf16[2,4,8,8,128]{4,3,2,1,0:T(8,128)(2,1)} %param.5) | copy-start | bytes 393220
  8.1 10.1 %collective-permute-start = (bf16[2,1,8,8,128]{4,3,2,1,0:T(8,128)(2,1)S(1)}, bf16[2,1,8,8,128]{4,3,2,1,0:T(8,128)(2,1)S(1)}, u32[]{:S(2)}, u32[]{:S(2)}) collective-permute-start(bf16[2,1,8,8,128]{4,3,2,1,0:T(8,128)(2,1)S(1)} %get-tuple-element.30), channel_id=1, source_target_pairs={{0,16},{1,17},{2,18},{3,19},{4,20},{5,21},{6,22},{7,23},{8,24},{9,... | collective-permute-start | bytes 98312 | tf_op jit(solution)/shard_map/ppermute | solution.py:15
  12.9 5.8 %collective-permute-start.1 = (bf16[2,1,8,8,128]{4,3,2,1,0:T(8,128)(2,1)S(1)}, bf16[2,1,8,8,128]{4,3,2,1,0:T(8,128)(2,1)S(1)}, u32[]{:S(2)}, u32[]{:S(2)}) collective-permute-start(bf16[2,1,8,8,128]{4,3,2,1,0:T(8,128)(2,1)S(1)} %get-tuple-element.31), channel_id=1, source_target_pairs={{16,0},{17,1},{18,2},{19,3},{20,4},{21,5},{22,6},{23,7},{24,8},{25... | collective-permute-start | bytes 98312 | tf_op jit(solution)/shard_map/ppermute | solution.py:17
  14.2 11.8 %all-to-all-start = ((bf16[2,4,8,8,128]{4,3,2,1,0:T(8,128)(2,1)}), bf16[2,4,8,8,128]{4,3,2,1,0:T(8,128)(2,1)S(1)}, u32[]{:S(2)}, u32[]{:S(2)}) async-start(bf16[2,4,8,8,128]{4,3,2,1,0:T(8,128)(2,1)} %param.6), calls=%async_computation | async-start | bytes 262144 | tf_op jit(solution)/shard_map/all_to_all | solution.py:107
  19.8 4.4 %copy-start.3 = (bf16[3456,128]{1,0:T(8,128)(2,1)S(1)}, bf16[3456,128]{1,0:T(8,128)(2,1)}, u32[]{:S(2)}) copy-start(bf16[3456,128]{1,0:T(8,128)(2,1)} %param.7) | copy-start | bytes 2654212
  22.4 1.8 copy-start.1
  24.2 5.5 %copy-start.5 = (bf16[2048,128]{1,0:T(8,128)(2,1)S(1)}, bf16[2048,128]{1,0:T(8,128)(2,1)}, u32[]{:S(2)}) copy-start(bf16[2048,128]{1,0:T(8,128)(2,1)} %param.9) | copy-start | bytes 1572868
  26.0 6.0 %copy-start.6 = (u32[32]{0:T(128)S(1)}, u32[32]{0:T(128)}, u32[]{:S(2)}) copy-start(u32[32]{0:T(128)} %constant.20) | copy-start | bytes 388
  26.0 8.0 %all-to-all-start.1 = ((bf16[2,4,8,8,128]{4,3,2,1,0:T(8,128)(2,1)}), bf16[2,4,8,8,128]{4,3,2,1,0:T(8,128)(2,1)S(1)}, u32[]{:S(2)}, u32[]{:S(2)}) async-start(bf16[2,4,8,8,128]{4,3,2,1,0:T(8,128)(2,1)} %bitcast.7), calls=%async_computation.1 | async-start | bytes 262144 | tf_op jit(solution)/shard_map/all_to_all | solution.py:106
  31.9 13.0 %copy-start.4 = (bf16[2,4,8,8,128]{4,3,2,1,0:T(8,128)(2,1)S(1)}, bf16[2,4,8,8,128]{4,3,2,1,0:T(8,128)(2,1)}, u32[]{:S(2)}) copy-start(bf16[2,4,8,8,128]{4,3,2,1,0:T(8,128)(2,1)} %param.6) | copy-start | bytes 393220
  37.1 7.8 %all-to-all-start.2 = ((bf16[1,8,8,8,128]{4,3,2,0,1:T(8,128)(2,1)}), bf16[1,8,8,8,128]{4,3,2,0,1:T(8,128)(2,1)S(1)}, u32[]{:S(2)}, u32[]{:S(2)}) async-start(bf16[1,8,8,8,128]{4,3,2,0,1:T(8,128)(2,1)} %bitcast.11), calls=%async_computation.2 | async-start | bytes 262144 | tf_op jit(solution)/shard_map/all_to_all | solution.py:110
  40.5 75.2 %all-reduce.6.cloned.1.call-start = ((), (), s32[]{:S(2)}) async-start(), calls=%async_computation.3 | async-start | bytes 3866624 | tf_op jit(solution)/shard_map/psum | solution.py:128
  49.2 4.7 %collective-permute-start.2 = (bf16[2,1,8,8,128]{4,3,2,1,0:T(8,128)(2,1)S(1)}, bf16[2,1,8,8,128]{4,3,2,1,0:T(8,128)(2,1)S(1)}, u32[]{:S(2)}, u32[]{:S(2)}) collective-permute-start(bf16[2,1,8,8,128]{4,3,2,1,0:T(8,128)(2,1)S(1)} %get-tuple-element.28), channel_id=1, source_target_pairs={{0,16},{1,17},{2,18},{3,19},{4,20},{5,21},{6,22},{7,23},{8,24},{9,... | collective-permute-start | bytes 98312 | tf_op jit(solution)/shard_map/ppermute | solution.py:15
  51.1 5.8 %collective-permute-start.3 = (bf16[2,1,8,8,128]{4,3,2,1,0:T(8,128)(2,1)S(1)}, bf16[2,1,8,8,128]{4,3,2,1,0:T(8,128)(2,1)S(1)}, u32[]{:S(2)}, u32[]{:S(2)}) collective-permute-start(bf16[2,1,8,8,128]{4,3,2,1,0:T(8,128)(2,1)S(1)} %get-tuple-element.29), channel_id=1, source_target_pairs={{16,0},{17,1},{18,2},{19,3},{20,4},{21,5},{22,6},{23,7},{24,8},{25... | collective-permute-start | bytes 98312 | tf_op jit(solution)/shard_map/ppermute | solution.py:17
Sparse Core Ops, SparseCore 0:
  54.0 61.7 all-reduce.5
where the time goes:
time: 216 us; the launch traced here: 214 us
  blocking collectives  90 us (42%)
  waiting for transfers between devices  63 us (29%)
  starting transfers between devices  20.2 us (9%)
  between operations  15.3 us (7%)
  local copies, waits for them, and re-layouts  10.2 us (5%)
  matrix products  9.1 us (4%)
  other arithmetic  6.42 us (3%)
    unnamed x1, blocking collectives  90 us
    psum x1, waiting for transfers between devices, per_device(): lax.psum(local_sums.astype(jnp.bfloat16), 'sp').astype(jnp.float32)  55.1 us
    ppermute x2, starting transfers between devices, extended(): lax.ppermute(tail, axis, [(i, (i + 1) % count) for i in range(ends)])  6.74 us
    unnamed x66, local copies, waits for them, and re-layouts  5.03 us
  transfers between devices with their start and end apart: 8, of which 5 were waited for; matrix products, arithmetic and copies ran while one was open for 7% of the time, Pallas kernels for 0%

commit v1 on v0

--- a/solution.py
+++ b/solution.py
@@ -133,9 +133,101 @@
     return (grad_input, grad_share * norm_factor)
 
 
+def swap_x(value):
+    return lax.ppermute(value, "sp", [(0, 1), (1, 0)])
+
+
+def swap_dp(value, mask):
+    return lax.ppermute(value, "dp", [(i, i ^ mask) for i in range(16)])
+
+
+def pick(value, dim, index):
+    return lax.dynamic_index_in_dim(value, index, dim, keepdims=False)
+
+
+def sum_shares(mine, passed, scale):
+    at = lax.axis_index("dp")
+    side = lax.axis_index("sp")
+    row, near, far = (at >> 1) & 1, (at >> 2) & 1, (at >> 3) & 1
+
+    def chip_sum(z, y):
+        return pick(pick(mine, 1, z), 1, y).astype(jnp.float32) + pick(
+            pick(passed, 1, z), 1, y
+        ).astype(jnp.float32)
+
+    diagonal = swap_dp(chip_sum(1 - near, 1 - row).astype(jnp.bfloat16), 6)
+    along_y = swap_dp(chip_sum(near, 1 - row).astype(jnp.bfloat16), 2)
+    along_z = swap_dp(chip_sum(1 - near, row).astype(jnp.bfloat16), 4)
+    square = (
+        chip_sum(near, row)
+        + along_y.astype(jnp.float32)
+        + along_z.astype(jnp.float32)
+        + diagonal.astype(jnp.float32)
+    )
+    across = swap_dp(pick(square, 0, 1 - far).astype(jnp.bfloat16), 8)
+    total = (pick(square, 0, far) + across.astype(jnp.float32)).astype(jnp.bfloat16)
+    other = swap_x(total)
+    low = jnp.where(side == 0, total, other)
+    high = jnp.where(side == 0, other, total)
+    return low.astype(jnp.float32) * scale, high.astype(jnp.float32) * scale
+
+
+def per_device_pairs(inputs, cotangent, w_conv, w_down, w_up):
+    width_in = w_conv.shape[1]
+    side = lax.axis_index("sp")
+    other_in = swap_x(inputs)
+    other_up = swap_x(cotangent)
+
+    def whole(own, other):
+        low = jnp.where(side == 0, own, other)
+        high = jnp.where(side == 0, other, own)
+        return jnp.concatenate([low, high], axis=1)
+
+    volume = whole(inputs, other_in)
+    upstream = whole(cotangent, other_up)
+    edge_pad = ((0, 0), (1, 1), (1, 1), (1, 1), (0, 0))
+    columns = unfold_taps(jnp.pad(volume, edge_pad))
+    pre_conv = jnp.dot(columns, w_conv, preferred_element_type=jnp.float32)
+    hidden = jax.nn.silu(pre_conv).astype(jnp.bfloat16).reshape(volume.shape)
+    grad_down, grad_up, back_down = deep_level(hidden, upstream, w_down, w_up)
+    summed = upstream.astype(jnp.float32).reshape(-1, width_in) + back_down.astype(
+        jnp.float32
+    ).reshape(-1, width_in)
+    grad_pre = (summed * silu_slope(pre_conv)).astype(jnp.bfloat16)
+    grad_conv = lax.dot_general(
+        columns, grad_pre, (((0,), (0,)), ((), ())), preferred_element_type=jnp.float32
+    )
+    padded_grad = jnp.pad(grad_pre.reshape(volume.shape), edge_pad)
+    slab = lax.dynamic_slice_in_dim(
+        padded_grad, side * inputs.shape[1], inputs.shape[1] + 2, axis=1
+    )
+    grad_input = jnp.dot(
+        unfold_taps(slab), flip_taps(w_conv), preferred_element_type=jnp.float32
+    )
+    grad_input = grad_input.astype(jnp.bfloat16).reshape(inputs.shape)
+
+    lanes = 128
+    rows = jnp.concatenate(
+        [part.reshape(-1, lanes) for part in (grad_conv, grad_down, grad_up)]
+    ).astype(jnp.bfloat16)
+    shares = rows.reshape(16, -1, lanes)
+    per_share = shares.shape[1]
+    half = -(-per_share // 32) * 16
+    part = lax.dynamic_slice_in_dim(shares, side * (per_share - half), half, axis=1)
+    part = part.reshape(2, 2, 2, 2, half, lanes)
+    core = lax.axis_index("dp") & 1
+    passed = swap_dp(pick(part, 3, 1 - core), 1)
+    crop_total = inputs.shape[0] * lax.axis_size("dp")
+    scale = 1.0 / jnp.sqrt(jnp.float32(crop_total * inputs.shape[2] ** 3))
+    low, high = sum_shares(pick(part, 3, core), passed, scale)
+    grad_share = jnp.concatenate([low, high[2 * half - per_share :]]).reshape(-1)
+    return (grad_input, grad_share)
+
+
 def solution(mesh):
+    pairs = dict(mesh.shape) == {"sp": 2, "dp": 16}
     return jax.shard_map(
-        per_device,
+        per_device_pairs if pairs else per_device,
         mesh=mesh,
         in_specs=(P("dp", "sp", None, None, None), P("dp", "sp", None, None, None), P(), P(), P()),
         out_specs=(P("dp", "sp", None, None, None), P("dp")),

time: 216 us -> 47.4 us (0.22)
  blocking collectives: 90 us -> 0 us
  waiting for transfers between devices: 63 us -> 11.8 us
  between operations: 15.3 us -> 1.22 us
  starting transfers between devices: 20.2 us -> 11.1 us
  other arithmetic: 6.42 us -> 1.48 us
    unnamed x1 -> x0, blocking collectives: 90 us -> none
    psum x1 -> x0, waiting for transfers between devices: 55.1 us -> none  [per_device(): lax.psum(local_sums.astype(jnp.bfloat16), 'sp').astype(jnp.float32)]
    all_to_all x3 -> x0, starting transfers between devices: 10.8 us -> none  [the longest x1 3.92 us: per_device(): lax.all_to_all(cotangent, 'sp', split_axis=0, concat_axis=1, tiled=True)]
    ppermute x4 -> x8, waiting for transfers between devices: 3.65 us -> 11.8 us  [the longest x5 8.49 us: swap_dp(): return lax.ppermute(value, 'dp', [(i, i ^ mask) for i in range(16)])]
    all_to_all x3 -> x0, waiting for transfers between devices: 4.25 us -> none  [the longest x1 3.66 us: per_device(): lax.all_to_all(back_down, 'sp', split_axis=1, concat_axis=0, tiled=True)]
    concatenate x4 -> x3, other arithmetic: 2.7 us -> 0.18 us  [the longest x1 0.13 us: per_device_pairs(): jnp.concatenate([part.reshape(-1, lanes) for part in (grad_conv, grad_dow...]
    ppermute x4 -> x8, starting transfers between devices: 9.33 us -> 11.1 us  [the longest x5 6.43 us: swap_dp(): return lax.ppermute(value, 'dp', [(i, i ^ mask) for i in range(16)])]
    unnamed x66 -> x63, local copies, waits for them, and re-layouts: 5.03 us -> 5.19 us
  transfers between devices with their start and end apart: 8 -> 8, of which waited for: 5 -> 7; matrix products, arithmetic and copies ran while one was open for 7% -> 17% of each run, Pallas kernels for 0% -> 0%
where the time goes in v1:
time: 47.4 us; the launch traced here: 47.2 us
  waiting for transfers between devices  11.8 us (25%)
  local copies, waits for them, and re-layouts  11.4 us (24%)
  starting transfers between devices  11.1 us (23%)
  matrix products  10.3 us (22%)
  other arithmetic  1.48 us (3%)
  between operations  1.22 us (3%)
    ppermute x5, waiting for transfers between devices, swap_dp(): return lax.ppermute(value, 'dp', [(i, i ^ mask) for i in range(16)])  8.49 us
    ppermute x5, starting transfers between devices, swap_dp(): return lax.ppermute(value, 'dp', [(i, i ^ mask) for i in range(16)])  6.43 us
    unnamed x63, local copies, waits for them, and re-layouts  5.19 us
    dot_general x1, matrix products, per_device_pairs(): lax.dot_general(columns, grad_pre, (((0,), (0,)), ((), ())), preferred_el...  5.07 us
    ppermute x3, starting transfers between devices, swap_x(): return lax.ppermute(value, 'sp', [(0, 1), (1, 0)])  4.64 us
    ppermute x3, waiting for transfers between devices, swap_x(): return lax.ppermute(value, 'sp', [(0, 1), (1, 0)])  3.28 us
    transpose x2, local copies, waits for them, and re-layouts, flip_taps(): return w_conv.reshape(27, width_in, width_in)[::-1].transpose(0, 2, 1).re...  2.86 us
    dot_general x1, matrix products, per_device_pairs(): pre_conv = jnp.dot(columns, w_conv, preferred_element_type=jnp.float32)  2.02 us
  transfers between devices with their start and end apart: 8, of which 7 were waited for; matrix products, arithmetic and copies ran while one was open for 17% of the time, Pallas kernels for 0%

profile of v1, /device:TPU:0, one launch (start us, length us, event | category | flops | bytes accessed | tf_op | source)
XLA Modules:
  0.0 47.2 jit_solution(16788721762018388641)
XLA Ops:
  0.7 3.0 %collective-permute-start = (bf16[2,4,8,8,128]{4,3,2,1,0:T(8,128)(2,1)}, bf16[2,4,8,8,128]{4,3,2,1,0:T(8,128)(2,1)S(1)}, u32[]{:S(2)}, u32[]{:S(2)}) collective-permute-start(bf16[2,4,8,8,128]{4,3,2,1,0:T(8,128)(2,1)} %param.6), channel_id=1, source_target_pairs={{0,16},{16,0},{1,17},{17,1},{2,18},{18,2},{3,19},{19,3},{4,20},{20... | collective-permute-start | bytes 393224 | tf_op jit(solution)/shard_map/ppermute | solution.py:137
  3.7 1.2 %copy.23 = bf16[8,128,256]{2,1,0:T(8,128)(2,1)S(1)} copy(bf16[8,128,256]{1,2,0:T(8,128)(2,1)} %bitcast.131) | data formatting | bytes 1048576 | tf_op jit(solution)/shard_map/transpose | solution.py:77
  5.0 1.2 %reverse_bitcast_fusion = bf16[27,128,128]{1,2,0:T(8,128)(2,1)S(1)} fusion(bf16[27,128,128]{2,1,0:T(8,128)(2,1)} %bitcast.129), kind=kLoop, calls=%fused_computation.62 | loop fusion | bytes 1769472 | tf_op jit(solution)/shard_map/transpose | solution.py:64
  6.3 1.6 %copy.26 = bf16[27,128,128]{2,1,0:T(8,128)(2,1)} copy(bf16[27,128,128]{1,2,0:T(8,128)(2,1)S(1)} %reverse_bitcast_fusion) | data formatting | bytes 1769472 | tf_op jit(solution)/shard_map/transpose | solution.py:64
  7.9 0.3 collective-permute-done
  8.2 2.0 %collective-permute-done.1 = bf16[2,4,8,8,128]{4,3,2,1,0:T(8,128)(2,1)S(1)} collective-permute-done((bf16[2,4,8,8,128]{4,3,2,1,0:T(8,128)(2,1)}, bf16[2,4,8,8,128]{4,3,2,1,0:T(8,128)(2,1)S(1)}, u32[]{:S(2)}, u32[]{:S(2)}) %collective-permute-start.1) | collective-permute-done | bytes 131104 | tf_op jit(solution)/shard_map/ppermute | solution.py:137
  12.9 2.0 %multiply_convert_fusion = (bf16[1024,128]{1,0:T(8,128)(2,1)S(1)}, f32[1024,128]{1,0:T(8,128)S(1)}) fusion(bf16[1024,3456]{1,0:T(8,128)(2,1)S(1)} %bitcast.134, bf16[3456,128]{1,0:T(8,128)(2,1)S(1)} %copy-done.1), kind=kOutput, calls=%fused_computation.66 | convolution fusion | flops 906625024 | bytes 8749056 | tf_op jit(solution)/shard_map/dot_general | solution.py:190
  15.0 0.2 copy.41
  15.1 0.6 %copy-done.5 = bf16[2,8,8,8,3456]{4,3,2,1,0:T(8,128)(2,1)} copy-done((bf16[2,8,8,8,3456]{4,3,2,1,0:T(8,128)(2,1)}, bf16[2,8,8,8,3456]{4,3,2,1,0:T(8,128)(2,1)S(1)}, u32[]{:S(2)}) %copy-start.5) | copy-done | bytes 7077912
  16.0 0.2 copy.42
  16.2 0.2 reshape.106
  16.4 0.2 fusion.67
  16.6 0.2 fusion.1
  16.9 0.3 fusion
  17.2 0.3 convolution_convert_fusion.2
  17.5 0.4 reshape.130
  18.0 0.2 copy.25
  18.2 0.2 fusion.3
  18.4 5.1 %convolution_convert_fusion = bf16[3456,128]{1,0:T(8,128)(2,1)S(1)} fusion(bf16[1024,3456]{1,0:T(8,128)(2,1)} %bitcast.135, bf16[1024,128]{1,0:T(8,128)(2,1)S(1)} %fusion.3), kind=kOutput, calls=%fused_computation.53 | convolution fusion | flops 906412032 | bytes 8224768 | tf_op jit(solution)/shard_map/dot_general | solution.py:197
  23.5 0.2 reshape.116
  23.9 0.3 convolution_convert_fusion.1
  26.9 1.8 %collective-permute-start.3 = (bf16[2,240,128]{2,1,0:T(8,128)(2,1)S(1)}, bf16[2,240,128]{2,1,0:T(8,128)(2,1)S(1)}, u32[]{:S(2)}, u32[]{:S(2)}) collective-permute-start(bf16[2,240,128]{2,1,0:T(8,128)(2,1)S(1)} %get-tuple-element.2), channel_id=1, source_target_pairs={{0,2},{1,3},{2,0},{3,1},{4,6},{5,7},{6,4},{7,5},{8,10},{9,11},{10,... | collective-permute-start | bytes 368648 | tf_op jit(solution)/shard_map/ppermute | solution.py:141
  28.7 1.6 %collective-permute-start.4 = (bf16[2,240,128]{2,1,0:T(8,128)(2,1)S(1)}, bf16[2,240,128]{2,1,0:T(8,128)(2,1)S(1)}, u32[]{:S(2)}, u32[]{:S(2)}) collective-permute-start(bf16[2,240,128]{2,1,0:T(8,128)(2,1)S(1)} %get-tuple-element.4), channel_id=1, source_target_pairs={{0,4},{1,5},{2,6},{3,7},{4,0},{5,1},{6,2},{7,3},{8,12},{9,13},{10,... | collective-permute-start | bytes 368648 | tf_op jit(solution)/shard_map/ppermute | solution.py:141
  30.6 2.1 %collective-permute-done.3 = bf16[2,240,128]{2,1,0:T(8,128)(2,1)S(1)} collective-permute-done((bf16[2,240,128]{2,1,0:T(8,128)(2,1)S(1)}, bf16[2,240,128]{2,1,0:T(8,128)(2,1)S(1)}, u32[]{:S(2)}, u32[]{:S(2)}) %collective-permute-start.3) | collective-permute-done | bytes 122912 | tf_op jit(solution)/shard_map/ppermute | solution.py:141
  32.7 2.2 %collective-permute-done.4 = bf16[2,240,128]{2,1,0:T(8,128)(2,1)S(1)} collective-permute-done((bf16[2,240,128]{2,1,0:T(8,128)(2,1)S(1)}, bf16[2,240,128]{2,1,0:T(8,128)(2,1)S(1)}, u32[]{:S(2)}, u32[]{:S(2)}) %collective-permute-start.4) | collective-permute-done | bytes 122912 | tf_op jit(solution)/shard_map/ppermute | solution.py:141
  34.9 1.7 %collective-permute-done.5 = bf16[2,240,128]{2,1,0:T(8,128)(2,1)S(1)} collective-permute-done((bf16[2,240,128]{2,1,0:T(8,128)(2,1)S(1)}, bf16[2,240,128]{2,1,0:T(8,128)(2,1)S(1)}, u32[]{:S(2)}, u32[]{:S(2)}) %collective-permute-start.5) | collective-permute-done | bytes 122912 | tf_op jit(solution)/shard_map/ppermute | solution.py:141
  36.7 2.8 %collective-permute-start.6 = (bf16[240,128]{1,0:T(8,128)(2,1)S(1)}, bf16[240,128]{1,0:T(8,128)(2,1)S(1)}, u32[]{:S(2)}, u32[]{:S(2)}) collective-permute-start(bf16[240,128]{1,0:T(8,128)(2,1)S(1)} %fusion.65), channel_id=1, source_target_pairs={{0,8},{1,9},{2,10},{3,11},{4,12},{5,13},{6,14},{7,15},{8,0},{9,1},... | collective-permute-start | bytes 184328 | tf_op jit(solution)/shard_map/ppermute | solution.py:141
  39.6 2.5 %collective-permute-done.6 = bf16[240,128]{1,0:T(8,128)(2,1)S(1)} collective-permute-done((bf16[240,128]{1,0:T(8,128)(2,1)S(1)}, bf16[240,128]{1,0:T(8,128)(2,1)S(1)}, u32[]{:S(2)}, u32[]{:S(2)}) %collective-permute-start.6) | collective-permute-done | bytes 61472 | tf_op jit(solution)/shard_map/ppermute | solution.py:141
  42.1 1.6 %collective-permute-start.7 = (bf16[240,128]{1,0:T(8,128)(2,1)S(1)}, bf16[240,128]{1,0:T(8,128)(2,1)S(1)}, u32[]{:S(2)}, u32[]{:S(2)}) collective-permute-start(bf16[240,128]{1,0:T(8,128)(2,1)S(1)} %fusion.63), channel_id=1, source_target_pairs={{0,16},{16,0},{1,17},{17,1},{2,18},{18,2},{3,19},{19,3},{4,20},{20... | collective-permute-start | bytes 184328 | tf_op jit(solution)/shard_map/ppermute | solution.py:137
  43.7 1.7 %convolution_convert_fusion.4 = bf16[512,128]{1,0:T(8,128)(2,1)} fusion(bf16[512,3456]{1,0:T(8,128)(2,1)S(1)} %bitcast.136, bf16[3456,128]{1,0:T(8,128)(2,1)S(1)} %bitcast.130), kind=kOutput, calls=%fused_computation.59 | convolution fusion | flops 453050368 | bytes 4554752 | tf_op jit(solution)/shard_map/dot_general | solution.py:204
  45.4 1.0 %collective-permute-done.7 = bf16[240,128]{1,0:T(8,128)(2,1)S(1)} collective-permute-done((bf16[240,128]{1,0:T(8,128)(2,1)S(1)}, bf16[240,128]{1,0:T(8,128)(2,1)S(1)}, u32[]{:S(2)}, u32[]{:S(2)}) %collective-permute-start.7) | collective-permute-done | bytes 61472 | tf_op jit(solution)/shard_map/ppermute | solution.py:137
  46.4 0.7 %maximum_bitcast_fusion = f32[60416]{0:T(1024)} fusion(f32[232,128]{1,0:T(8,128)S(1)} %convert_multiply_fusion.1, f32[240,128]{1,0:T(8,128)S(1)} %convert_multiply_fusion), kind=kLoop, calls=%fused_computation.109 | loop fusion | flops 60416 | bytes 483328 | tf_op jit(solution)/shard_map/reshape | solution.py:223
  (83 shorter events, 6.0 us)
Async XLA Ops:
  0.6 15.7 %copy-start = (bf16[1024,256]{1,0:T(8,128)(2,1)S(1)}, bf16[1024,256]{1,0:T(8,128)(2,1)}, u32[]{:S(2)}) copy-start(bf16[1024,256]{1,0:T(8,128)(2,1)} %param.8) | copy-start | bytes 1572868
  0.6 9.5 %copy-start.4 = (bf16[2,4,8,8,128]{4,3,2,1,0:T(8,128)(2,1)S(1)}, bf16[2,4,8,8,128]{4,3,2,1,0:T(8,128)(2,1)}, u32[]{:S(2)}) copy-start(bf16[2,4,8,8,128]{4,3,2,1,0:T(8,128)(2,1)} %param.6) | copy-start | bytes 393220
  0.7 9.5 %copy-start.3 = (bf16[2,4,8,8,128]{4,3,2,1,0:T(8,128)(2,1)S(1)}, bf16[2,4,8,8,128]{4,3,2,1,0:T(8,128)(2,1)}, u32[]{:S(2)}) copy-start(bf16[2,4,8,8,128]{4,3,2,1,0:T(8,128)(2,1)} %param.5) | copy-start | bytes 393220
  0.7 7.5 %collective-permute-start = (bf16[2,4,8,8,128]{4,3,2,1,0:T(8,128)(2,1)}, bf16[2,4,8,8,128]{4,3,2,1,0:T(8,128)(2,1)S(1)}, u32[]{:S(2)}, u32[]{:S(2)}) collective-permute-start(bf16[2,4,8,8,128]{4,3,2,1,0:T(8,128)(2,1)} %param.6), channel_id=1, source_target_pairs={{0,16},{16,0},{1,17},{17,1},{2,18},{18,2},{3,19},{19,3},{4,20},{20... | collective-permute-start | bytes 393224 | tf_op jit(solution)/shard_map/ppermute | solution.py:137
  3.7 6.5 %collective-permute-start.1 = (bf16[2,4,8,8,128]{4,3,2,1,0:T(8,128)(2,1)}, bf16[2,4,8,8,128]{4,3,2,1,0:T(8,128)(2,1)S(1)}, u32[]{:S(2)}, u32[]{:S(2)}) collective-permute-start(bf16[2,4,8,8,128]{4,3,2,1,0:T(8,128)(2,1)} %param.5), channel_id=1, source_target_pairs={{0,16},{16,0},{1,17},{17,1},{2,18},{18,2},{3,19},{19,3},{4,20},{20... | collective-permute-start | bytes 393224 | tf_op jit(solution)/shard_map/ppermute | solution.py:137
  11.4 1.5 %copy-start.1 = (bf16[3456,128]{1,0:T(8,128)(2,1)S(1)}, bf16[3456,128]{1,0:T(8,128)(2,1)}, u32[]{:S(2)}) copy-start(bf16[3456,128]{1,0:T(8,128)(2,1)} %param.7) | copy-start | bytes 2654212
  12.9 2.9 %copy-start.5 = (bf16[2,8,8,8,3456]{4,3,2,1,0:T(8,128)(2,1)}, bf16[2,8,8,8,3456]{4,3,2,1,0:T(8,128)(2,1)S(1)}, u32[]{:S(2)}) copy-start(bf16[2,8,8,8,3456]{4,3,2,1,0:T(8,128)(2,1)S(1)} %fusion.29) | copy-start | bytes 21233668
  24.5 2.3 %collective-permute-start.2 = (bf16[2,2,2,240,128]{4,3,0,2,1:T(8,128)(2,1)S(1)}, bf16[2,2,2,240,128]{4,3,0,2,1:T(8,128)(2,1)S(1)}, u32[]{:S(2)}, u32[]{:S(2)}) collective-permute-start(bf16[2,2,2,240,128]{4,3,0,2,1:T(8,128)(2,1)S(1)} %copy_bitcast_fusion), channel_id=1, source_target_pairs={{0,1},{1,0},{2,3},{3,2},{4,5},{5,4},{6,7},{7,6},{8,9},{9,8},{10,11... | collective-permute-start | bytes 1474568 | tf_op jit(solution)/shard_map/ppermute | solution.py:141
  25.7 18.0 %copy-start.2 = (bf16[27,128,128]{2,1,0:T(8,128)(2,1)S(1)}, bf16[27,128,128]{2,1,0:T(8,128)(2,1)}, u32[]{:S(2)}) copy-start(bf16[27,128,128]{2,1,0:T(8,128)(2,1)} %copy.26) | copy-start | bytes 2654212
  26.9 5.8 %collective-permute-start.3 = (bf16[2,240,128]{2,1,0:T(8,128)(2,1)S(1)}, bf16[2,240,128]{2,1,0:T(8,128)(2,1)S(1)}, u32[]{:S(2)}, u32[]{:S(2)}) collective-permute-start(bf16[2,240,128]{2,1,0:T(8,128)(2,1)S(1)} %get-tuple-element.2), channel_id=1, source_target_pairs={{0,2},{1,3},{2,0},{3,1},{4,6},{5,7},{6,4},{7,5},{8,10},{9,11},{10,... | collective-permute-start | bytes 368648 | tf_op jit(solution)/shard_map/ppermute | solution.py:141
  28.7 6.2 %collective-permute-start.4 = (bf16[2,240,128]{2,1,0:T(8,128)(2,1)S(1)}, bf16[2,240,128]{2,1,0:T(8,128)(2,1)S(1)}, u32[]{:S(2)}, u32[]{:S(2)}) collective-permute-start(bf16[2,240,128]{2,1,0:T(8,128)(2,1)S(1)} %get-tuple-element.4), channel_id=1, source_target_pairs={{0,4},{1,5},{2,6},{3,7},{4,0},{5,1},{6,2},{7,3},{8,12},{9,13},{10,... | collective-permute-start | bytes 368648 | tf_op jit(solution)/shard_map/ppermute | solution.py:141
  30.3 6.3 %collective-permute-start.5 = (bf16[2,240,128]{2,1,0:T(8,128)(2,1)S(1)}, bf16[2,240,128]{2,1,0:T(8,128)(2,1)S(1)}, u32[]{:S(2)}, u32[]{:S(2)}) collective-permute-start(bf16[2,240,128]{2,1,0:T(8,128)(2,1)S(1)} %get-tuple-element.3), channel_id=1, source_target_pairs={{0,6},{1,7},{2,4},{3,5},{4,2},{5,3},{6,0},{7,1},{8,14},{9,15},{10,... | collective-permute-start | bytes 368648 | tf_op jit(solution)/shard_map/ppermute | solution.py:141
  36.7 5.4 %collective-permute-start.6 = (bf16[240,128]{1,0:T(8,128)(2,1)S(1)}, bf16[240,128]{1,0:T(8,128)(2,1)S(1)}, u32[]{:S(2)}, u32[]{:S(2)}) collective-permute-start(bf16[240,128]{1,0:T(8,128)(2,1)S(1)} %fusion.65), channel_id=1, source_target_pairs={{0,8},{1,9},{2,10},{3,11},{4,12},{5,13},{6,14},{7,15},{8,0},{9,1},... | collective-permute-start | bytes 184328 | tf_op jit(solution)/shard_map/ppermute | solution.py:141
  42.1 4.3 %collective-permute-start.7 = (bf16[240,128]{1,0:T(8,128)(2,1)S(1)}, bf16[240,128]{1,0:T(8,128)(2,1)S(1)}, u32[]{:S(2)}, u32[]{:S(2)}) collective-permute-start(bf16[240,128]{1,0:T(8,128)(2,1)S(1)} %fusion.63), channel_id=1, source_target_pairs={{0,16},{16,0},{1,17},{17,1},{2,18},{18,2},{3,19},{19,3},{4,20},{20... | collective-permute-start | bytes 184328 | tf_op jit(solution)/shard_map/ppermute | solution.py:137

commit v2 on v0

--- a/solution.py
+++ b/solution.py
@@ -1,6 +1,8 @@
 import jax
 import jax.numpy as jnp
 from jax import lax
+from jax.experimental import pallas as pl
+from jax.experimental.pallas import tpu as pltpu
 from jax.sharding import PartitionSpec as P
 
 
@@ -133,9 +135,300 @@
     return (grad_input, grad_share * norm_factor)
 
 
+def swap_x(value):
+    return lax.ppermute(value, "sp", [(0, 1), (1, 0)])
+
+
+def swap_dp(value, mask):
+    return lax.ppermute(value, "dp", [(i, i ^ mask) for i in range(16)])
+
+
+def pick(value, dim, index):
+    return lax.dynamic_index_in_dim(value, index, dim, keepdims=False)
+
+
+def sum_shares(mine, passed, scale):
+    at = lax.axis_index("dp")
+    side = lax.axis_index("sp")
+    row, near, far = (at >> 1) & 1, (at >> 2) & 1, (at >> 3) & 1
+
+    def chip_sum(z, y):
+        return pick(pick(mine, 1, z), 1, y).astype(jnp.float32) + pick(
+            pick(passed, 1, z), 1, y
+        ).astype(jnp.float32)
+
+    diagonal = swap_dp(chip_sum(1 - near, 1 - row).astype(jnp.bfloat16), 6)
+    along_y = swap_dp(chip_sum(near, 1 - row).astype(jnp.bfloat16), 2)
+    along_z = swap_dp(chip_sum(1 - near, row).astype(jnp.bfloat16), 4)
+    square = (
+        chip_sum(near, row)
+        + along_y.astype(jnp.float32)
+        + along_z.astype(jnp.float32)
+        + diagonal.astype(jnp.float32)
+    )
+    across = swap_dp(pick(square, 0, 1 - far).astype(jnp.bfloat16), 8)
+    total = (pick(square, 0, far) + across.astype(jnp.float32)).astype(jnp.bfloat16)
+    other = swap_x(total)
+    low = jnp.where(side == 0, total, other)
+    high = jnp.where(side == 0, other, total)
+    return low.astype(jnp.float32) * scale, high.astype(jnp.float32) * scale
+
+
+LANES = 128
+VMEM = pl.BlockSpec(memory_space=pltpu.VMEM)
+
+
+def load_crops(own_ref, other_ref, natural_ref, side):
+    depth = own_ref.shape[1]
+    for ref, first in ((own_ref, side * depth), (other_ref, (1 - side) * depth)):
+        for crop in range(2):
+            natural_ref[pl.ds(first, depth), :, 8 * crop : 8 * crop + 8, :] = ref[crop].astype(
+                jnp.float32
+            )
+
+
+def fill_taps(taps_ref, even, odd):
+    planes = even.shape[0]
+    kk = lax.broadcasted_iota(jnp.int32, even.shape, 2) % 4
+    before = jnp.where(kk == 0, 0.0, pltpu.roll(odd, 1, 2))
+    after = jnp.where(kk == 3, 0.0, pltpu.roll(even, 7, 2))
+    rows = pl.ds(1, 8)
+    for tap, (low, high) in enumerate(((before, even), (even, odd), (odd, after))):
+        taps_ref[1 : 1 + planes, rows, :, tap * LANES : (tap + 1) * LANES] = jnp.concatenate(
+            [low, high], axis=2
+        ).astype(jnp.bfloat16)
+
+
+def clear_rim(taps_ref, with_planes):
+    planes, rows, tile, lanes = taps_ref.shape
+    row = jnp.zeros((planes, tile, lanes), jnp.bfloat16)
+    taps_ref[:, 0] = row
+    taps_ref[:, rows - 1] = row
+    if with_planes:
+        plane = jnp.zeros((rows, tile, lanes), jnp.bfloat16)
+        taps_ref[0] = plane
+        taps_ref[planes - 1] = plane
+
+
+def across(tile):
+    return jnp.concatenate(tile, axis=-1)
+
+
+def forward_kernel(own_ref, other_ref, w_ref, pre_ref, turned_ref, natural_ref, taps_ref):
+    side = lax.axis_index("sp")
+    load_crops(own_ref, other_ref, natural_ref, side)
+    even = natural_ref[:, :, pl.ds(0, 8, stride=2), :]
+    odd = natural_ref[:, :, pl.ds(1, 8, stride=2), :]
+    clear_rim(taps_ref, False)
+    fill_taps(taps_ref, even, odd)
+    wide = 3 * LANES
+    planes = even.shape[0]
+    size = planes * 128
+    centre = taps_ref[1 : 1 + planes, 1:9, :, LANES : 2 * LANES].reshape(size, LANES)
+    turned_ref[...] = centre.astype(jnp.float32).T.astype(jnp.bfloat16)
+    cells = across(
+        [taps_ref[1 : 1 + planes, j : j + 8].reshape(size, wide) for j in range(3)]
+    )
+
+    def weights(i):
+        return w_ref[i * 3 * wide : (i + 1) * 3 * wide, :]
+
+    first = jnp.dot(
+        cells, across([weights(0), weights(1)]), preferred_element_type=jnp.float32
+    )
+    last = jnp.dot(cells, weights(2), preferred_element_type=jnp.float32)
+    rim = jnp.zeros((128, LANES), jnp.float32)
+    pre = (
+        jnp.concatenate([rim, first[:-128, :LANES]])
+        + first[:, LANES:]
+        + jnp.concatenate([last[128:], rim])
+    )
+    pre_ref[...] = pre.reshape(pre_ref.shape)
+
+
+def against(a, b):
+    return lax.dot_general(
+        a, b, (((1,), (1,)), ((), ())), preferred_element_type=jnp.float32
+    )
+
+
+def backward_kernel(
+    pre_ref,
+    turned_ref,
+    own_ref,
+    other_ref,
+    w_down_ref,
+    w_up_ref,
+    mine_ref,
+    passed_ref,
+    slab_ref,
+    natural_ref,
+    folded_ref,
+    taps_ref,
+    rows_ref,
+):
+    side = lax.axis_index("sp")
+    core = lax.axis_index("dp") % 2
+    load_crops(own_ref, other_ref, natural_ref, side)
+    up = [
+        natural_ref[:, :, pl.ds(parity, 8, stride=2), :].reshape(4, 2, 4, 2, 8, LANES)
+        for parity in range(2)
+    ]
+    places = [(i, j, k) for i in range(2) for j in range(2) for k in range(2)]
+
+    def block(i, j, k):
+        return pre_ref[:, i, :, j, k].reshape(128, LANES)
+
+    def up_block(i, j, k):
+        return up[k][:, i, :, j].reshape(128, LANES)
+
+    hidden = across([jax.nn.silu(block(*at)).astype(jnp.bfloat16) for at in places])
+    upstream = across([up_block(*at).astype(jnp.bfloat16) for at in places])
+    pre_deep = jnp.dot(hidden, w_down_ref[...], preferred_element_type=jnp.float32)
+    deep = pre_deep.shape[1]
+    grad_act = against(
+        upstream, across([w_up_ref[tap * deep : (tap + 1) * deep, :] for tap in range(8)])
+    )
+    grad_deep = (grad_act * silu_slope(pre_deep)).astype(jnp.bfloat16)
+    back = against(grad_deep, w_down_ref[...]).astype(jnp.bfloat16).astype(jnp.float32)
+    for tap, at in enumerate(places):
+        i, j, k = at
+        summed = up_block(*at) + back[:, tap * LANES : (tap + 1) * LANES]
+        folded_ref[:, i, :, j, k] = (summed * silu_slope(block(*at))).reshape(4, 4, 8, LANES)
+    planes = 8
+    whole = (planes, 8, 8, LANES)
+    clear_rim(taps_ref, True)
+    fill_taps(
+        taps_ref,
+        folded_ref[:, :, :, :, 0].reshape(whole),
+        folded_ref[:, :, :, :, 1].reshape(whole),
+    )
+    slab_ref[...] = taps_ref[
+        pl.ds(side * (planes // 2), planes // 2 + 2), 1:9, :, LANES : 2 * LANES
+    ]
+
+    deep_act = jax.nn.silu(pre_deep).T.astype(jnp.bfloat16)
+    grad_up = jnp.dot(deep_act, upstream, preferred_element_type=jnp.float32)
+    down_at = 27 * LANES
+    up_at = down_at + 8 * deep
+    for tap in range(8):
+        rows_ref[up_at + tap * deep : up_at + (tap + 1) * deep, :] = grad_up[
+            :, tap * LANES : (tap + 1) * LANES
+        ]
+    grad_down = jnp.dot(
+        hidden.astype(jnp.float32).T.astype(jnp.bfloat16),
+        grad_deep,
+        preferred_element_type=jnp.float32,
+    )
+    for part in range(deep // LANES):
+        rows_ref[pl.ds(down_at + part, 8 * LANES, stride=deep // LANES), :] = grad_down[
+            :, part * LANES : (part + 1) * LANES
+        ]
+    turned = turned_ref[...]
+    for i in range(3):
+        for j in range(3):
+            cells = taps_ref[i : i + planes, j : j + 8].reshape(planes * 128, 3 * LANES)
+            sums = jnp.dot(turned, cells, preferred_element_type=jnp.float32)
+            for k in range(3):
+                at = (26 - 9 * i - 3 * j - k) * LANES
+                rows_ref[at : at + LANES, :] = sums[:, k * LANES : (k + 1) * LANES]
+    share = rows_ref.shape[0] // 16
+    half = mine_ref.shape[1]
+    for pair in range(8):
+        at = 2 * pair * share + side * (share - half)
+        keep = pl.multiple_of(at + core * share, 8)
+        give = pl.multiple_of(at + (1 - core) * share, 8)
+        mine_ref[pair] = rows_ref[pl.ds(keep, half), :].astype(jnp.bfloat16)
+        passed_ref[pair] = rows_ref[pl.ds(give, half), :].astype(jnp.bfloat16)
+
+
+def input_kernel(slab_ref, w_ref, out_ref, taps_ref, natural_ref):
+    slab = slab_ref[...].astype(jnp.float32)
+    planes = slab.shape[0]
+    clear_rim(taps_ref, False)
+    fill_taps(taps_ref, slab[:, :, :8], slab[:, :, 8:])
+    own = planes - 2
+    size = own * 128
+    total = jnp.zeros((size, LANES), jnp.float32)
+    for i in range(3):
+        for j in range(3):
+            first = 26 - 9 * i - 3 * j
+            weights = across(
+                [w_ref[(first - k) * LANES : (first - k + 1) * LANES, :] for k in range(3)]
+            )
+            cells = taps_ref[1 + i : 1 + i + own, j : j + 8].reshape(size, 3 * LANES)
+            total += against(cells, weights)
+    total = total.reshape(own, 8, 2, 8, LANES)
+    for parity in range(2):
+        natural_ref[:, :, pl.ds(parity, 8, stride=2), :] = total[:, :, parity]
+    for crop in range(2):
+        out_ref[crop] = natural_ref[:, :, 8 * crop : 8 * crop + 8, :].astype(jnp.bfloat16)
+
+
+def kernel_call(body, outs, scratch, flops, count):
+    return pl.pallas_call(
+        body,
+        out_shape=outs,
+        in_specs=[VMEM] * count,
+        out_specs=tuple(VMEM for _ in outs),
+        scratch_shapes=[pltpu.VMEM(shape, kind) for shape, kind in scratch],
+        compiler_params=pltpu.CompilerParams(vmem_limit_bytes=40 << 20),
+        cost_estimate=pl.CostEstimate(flops=flops, bytes_accessed=1 << 21, transcendentals=0),
+    )
+
+
+def per_device_pairs(inputs, cotangent, w_conv, w_down, w_up):
+    bf16, f32 = jnp.bfloat16, jnp.float32
+    shape = jax.ShapeDtypeStruct
+    other_in = swap_x(inputs)
+    other_up = swap_x(cotangent)
+    pre, turned = kernel_call(
+        forward_kernel,
+        (shape((4, 2, 4, 2, 2, 8, LANES), f32), shape((LANES, 1024), bf16)),
+        [((8, 8, 16, LANES), f32), ((10, 10, 16, 3 * LANES), bf16)],
+        10**9,
+        3,
+    )(inputs, other_in, w_conv)
+    total_rows = (w_conv.size + w_down.size + w_up.size) // LANES
+    per_share = total_rows // 16
+    half = -(-per_share // 32) * 16
+    mine, passed, slab = kernel_call(
+        backward_kernel,
+        (
+            shape((8, half, LANES), bf16),
+            shape((8, half, LANES), bf16),
+            shape((6, 8, 16, LANES), bf16),
+        ),
+        [
+            ((8, 8, 16, LANES), f32),
+            ((4, 2, 4, 2, 2, 8, LANES), f32),
+            ((10, 10, 16, 3 * LANES), bf16),
+            ((total_rows, LANES), f32),
+        ],
+        10**9,
+        6,
+    )(pre, turned, cotangent, other_up, w_down, w_up)
+    (grad_input,) = kernel_call(
+        input_kernel,
+        (shape(inputs.shape, bf16),),
+        [((8, 10, 16, 3 * LANES), bf16), ((4, 8, 16, LANES), f32)],
+        10**9,
+        2,
+    )(slab, w_conv)
+
+    passed = swap_dp(passed, 1)
+    crop_total = inputs.shape[0] * lax.axis_size("dp")
+    scale = 1.0 / jnp.sqrt(jnp.float32(crop_total * inputs.shape[2] ** 3))
+    grid = (2, 2, 2, half, LANES)
+    low, high = sum_shares(mine.reshape(grid), passed.reshape(grid), scale)
+    grad_share = jnp.concatenate([low, high[2 * half - per_share :]]).reshape(-1)
+    return (grad_input, grad_share)
+
+
 def solution(mesh):
+    pairs = dict(mesh.shape) == {"sp": 2, "dp": 16}
     return jax.shard_map(
-        per_device,
+        per_device_pairs if pairs else per_device,
         mesh=mesh,
         in_specs=(P("dp", "sp", None, None, None), P("dp", "sp", None, None, None), P(), P(), P()),
         out_specs=(P("dp", "sp", None, None, None), P("dp")),

time: 216 us -> 36.5 us (0.17)
  blocking collectives: 90 us -> 0 us
  waiting for transfers between devices: 63 us -> 15.5 us
  between operations: 15.3 us -> 0.76 us
  matrix products: 9.1 us -> 0 us
  starting transfers between devices: 20.2 us -> 11.2 us
  local copies, waits for them, and re-layouts: 10.2 us -> 2.11 us
  Pallas kernels: 0 us -> 5.78 us
  other arithmetic: 6.42 us -> 0.95 us
    unnamed x1 -> x0, blocking collectives: 90 us -> none
    psum x1 -> x0, waiting for transfers between devices: 55.1 us -> none  [per_device(): lax.psum(local_sums.astype(jnp.bfloat16), 'sp').astype(jnp.float32)]
    ppermute x4 -> x8, waiting for transfers between devices: 3.65 us -> 15.5 us  [the longest x5 10.1 us: swap_dp(): return lax.ppermute(value, 'dp', [(i, i ^ mask) for i in range(16)])]
    all_to_all x3 -> x0, starting transfers between devices: 10.8 us -> none  [the longest x1 3.92 us: per_device(): lax.all_to_all(cotangent, 'sp', split_axis=0, concat_axis=1, tiled=True)]
    dot_general x8 -> x0, matrix products: 9.1 us -> none  [the longest x1 3.14 us: per_device(): lax.dot_general(columns, grad_pre, (((0,), (0,)), ((), ())), preferred_el...]
    pallas_call x0 -> x3, Pallas kernels: none -> 5.78 us  [the longest x1 2.46 us: per_device_pairs(): kernel_call(backward_kernel, (shape((8, half, LANES), bf16), shape((8, ha...]
    all_to_all x3 -> x0, waiting for transfers between devices: 4.25 us -> none  [the longest x1 3.66 us: per_device(): lax.all_to_all(back_down, 'sp', split_axis=1, concat_axis=0, tiled=True)]
    transpose x5 -> x0, local copies, waits for them, and re-layouts: 3.24 us -> none  [the longest x2 1.38 us: flip_taps(): return w_conv.reshape(27, width_in, width_in)[::-1].transpose(0, 2, 1).re...]
  transfers between devices with their start and end apart: 8 -> 8, of which waited for: 5 -> 6; matrix products, arithmetic and copies ran while one was open for 7% -> 0% of each run, Pallas kernels for 0% -> 9%
where the time goes in v2:
time: 36.5 us; the launch traced here: 36.3 us
  waiting for transfers between devices  15.5 us (42%)
  starting transfers between devices  11.2 us (31%)
  Pallas kernels  5.78 us (16%)
  local copies, waits for them, and re-layouts  2.11 us (6%)
  other arithmetic  0.95 us (3%)
  between operations  0.76 us (2%)
    ppermute x5, waiting for transfers between devices, swap_dp(): return lax.ppermute(value, 'dp', [(i, i ^ mask) for i in range(16)])  10.1 us
    ppermute x5, starting transfers between devices, swap_dp(): return lax.ppermute(value, 'dp', [(i, i ^ mask) for i in range(16)])  6.55 us
    ppermute x3, waiting for transfers between devices, swap_x(): return lax.ppermute(value, 'sp', [(0, 1), (1, 0)])  5.4 us
    ppermute x3, starting transfers between devices, swap_x(): return lax.ppermute(value, 'sp', [(0, 1), (1, 0)])  4.65 us
    pallas_call x1, Pallas kernels, per_device_pairs(): kernel_call(backward_kernel, (shape((8, half, LANES), bf16), shape((8, ha...  2.46 us
    unnamed x12, local copies, waits for them, and re-layouts  2.09 us
    pallas_call x1, Pallas kernels, per_device_pairs(): kernel_call(input_kernel, (shape(inputs.shape, bf16),), [((8, 10, 16, 3 *...  1.78 us
    pallas_call x1, Pallas kernels, per_device_pairs(): kernel_call(forward_kernel, (shape((4, 2, 4, 2, 2, 8, LANES), f32), shape...  1.54 us
  transfers between devices with their start and end apart: 8, of which 6 were waited for; matrix products, arithmetic and copies ran while one was open for 0% of the time, Pallas kernels for 9%

profile of v2, /device:TPU:0, one launch (start us, length us, event | category | flops | bytes accessed | tf_op | source)
XLA Modules:
  0.0 36.3 jit_solution(15028428238315458277)
XLA Ops:
  0.6 3.0 %collective-permute-start = (bf16[2,4,8,8,128]{4,3,2,1,0:T(8,128)(2,1)}, bf16[2,4,8,8,128]{4,3,2,1,0:T(8,128)(2,1)S(1)}, u32[]{:S(2)}, u32[]{:S(2)}) collective-permute-start(bf16[2,4,8,8,128]{4,3,2,1,0:T(8,128)(2,1)} %own_ref.2), channel_id=1, source_target_pairs={{0,16},{16,0},{1,17},{17,1},{2,18},{18,2},{3,19},{19,3},{4,20},{20... | collective-permute-start | bytes 393224 | tf_op jit(solution)/shard_map/ppermute | solution.py:139
  3.6 0.1 collective-permute-start.1
  3.7 4.5 %collective-permute-done.other_ref = bf16[2,4,8,8,128]{4,3,2,1,0:T(8,128)(2,1)S(1)} collective-permute-done((bf16[2,4,8,8,128]{4,3,2,1,0:T(8,128)(2,1)}, bf16[2,4,8,8,128]{4,3,2,1,0:T(8,128)(2,1)S(1)}, u32[]{:S(2)}, u32[]{:S(2)}) %collective-permute-start) | collective-permute-done | bytes 131104 | tf_op jit(solution)/shard_map/ppermute | solution.py:139
  8.2 0.0 copy-start
  8.2 1.2 %copy-done = bf16[3456,128]{1,0:T(8,128)(2,1)S(1)} copy-done((bf16[3456,128]{1,0:T(8,128)(2,1)S(1)}, bf16[3456,128]{1,0:T(8,128)(2,1)}, u32[]{:S(2)}) %copy-start) | copy-done | bytes 884760
  9.3 0.0 copy-start.4
  9.3 0.9 %copy-done.4 = bf16[2,4,8,8,128]{4,3,2,1,0:T(8,128)(2,1)S(1)} copy-done((bf16[2,4,8,8,128]{4,3,2,1,0:T(8,128)(2,1)S(1)}, bf16[2,4,8,8,128]{4,3,2,1,0:T(8,128)(2,1)}, u32[]{:S(2)}) %copy-start.4) | copy-done | bytes 131096
  10.2 0.0 copy-start.3
  10.2 1.5 %shard_map.68 = (f32[4,2,4,2,2,8,128]{6,5,4,3,2,1,0:T(8,128)S(1)}, bf16[128,1024]{1,0:T(8,128)(2,1)S(1)}) custom-call(bf16[2,4,8,8,128]{4,3,2,1,0:T(8,128)(2,1)S(1)} %copy-done.4, bf16[2,4,8,8,128]{4,3,2,1,0:T(8,128)(2,1)S(1)} %collective-permute-done.other_ref, bf16[3456,128]{1,0:T(8,128)(2,1)S(1)} %copy-done), custom_call_target="tpu_custom_call" | custom-call | flops 1000000000 | bytes 2097152 | tf_op jit(solution)/shard_map/pallas_call | solution.py:385
  11.8 0.0 collective-permute-done.1.other_ref
  11.8 0.0 copy-done.2
  11.8 0.0 copy-done.3
  11.8 0.0 copy-done.5
  11.8 2.5 %shard_map.69 = (bf16[8,240,128]{2,1,0:T(8,128)(2,1)S(1)}, bf16[8,240,128]{2,1,0:T(8,128)(2,1)S(1)}, bf16[6,8,16,128]{3,2,1,0:T(8,128)(2,1)S(1)}) custom-call(f32[4,2,4,2,2,8,128]{6,5,4,3,2,1,0:T(8,128)S(1)} %get-tuple-element.7.pre_ref, bf16[128,1024]{1,0:T(8,128)(2,1)S(1)} %get-tuple-element.8.turned_ref, bf16[2,4,8,8,128]{4,3,2,1,0:T(8,128)(2,1)S(1)} %copy-done.5, ...), custom_call_target="tpu_custom_call" | custom-call | flops 1000000000 | bytes 2097152 | tf_op jit(solution)/shard_map/pallas_call | solution.py:395
  14.3 0.1 collective-permute-start.2
  14.4 1.8 %collective-permute-done.2 = bf16[8,240,128]{2,1,0:T(8,128)(2,1)S(1)} collective-permute-done((bf16[8,240,128]{2,1,0:T(8,128)(2,1)S(1)}, bf16[8,240,128]{2,1,0:T(8,128)(2,1)S(1)}, u32[]{:S(2)}, u32[]{:S(2)}) %collective-permute-start.2) | collective-permute-done | bytes 491552 | tf_op jit(solution)/shard_map/ppermute | solution.py:143
  16.3 0.0 copy-start.1
  16.3 3.2 %collective-permute-start.5 = (bf16[2,240,128]{2,1,0:T(8,128)(2,1)S(1)}, bf16[2,240,128]{2,1,0:T(8,128)(2,1)S(1)}, u32[]{:S(2)}, u32[]{:S(2)}) collective-permute-start(bf16[2,240,128]{2,1,0:T(8,128)(2,1)S(1)} %fusion.4), channel_id=1, source_target_pairs={{0,6},{1,7},{2,4},{3,5},{4,2},{5,3},{6,0},{7,1},{8,14},{9,15},{10,... | collective-permute-start | bytes 368648 | tf_op jit(solution)/shard_map/ppermute | solution.py:143
  19.4 0.1 fusion.2
  19.5 0.5 %collective-permute-start.4 = (bf16[2,240,128]{2,1,0:T(8,128)(2,1)S(1)}, bf16[2,240,128]{2,1,0:T(8,128)(2,1)S(1)}, u32[]{:S(2)}, u32[]{:S(2)}) collective-permute-start(bf16[2,240,128]{2,1,0:T(8,128)(2,1)S(1)} %get-tuple-element.13), channel_id=1, source_target_pairs={{0,4},{1,5},{2,6},{3,7},{4,0},{5,1},{6,2},{7,3},{8,12},{9,13},{10,... | collective-permute-start | bytes 368648 | tf_op jit(solution)/shard_map/ppermute | solution.py:143
  20.0 0.1 collective-permute-start.3
  20.2 3.4 %collective-permute-done.5 = bf16[2,240,128]{2,1,0:T(8,128)(2,1)S(1)} collective-permute-done((bf16[2,240,128]{2,1,0:T(8,128)(2,1)S(1)}, bf16[2,240,128]{2,1,0:T(8,128)(2,1)S(1)}, u32[]{:S(2)}, u32[]{:S(2)}) %collective-permute-start.5) | collective-permute-done | bytes 122912 | tf_op jit(solution)/shard_map/ppermute | solution.py:143
  23.6 2.3 %collective-permute-done.4 = bf16[2,240,128]{2,1,0:T(8,128)(2,1)S(1)} collective-permute-done((bf16[2,240,128]{2,1,0:T(8,128)(2,1)S(1)}, bf16[2,240,128]{2,1,0:T(8,128)(2,1)S(1)}, u32[]{:S(2)}, u32[]{:S(2)}) %collective-permute-start.4) | collective-permute-done | bytes 122912 | tf_op jit(solution)/shard_map/ppermute | solution.py:143
  25.9 0.0 collective-permute-done.3
  25.9 0.1 fusion.1
  26.0 2.7 %collective-permute-start.6 = (bf16[240,128]{1,0:T(8,128)(2,1)S(1)}, bf16[240,128]{1,0:T(8,128)(2,1)S(1)}, u32[]{:S(2)}, u32[]{:S(2)}) collective-permute-start(bf16[240,128]{1,0:T(8,128)(2,1)S(1)} %fusion.6), channel_id=1, source_target_pairs={{0,8},{1,9},{2,10},{3,11},{4,12},{5,13},{6,14},{7,15},{8,0},{9,1},... | collective-permute-start | bytes 184328 | tf_op jit(solution)/shard_map/ppermute | solution.py:143
  28.6 2.6 %collective-permute-done.6 = bf16[240,128]{1,0:T(8,128)(2,1)S(1)} collective-permute-done((bf16[240,128]{1,0:T(8,128)(2,1)S(1)}, bf16[240,128]{1,0:T(8,128)(2,1)S(1)}, u32[]{:S(2)}, u32[]{:S(2)}) %collective-permute-start.6) | collective-permute-done | bytes 61472 | tf_op jit(solution)/shard_map/ppermute | solution.py:143
  31.3 1.6 %collective-permute-start.7 = (bf16[240,128]{1,0:T(8,128)(2,1)S(1)}, bf16[240,128]{1,0:T(8,128)(2,1)S(1)}, u32[]{:S(2)}, u32[]{:S(2)}) collective-permute-start(bf16[240,128]{1,0:T(8,128)(2,1)S(1)} %fusion.5), channel_id=1, source_target_pairs={{0,16},{16,0},{1,17},{17,1},{2,18},{18,2},{3,19},{19,3},{4,20},{20... | collective-permute-start | bytes 184328 | tf_op jit(solution)/shard_map/ppermute | solution.py:139
  32.8 0.0 copy-done.1
  32.8 1.8 %shard_map.70 = bf16[2,4,8,8,128]{4,3,2,1,0:T(8,128)(2,1)} custom-call(bf16[6,8,16,128]{3,2,1,0:T(8,128)(2,1)S(1)} %get-tuple-element.9.slab_ref, bf16[3456,128]{1,0:T(8,128)(2,1)S(1)} %copy-done.1), custom_call_target="tpu_custom_call" | custom-call | flops 1000000000 | bytes 2097152 | tf_op jit(solution)/shard_map/pallas_call | solution.py:411
  34.6 0.9 %collective-permute-done.7 = bf16[240,128]{1,0:T(8,128)(2,1)S(1)} collective-permute-done((bf16[240,128]{1,0:T(8,128)(2,1)S(1)}, bf16[240,128]{1,0:T(8,128)(2,1)S(1)}, u32[]{:S(2)}, u32[]{:S(2)}) %collective-permute-start.7) | collective-permute-done | bytes 61472 | tf_op jit(solution)/shard_map/ppermute | solution.py:139
  35.6 0.7 %maximum_bitcast_fusion = f32[60416]{0:T(1024)} fusion(f32[232,128]{1,0:T(8,128)S(1)} %convert_multiply_fusion.1, f32[240,128]{1,0:T(8,128)S(1)} %convert_multiply_fusion), kind=kLoop, calls=%fused_computation.6 | loop fusion | flops 60416 | bytes 483328 | tf_op jit(solution)/shard_map/reshape | solution.py:424
  (7 shorter events, 0.1 us)
Async XLA Ops:
  0.6 7.5 %collective-permute-start = (bf16[2,4,8,8,128]{4,3,2,1,0:T(8,128)(2,1)}, bf16[2,4,8,8,128]{4,3,2,1,0:T(8,128)(2,1)S(1)}, u32[]{:S(2)}, u32[]{:S(2)}) collective-permute-start(bf16[2,4,8,8,128]{4,3,2,1,0:T(8,128)(2,1)} %own_ref.2), channel_id=1, source_target_pairs={{0,16},{16,0},{1,17},{17,1},{2,18},{18,2},{3,19},{19,3},{4,20},{20... | collective-permute-start | bytes 393224 | tf_op jit(solution)/shard_map/ppermute | solution.py:139
  3.6 8.2 %collective-permute-start.1 = (bf16[2,4,8,8,128]{4,3,2,1,0:T(8,128)(2,1)}, bf16[2,4,8,8,128]{4,3,2,1,0:T(8,128)(2,1)S(1)}, u32[]{:S(2)}, u32[]{:S(2)}) collective-permute-start(bf16[2,4,8,8,128]{4,3,2,1,0:T(8,128)(2,1)} %own_ref.3), channel_id=1, source_target_pairs={{0,16},{16,0},{1,17},{17,1},{2,18},{18,2},{3,19},{19,3},{4,20},{20... | collective-permute-start | bytes 393224 | tf_op jit(solution)/shard_map/ppermute | solution.py:139
  8.2 1.2 %copy-start = (bf16[3456,128]{1,0:T(8,128)(2,1)S(1)}, bf16[3456,128]{1,0:T(8,128)(2,1)}, u32[]{:S(2)}) copy-start(bf16[3456,128]{1,0:T(8,128)(2,1)} %w_ref.3) | copy-start | bytes 2654212
  9.3 0.9 %copy-start.4 = (bf16[2,4,8,8,128]{4,3,2,1,0:T(8,128)(2,1)S(1)}, bf16[2,4,8,8,128]{4,3,2,1,0:T(8,128)(2,1)}, u32[]{:S(2)}) copy-start(bf16[2,4,8,8,128]{4,3,2,1,0:T(8,128)(2,1)} %own_ref.2) | copy-start | bytes 393220
  10.2 1.6 %copy-start.2 = (bf16[1024,256]{1,0:T(8,128)(2,1)S(1)}, bf16[1024,256]{1,0:T(8,128)(2,1)}, u32[]{:S(2)}) copy-start(bf16[1024,256]{1,0:T(8,128)(2,1)} %w_down_ref.1) | copy-start | bytes 1572868
  10.2 1.6 %copy-start.3 = (bf16[2048,128]{1,0:T(8,128)(2,1)S(1)}, bf16[2048,128]{1,0:T(8,128)(2,1)}, u32[]{:S(2)}) copy-start(bf16[2048,128]{1,0:T(8,128)(2,1)} %w_up_ref.1) | copy-start | bytes 1572868
  10.2 1.6 %copy-start.5 = (bf16[2,4,8,8,128]{4,3,2,1,0:T(8,128)(2,1)S(1)}, bf16[2,4,8,8,128]{4,3,2,1,0:T(8,128)(2,1)}, u32[]{:S(2)}) copy-start(bf16[2,4,8,8,128]{4,3,2,1,0:T(8,128)(2,1)} %own_ref.3) | copy-start | bytes 393220
  14.3 1.9 %collective-permute-start.2 = (bf16[8,240,128]{2,1,0:T(8,128)(2,1)S(1)}, bf16[8,240,128]{2,1,0:T(8,128)(2,1)S(1)}, u32[]{:S(2)}, u32[]{:S(2)}) collective-permute-start(bf16[8,240,128]{2,1,0:T(8,128)(2,1)S(1)} %get-tuple-element.11), channel_id=1, source_target_pairs={{0,1},{1,0},{2,3},{3,2},{4,5},{5,4},{6,7},{7,6},{8,9},{9,8},{10,11... | collective-permute-start | bytes 1474568 | tf_op jit(solution)/shard_map/ppermute | solution.py:143
  16.3 16.6 %copy-start.1 = (bf16[3456,128]{1,0:T(8,128)(2,1)S(1)}, bf16[3456,128]{1,0:T(8,128)(2,1)}, u32[]{:S(2)}) copy-start(bf16[3456,128]{1,0:T(8,128)(2,1)} %w_ref.3) | copy-start | bytes 2654212
  16.3 7.3 %collective-permute-start.5 = (bf16[2,240,128]{2,1,0:T(8,128)(2,1)S(1)}, bf16[2,240,128]{2,1,0:T(8,128)(2,1)S(1)}, u32[]{:S(2)}, u32[]{:S(2)}) collective-permute-start(bf16[2,240,128]{2,1,0:T(8,128)(2,1)S(1)} %fusion.4), channel_id=1, source_target_pairs={{0,6},{1,7},{2,4},{3,5},{4,2},{5,3},{6,0},{7,1},{8,14},{9,15},{10,... | collective-permute-start | bytes 368648 | tf_op jit(solution)/shard_map/ppermute | solution.py:143
  19.5 6.3 %collective-permute-start.4 = (bf16[2,240,128]{2,1,0:T(8,128)(2,1)S(1)}, bf16[2,240,128]{2,1,0:T(8,128)(2,1)S(1)}, u32[]{:S(2)}, u32[]{:S(2)}) collective-permute-start(bf16[2,240,128]{2,1,0:T(8,128)(2,1)S(1)} %get-tuple-element.13), channel_id=1, source_target_pairs={{0,4},{1,5},{2,6},{3,7},{4,0},{5,1},{6,2},{7,3},{8,12},{9,13},{10,... | collective-permute-start | bytes 368648 | tf_op jit(solution)/shard_map/ppermute | solution.py:143
  20.0 5.8 %collective-permute-start.3 = (bf16[2,240,128]{2,1,0:T(8,128)(2,1)S(1)}, bf16[2,240,128]{2,1,0:T(8,128)(2,1)S(1)}, u32[]{:S(2)}, u32[]{:S(2)}) collective-permute-start(bf16[2,240,128]{2,1,0:T(8,128)(2,1)S(1)} %get-tuple-element.12), channel_id=1, source_target_pairs={{0,2},{1,3},{2,0},{3,1},{4,6},{5,7},{6,4},{7,5},{8,10},{9,11},{10,... | collective-permute-start | bytes 368648 | tf_op jit(solution)/shard_map/ppermute | solution.py:143
  26.0 5.3 %collective-permute-start.6 = (bf16[240,128]{1,0:T(8,128)(2,1)S(1)}, bf16[240,128]{1,0:T(8,128)(2,1)S(1)}, u32[]{:S(2)}, u32[]{:S(2)}) collective-permute-start(bf16[240,128]{1,0:T(8,128)(2,1)S(1)} %fusion.6), channel_id=1, source_target_pairs={{0,8},{1,9},{2,10},{3,11},{4,12},{5,13},{6,14},{7,15},{8,0},{9,1},... | collective-permute-start | bytes 184328 | tf_op jit(solution)/shard_map/ppermute | solution.py:143
  31.3 4.3 %collective-permute-start.7 = (bf16[240,128]{1,0:T(8,128)(2,1)S(1)}, bf16[240,128]{1,0:T(8,128)(2,1)S(1)}, u32[]{:S(2)}, u32[]{:S(2)}) collective-permute-start(bf16[240,128]{1,0:T(8,128)(2,1)S(1)} %fusion.5), channel_id=1, source_target_pairs={{0,16},{16,0},{1,17},{17,1},{2,18},{18,2},{3,19},{19,3},{4,20},{20... | collective-permute-start | bytes 184328 | tf_op jit(solution)/shard_map/ppermute | solution.py:139

commit v3 on v2

--- a/solution.py
+++ b/solution.py
@@ -176,15 +176,26 @@
 
 LANES = 128
 VMEM = pl.BlockSpec(memory_space=pltpu.VMEM)
-
-
-def load_crops(own_ref, other_ref, natural_ref, side):
-    depth = own_ref.shape[1]
-    for ref, first in ((own_ref, side * depth), (other_ref, (1 - side) * depth)):
-        for crop in range(2):
-            natural_ref[pl.ds(first, depth), :, 8 * crop : 8 * crop + 8, :] = ref[crop].astype(
-                jnp.float32
-            )
+BF16, F32 = jnp.bfloat16, jnp.float32
+PLACES = tuple((i, j, k) for i in range(2) for j in range(2) for k in range(2))
+
+
+def dot(a, b):
+    return jnp.dot(a, b, preferred_element_type=F32)
+
+
+def against(a, b):
+    return lax.dot_general(a, b, (((1,), (1,)), ((), ())), preferred_element_type=F32)
+
+
+def across(parts):
+    return jnp.concatenate(parts, axis=-1)
+
+
+def split_parity(slab_ref, natural_ref):
+    for crop in range(2):
+        natural_ref[:, :, 8 * crop : 8 * crop + 8, :] = slab_ref[crop].astype(F32)
+    return [natural_ref[:, :, pl.ds(parity, 8, stride=2), :] for parity in range(2)]
 
 
 def fill_taps(taps_ref, even, odd):
@@ -192,109 +203,146 @@
     kk = lax.broadcasted_iota(jnp.int32, even.shape, 2) % 4
     before = jnp.where(kk == 0, 0.0, pltpu.roll(odd, 1, 2))
     after = jnp.where(kk == 3, 0.0, pltpu.roll(even, 7, 2))
-    rows = pl.ds(1, 8)
     for tap, (low, high) in enumerate(((before, even), (even, odd), (odd, after))):
-        taps_ref[1 : 1 + planes, rows, :, tap * LANES : (tap + 1) * LANES] = jnp.concatenate(
+        taps_ref[1 : 1 + planes, pl.ds(1, 8), :, tap * LANES : (tap + 1) * LANES] = jnp.concatenate(
             [low, high], axis=2
-        ).astype(jnp.bfloat16)
+        ).astype(BF16)
 
 
 def clear_rim(taps_ref, with_planes):
     planes, rows, tile, lanes = taps_ref.shape
-    row = jnp.zeros((planes, tile, lanes), jnp.bfloat16)
+    row = jnp.zeros((planes, tile, lanes), BF16)
     taps_ref[:, 0] = row
     taps_ref[:, rows - 1] = row
     if with_planes:
-        plane = jnp.zeros((rows, tile, lanes), jnp.bfloat16)
+        plane = jnp.zeros((rows, tile, lanes), BF16)
         taps_ref[0] = plane
         taps_ref[planes - 1] = plane
 
 
-def across(tile):
-    return jnp.concatenate(tile, axis=-1)
-
-
-def forward_kernel(own_ref, other_ref, w_ref, pre_ref, turned_ref, natural_ref, taps_ref):
-    side = lax.axis_index("sp")
-    load_crops(own_ref, other_ref, natural_ref, side)
-    even = natural_ref[:, :, pl.ds(0, 8, stride=2), :]
-    odd = natural_ref[:, :, pl.ds(1, 8, stride=2), :]
+def slab_conv(slab_ref, w_ref, natural_ref, taps_ref):
+    even, odd = split_parity(slab_ref, natural_ref)
     clear_rim(taps_ref, False)
     fill_taps(taps_ref, even, odd)
-    wide = 3 * LANES
     planes = even.shape[0]
     size = planes * 128
+    wide = 3 * LANES
     centre = taps_ref[1 : 1 + planes, 1:9, :, LANES : 2 * LANES].reshape(size, LANES)
-    turned_ref[...] = centre.astype(jnp.float32).T.astype(jnp.bfloat16)
-    cells = across(
-        [taps_ref[1 : 1 + planes, j : j + 8].reshape(size, wide) for j in range(3)]
-    )
+    turned = centre.astype(F32).T.astype(BF16)
+    cells = across([taps_ref[1 : 1 + planes, j : j + 8].reshape(size, wide) for j in range(3)])
 
     def weights(i):
         return w_ref[i * 3 * wide : (i + 1) * 3 * wide, :]
 
-    first = jnp.dot(
-        cells, across([weights(0), weights(1)]), preferred_element_type=jnp.float32
-    )
-    last = jnp.dot(cells, weights(2), preferred_element_type=jnp.float32)
-    rim = jnp.zeros((128, LANES), jnp.float32)
-    pre = (
-        jnp.concatenate([rim, first[:-128, :LANES]])
-        + first[:, LANES:]
-        + jnp.concatenate([last[128:], rim])
-    )
-    pre_ref[...] = pre.reshape(pre_ref.shape)
-
-
-def against(a, b):
-    return lax.dot_general(
-        a, b, (((1,), (1,)), ((), ())), preferred_element_type=jnp.float32
+    first = dot(cells, across([weights(0), weights(1)])).reshape(planes, 128, 2 * LANES)
+    last = dot(cells, weights(2)).reshape(planes, 128, LANES)
+    none = jnp.zeros((1, 128, LANES), F32)
+    two = jnp.zeros((2, 128, LANES), F32)
+    added = (
+        jnp.concatenate([two, first[:, :, :LANES]])
+        + jnp.concatenate([none, first[:, :, LANES:], none])
+        + jnp.concatenate([last, two])
+    )
+    return added, turned
+
+
+def blocks(parts, tap):
+    i, j, k = PLACES[tap]
+    even_odd = parts[k]
+    planes = even_odd.shape[0]
+    folded = even_odd.reshape(planes // 2, 2, 4, 2, 8, LANES)
+    return folded[:, i, :, j].reshape(planes * 16, LANES)
+
+
+def deep_gradient(parts, w_up_ref):
+    upstream = across([blocks(parts, tap).astype(BF16) for tap in range(8)])
+    deep = w_up_ref.shape[0] // 8
+    w_up = across([w_up_ref[tap * deep : (tap + 1) * deep, :] for tap in range(8)])
+    return upstream, against(upstream, w_up)
+
+
+def own_kernel(in_ref, w_ref, add_ref, turned_ref, natural_ref, taps_ref):
+    add_ref[...], turned_ref[...] = slab_conv(in_ref, w_ref, natural_ref, taps_ref)
+
+
+def forward_kernel(
+    in_ref,
+    w_ref,
+    add_ref,
+    turned_own_ref,
+    w_down_ref,
+    up_ref,
+    w_up_ref,
+    slope_ref,
+    turned_ref,
+    hidden_ref,
+    act_ref,
+    deep_slope_ref,
+    blocks_own_ref,
+    act_own_ref,
+    natural_ref,
+    taps_ref,
+    sum_ref,
+):
+    side = lax.axis_index("sp")
+    planes = in_ref.shape[1]
+    added, turned = slab_conv(in_ref, w_ref, natural_ref, taps_ref)
+    sum_ref[...] = jnp.zeros_like(sum_ref)
+    sum_ref[pl.ds(side * planes, planes + 2)] = add_ref[...]
+    sum_ref[pl.ds((1 - side) * planes, planes + 2)] += added
+    turned_ref[side] = turned_own_ref[...]
+    turned_ref[1 - side] = turned
+    folded = (planes, 2, 4, 2, 2, 8, LANES)
+    pre = sum_ref[1 : 1 + 2 * planes].reshape(folded)
+    sigmoid_value = jax.nn.sigmoid(pre)
+    slope_ref[...] = sigmoid_value * (1.0 + pre * (1.0 - sigmoid_value))
+    act = pre * sigmoid_value
+    hidden = across([act[:, i, :, j, k].reshape(128, LANES).astype(BF16) for i, j, k in PLACES])
+    hidden_ref[...] = hidden.astype(F32).T.astype(BF16)
+    pre_deep = dot(hidden, w_down_ref[...])
+    act_ref[...] = jax.nn.silu(pre_deep).T.astype(BF16)
+    deep_slope_ref[...] = silu_slope(pre_deep)
+    blocks_own_ref[...], act_own_ref[...] = deep_gradient(
+        split_parity(up_ref, natural_ref), w_up_ref
     )
 
 
 def backward_kernel(
-    pre_ref,
+    up_ref,
+    slope_ref,
     turned_ref,
-    own_ref,
-    other_ref,
+    hidden_ref,
+    deep_act_ref,
+    deep_slope_ref,
+    blocks_own_ref,
+    act_own_ref,
     w_down_ref,
     w_up_ref,
     mine_ref,
     passed_ref,
     slab_ref,
     natural_ref,
+    blocks_ref,
+    act_ref,
     folded_ref,
     taps_ref,
     rows_ref,
 ):
     side = lax.axis_index("sp")
     core = lax.axis_index("dp") % 2
-    load_crops(own_ref, other_ref, natural_ref, side)
-    up = [
-        natural_ref[:, :, pl.ds(parity, 8, stride=2), :].reshape(4, 2, 4, 2, 8, LANES)
-        for parity in range(2)
-    ]
-    places = [(i, j, k) for i in range(2) for j in range(2) for k in range(2)]
-
-    def block(i, j, k):
-        return pre_ref[:, i, :, j, k].reshape(128, LANES)
-
-    def up_block(i, j, k):
-        return up[k][:, i, :, j].reshape(128, LANES)
-
-    hidden = across([jax.nn.silu(block(*at)).astype(jnp.bfloat16) for at in places])
-    upstream = across([up_block(*at).astype(jnp.bfloat16) for at in places])
-    pre_deep = jnp.dot(hidden, w_down_ref[...], preferred_element_type=jnp.float32)
-    deep = pre_deep.shape[1]
-    grad_act = against(
-        upstream, across([w_up_ref[tap * deep : (tap + 1) * deep, :] for tap in range(8)])
-    )
-    grad_deep = (grad_act * silu_slope(pre_deep)).astype(jnp.bfloat16)
-    back = against(grad_deep, w_down_ref[...]).astype(jnp.bfloat16).astype(jnp.float32)
-    for tap, at in enumerate(places):
-        i, j, k = at
-        summed = up_block(*at) + back[:, tap * LANES : (tap + 1) * LANES]
-        folded_ref[:, i, :, j, k] = (summed * silu_slope(block(*at))).reshape(4, 4, 8, LANES)
+    parts = split_parity(up_ref, natural_ref)
+    upstream, grad_act = deep_gradient(parts, w_up_ref)
+    blocks_ref[side] = blocks_own_ref[...]
+    blocks_ref[1 - side] = upstream
+    act_ref[side] = act_own_ref[...]
+    act_ref[1 - side] = grad_act
+    upstream = blocks_ref[...].reshape(128, 8 * LANES)
+    grad_deep = (act_ref[...].reshape(deep_slope_ref.shape) * deep_slope_ref[...]).astype(BF16)
+    back = against(grad_deep, w_down_ref[...]).astype(BF16).astype(F32)
+    for tap, (i, j, k) in enumerate(PLACES):
+        lanes = slice(tap * LANES, (tap + 1) * LANES)
+        summed = (upstream[:, lanes].astype(F32) + back[:, lanes]).reshape(4, 4, 8, LANES)
+        folded_ref[:, i, :, j, k] = summed * slope_ref[:, i, :, j, k]
     planes = 8
     whole = (planes, 8, 8, LANES)
     clear_rim(taps_ref, True)
@@ -307,49 +355,48 @@
         pl.ds(side * (planes // 2), planes // 2 + 2), 1:9, :, LANES : 2 * LANES
     ]
 
-    deep_act = jax.nn.silu(pre_deep).T.astype(jnp.bfloat16)
-    grad_up = jnp.dot(deep_act, upstream, preferred_element_type=jnp.float32)
+    deep = w_down_ref.shape[1]
+    grad_up = dot(deep_act_ref[...], upstream)
     down_at = 27 * LANES
     up_at = down_at + 8 * deep
     for tap in range(8):
         rows_ref[up_at + tap * deep : up_at + (tap + 1) * deep, :] = grad_up[
             :, tap * LANES : (tap + 1) * LANES
         ]
-    grad_down = jnp.dot(
-        hidden.astype(jnp.float32).T.astype(jnp.bfloat16),
-        grad_deep,
-        preferred_element_type=jnp.float32,
-    )
+    grad_down = dot(hidden_ref[...], grad_deep)
     for part in range(deep // LANES):
         rows_ref[pl.ds(down_at + part, 8 * LANES, stride=deep // LANES), :] = grad_down[
             :, part * LANES : (part + 1) * LANES
         ]
-    turned = turned_ref[...]
+    turned = across([turned_ref[0], turned_ref[1]])
     for i in range(3):
-        for j in range(3):
-            cells = taps_ref[i : i + planes, j : j + 8].reshape(planes * 128, 3 * LANES)
-            sums = jnp.dot(turned, cells, preferred_element_type=jnp.float32)
-            for k in range(3):
-                at = (26 - 9 * i - 3 * j - k) * LANES
-                rows_ref[at : at + LANES, :] = sums[:, k * LANES : (k + 1) * LANES]
+        cells = across(
+            [
+                taps_ref[i : i + planes, j : j + 8].reshape(planes * 128, 3 * LANES)
+                for j in range(3)
+            ]
+        )
+        sums = dot(turned, cells)
+        for tap in range(9):
+            at = (26 - 9 * i - tap) * LANES
+            rows_ref[at : at + LANES, :] = sums[:, tap * LANES : (tap + 1) * LANES]
     share = rows_ref.shape[0] // 16
     half = mine_ref.shape[1]
     for pair in range(8):
         at = 2 * pair * share + side * (share - half)
         keep = pl.multiple_of(at + core * share, 8)
         give = pl.multiple_of(at + (1 - core) * share, 8)
-        mine_ref[pair] = rows_ref[pl.ds(keep, half), :].astype(jnp.bfloat16)
-        passed_ref[pair] = rows_ref[pl.ds(give, half), :].astype(jnp.bfloat16)
+        mine_ref[pair] = rows_ref[pl.ds(keep, half), :].astype(BF16)
+        passed_ref[pair] = rows_ref[pl.ds(give, half), :].astype(BF16)
 
 
 def input_kernel(slab_ref, w_ref, out_ref, taps_ref, natural_ref):
-    slab = slab_ref[...].astype(jnp.float32)
-    planes = slab.shape[0]
+    slab = slab_ref[...].astype(F32)
+    own = slab.shape[0] - 2
+    size = own * 128
     clear_rim(taps_ref, False)
     fill_taps(taps_ref, slab[:, :, :8], slab[:, :, 8:])
-    own = planes - 2
-    size = own * 128
-    total = jnp.zeros((size, LANES), jnp.float32)
+    total = jnp.zeros((size, LANES), F32)
     for i in range(3):
         for j in range(3):
             first = 26 - 9 * i - 3 * j
@@ -362,59 +409,76 @@
     for parity in range(2):
         natural_ref[:, :, pl.ds(parity, 8, stride=2), :] = total[:, :, parity]
     for crop in range(2):
-        out_ref[crop] = natural_ref[:, :, 8 * crop : 8 * crop + 8, :].astype(jnp.bfloat16)
-
-
-def kernel_call(body, outs, scratch, flops, count):
+        out_ref[crop] = natural_ref[:, :, 8 * crop : 8 * crop + 8, :].astype(BF16)
+
+
+def run(body, operands, outs, scratch, flops):
     return pl.pallas_call(
         body,
-        out_shape=outs,
-        in_specs=[VMEM] * count,
-        out_specs=tuple(VMEM for _ in outs),
+        out_shape=tuple(jax.ShapeDtypeStruct(shape, kind) for shape, kind in outs),
+        in_specs=[VMEM] * len(operands),
+        out_specs=(VMEM,) * len(outs),
         scratch_shapes=[pltpu.VMEM(shape, kind) for shape, kind in scratch],
         compiler_params=pltpu.CompilerParams(vmem_limit_bytes=40 << 20),
         cost_estimate=pl.CostEstimate(flops=flops, bytes_accessed=1 << 21, transcendentals=0),
-    )
+    )(*operands)
 
 
 def per_device_pairs(inputs, cotangent, w_conv, w_down, w_up):
-    bf16, f32 = jnp.bfloat16, jnp.float32
-    shape = jax.ShapeDtypeStruct
+    deep = w_down.shape[1]
     other_in = swap_x(inputs)
     other_up = swap_x(cotangent)
-    pre, turned = kernel_call(
+    natural = ((4, 8, 16, LANES), F32)
+    slab_taps = ((6, 10, 16, 3 * LANES), BF16)
+    blocked = ((64, 8 * LANES), BF16)
+    act = ((64, deep), F32)
+    added, turned_own = run(
+        own_kernel,
+        (inputs, w_conv),
+        [((6, 128, LANES), F32), ((LANES, 512), BF16)],
+        [natural, slab_taps],
+        10**9,
+    )
+    folded = ((4, 2, 4, 2, 2, 8, LANES), F32)
+    saved = run(
         forward_kernel,
-        (shape((4, 2, 4, 2, 2, 8, LANES), f32), shape((LANES, 1024), bf16)),
-        [((8, 8, 16, LANES), f32), ((10, 10, 16, 3 * LANES), bf16)],
+        (other_in, w_conv, added, turned_own, w_down, cotangent, w_up),
+        [
+            folded,
+            ((2, LANES, 512), BF16),
+            ((8 * LANES, 128), BF16),
+            ((deep, 128), BF16),
+            ((128, deep), F32),
+            blocked,
+            act,
+        ],
+        [natural, slab_taps, ((10, 128, LANES), F32)],
         10**9,
-        3,
-    )(inputs, other_in, w_conv)
+    )
     total_rows = (w_conv.size + w_down.size + w_up.size) // LANES
     per_share = total_rows // 16
     half = -(-per_share // 32) * 16
-    mine, passed, slab = kernel_call(
+    mine, passed, slab = run(
         backward_kernel,
-        (
-            shape((8, half, LANES), bf16),
-            shape((8, half, LANES), bf16),
-            shape((6, 8, 16, LANES), bf16),
-        ),
+        (other_up, *saved, w_down, w_up),
+        [((8, half, LANES), BF16), ((8, half, LANES), BF16), ((6, 8, 16, LANES), BF16)],
         [
-            ((8, 8, 16, LANES), f32),
-            ((4, 2, 4, 2, 2, 8, LANES), f32),
-            ((10, 10, 16, 3 * LANES), bf16),
-            ((total_rows, LANES), f32),
+            natural,
+            ((2, *blocked[0]), BF16),
+            ((2, *act[0]), F32),
+            folded,
+            ((10, 10, 16, 3 * LANES), BF16),
+            ((total_rows, LANES), F32),
         ],
         10**9,
-        6,
-    )(pre, turned, cotangent, other_up, w_down, w_up)
-    (grad_input,) = kernel_call(
+    )
+    (grad_input,) = run(
         input_kernel,
-        (shape(inputs.shape, bf16),),
-        [((8, 10, 16, 3 * LANES), bf16), ((4, 8, 16, LANES), f32)],
+        (slab, w_conv),
+        [(inputs.shape, BF16)],
+        [((8, 10, 16, 3 * LANES), BF16), natural],
         10**9,
-        2,
-    )(slab, w_conv)
+    )
 
     passed = swap_dp(passed, 1)
     crop_total = inputs.shape[0] * lax.axis_size("dp")

time: 36.5 us -> 34.4 us (0.942)
  waiting for transfers between devices: 15.5 us -> 13 us
  Pallas kernels: 5.78 us -> 6.24 us
    ppermute x3, waiting for transfers between devices: 5.4 us -> 2.95 us  [swap_x(): return lax.ppermute(value, 'sp', [(0, 1), (1, 0)])]
    pallas_call x3 -> x4, Pallas kernels: 5.78 us -> 6.24 us  [run(): pl.pallas_call(body, out_shape=tuple((jax.ShapeDtypeStruct(shape, kind) f...]
  transfers between devices with their start and end apart: 8 -> 8, of which waited for: 6 -> 8; matrix products, arithmetic and copies ran while one was open for 0% -> 0% of each run, Pallas kernels for 9% -> 12%
where the time goes in v3:
time: 34.4 us; the launch traced here: 34.2 us
  waiting for transfers between devices  13 us (38%)
  starting transfers between devices  11.2 us (33%)
  Pallas kernels  6.24 us (18%)
  local copies, waits for them, and re-layouts  2.1 us (6%)
  other arithmetic  0.96 us (3%)
  between operations  0.74 us (2%)
    ppermute x5, waiting for transfers between devices, swap_dp(): return lax.ppermute(value, 'dp', [(i, i ^ mask) for i in range(16)])  10 us
    ppermute x5, starting transfers between devices, swap_dp(): return lax.ppermute(value, 'dp', [(i, i ^ mask) for i in range(16)])  6.42 us
    pallas_call x4, Pallas kernels, run(): pl.pallas_call(body, out_shape=tuple((jax.ShapeDtypeStruct(shape, kind) f...  6.24 us
    ppermute x3, starting transfers between devices, swap_x(): return lax.ppermute(value, 'sp', [(0, 1), (1, 0)])  4.78 us
    ppermute x3, waiting for transfers between devices, swap_x(): return lax.ppermute(value, 'sp', [(0, 1), (1, 0)])  2.95 us
    unnamed x12, local copies, waits for them, and re-layouts  2.09 us
    reshape x1, other arithmetic, per_device_pairs(): grad_share = jnp.concatenate([low, high[2 * half - per_share:]]).reshape(-1)  0.71 us
  transfers between devices with their start and end apart: 8, of which 8 were waited for; matrix products, arithmetic and copies ran while one was open for 0% of the time, Pallas kernels for 12%

profile of v3, /device:TPU:0, one launch (start us, length us, event | category | flops | bytes accessed | tf_op | source)
XLA Modules:
  0.0 34.2 jit_solution(11949913769827709473)
XLA Ops:
  0.6 3.0 %collective-permute-start.1 = (bf16[2,4,8,8,128]{4,3,2,1,0:T(8,128)(2,1)}, bf16[2,4,8,8,128]{4,3,2,1,0:T(8,128)(2,1)S(1)}, u32[]{:S(2)}, u32[]{:S(2)}) collective-permute-start(bf16[2,4,8,8,128]{4,3,2,1,0:T(8,128)(2,1)} %in_ref.1), channel_id=1, source_target_pairs={{0,16},{16,0},{1,17},{17,1},{2,18},{18,2},{3,19},{19,3},{4,20},{20... | collective-permute-start | bytes 393224 | tf_op jit(solution)/shard_map/ppermute | solution.py:139
  3.6 0.1 collective-permute-start
  3.7 1.2 %copy-done = bf16[3456,128]{1,0:T(8,128)(2,1)S(1)} copy-done((bf16[3456,128]{1,0:T(8,128)(2,1)S(1)}, bf16[3456,128]{1,0:T(8,128)(2,1)}, u32[]{:S(2)}) %copy-start) | copy-done | bytes 884760
  4.9 0.0 copy-start.4
  4.9 0.9 %copy-done.4 = bf16[2,4,8,8,128]{4,3,2,1,0:T(8,128)(2,1)S(1)} copy-done((bf16[2,4,8,8,128]{4,3,2,1,0:T(8,128)(2,1)S(1)}, bf16[2,4,8,8,128]{4,3,2,1,0:T(8,128)(2,1)}, u32[]{:S(2)}) %copy-start.4) | copy-done | bytes 131096
  5.8 0.0 copy-start.1
  5.8 0.0 copy-start.2
  5.8 0.8 %shard_map.68 = (f32[6,128,128]{2,1,0:T(8,128)S(1)}, bf16[128,512]{1,0:T(8,128)(2,1)S(1)}) custom-call(bf16[2,4,8,8,128]{4,3,2,1,0:T(8,128)(2,1)S(1)} %copy-done.4, bf16[3456,128]{1,0:T(8,128)(2,1)S(1)} %copy-done), custom_call_target="tpu_custom_call" | custom-call | flops 1000000000 | bytes 2097152 | tf_op jit(solution)/shard_map/pallas_call | solution.py:416
  6.6 1.6 %collective-permute-done.1.in_ref = bf16[2,4,8,8,128]{4,3,2,1,0:T(8,128)(2,1)S(1)} collective-permute-done((bf16[2,4,8,8,128]{4,3,2,1,0:T(8,128)(2,1)}, bf16[2,4,8,8,128]{4,3,2,1,0:T(8,128)(2,1)S(1)}, u32[]{:S(2)}, u32[]{:S(2)}) %collective-permute-start.1) | collective-permute-done | bytes 131104 | tf_op jit(solution)/shard_map/ppermute | solution.py:139
  8.2 0.0 copy-done.1
  8.2 0.0 copy-done.2
  8.2 0.0 copy-done.3
  8.2 0.0 copy-done.5
  8.2 1.4 %shard_map.69 = (f32[4,2,4,2,2,8,128]{6,5,4,3,2,1,0:T(8,128)S(1)}, bf16[2,128,512]{2,1,0:T(8,128)(2,1)S(1)}, bf16[1024,128]{1,0:T(8,128)(2,1)S(1)}, bf16[256,128...) custom-call(bf16[2,4,8,8,128]{4,3,2,1,0:T(8,128)(2,1)S(1)} %collective-permute-, ...), custom_call_target="tpu_custom_call" | custom-call | flops 1000000000 | bytes 2097152 | tf_op jit(solution)/shard_map/pallas_call | solution.py:416
  9.6 0.6 %collective-permute-done.up_ref = bf16[2,4,8,8,128]{4,3,2,1,0:T(8,128)(2,1)S(1)} collective-permute-done((bf16[2,4,8,8,128]{4,3,2,1,0:T(8,128)(2,1)}, bf16[2,4,8,8,128]{4,3,2,1,0:T(8,128)(2,1)S(1)}, u32[]{:S(2)}, u32[]{:S(2)}) %collective-permute-start) | collective-permute-done | bytes 131104 | tf_op jit(solution)/shard_map/ppermute | solution.py:139
  10.2 2.3 %shard_map.70 = (bf16[8,240,128]{2,1,0:T(8,128)(2,1)S(1)}, bf16[8,240,128]{2,1,0:T(8,128)(2,1)S(1)}, bf16[6,8,16,128]{3,2,1,0:T(8,128)(2,1)S(1)}) custom-call(bf16[2,4,8,8,128]{4,3,2,1,0:T(8,128)(2,1)S(1)} %collective-permute-done.up_ref, f32[4,2,4,2,2,8,128]{6,5,4,3,2,1,0:T(8,128)S(1)} %get-tuple-element.16.slope_ref, ...), custom_call_target="tpu_custom_call" | custom-call | flops 1000000000 | bytes 2097152 | tf_op jit(solution)/shard_map/pallas_call | solution.py:416
  12.4 0.1 collective-permute-start.2
  12.5 1.8 %collective-permute-done.2 = bf16[8,240,128]{2,1,0:T(8,128)(2,1)S(1)} collective-permute-done((bf16[8,240,128]{2,1,0:T(8,128)(2,1)S(1)}, bf16[8,240,128]{2,1,0:T(8,128)(2,1)S(1)}, u32[]{:S(2)}, u32[]{:S(2)}) %collective-permute-start.2) | collective-permute-done | bytes 491552 | tf_op jit(solution)/shard_map/ppermute | solution.py:143
  14.4 0.1 fusion.2
  14.5 1.8 %collective-permute-start.3 = (bf16[2,240,128]{2,1,0:T(8,128)(2,1)S(1)}, bf16[2,240,128]{2,1,0:T(8,128)(2,1)S(1)}, u32[]{:S(2)}, u32[]{:S(2)}) collective-permute-start(bf16[2,240,128]{2,1,0:T(8,128)(2,1)S(1)} %get-tuple-element.26), channel_id=1, source_target_pairs={{0,2},{1,3},{2,0},{3,1},{4,6},{5,7},{6,4},{7,5},{8,10},{9,11},{10,... | collective-permute-start | bytes 368648 | tf_op jit(solution)/shard_map/ppermute | solution.py:143
  16.3 1.6 %collective-permute-start.4 = (bf16[2,240,128]{2,1,0:T(8,128)(2,1)S(1)}, bf16[2,240,128]{2,1,0:T(8,128)(2,1)S(1)}, u32[]{:S(2)}, u32[]{:S(2)}) collective-permute-start(bf16[2,240,128]{2,1,0:T(8,128)(2,1)S(1)} %get-tuple-element.27), channel_id=1, source_target_pairs={{0,4},{1,5},{2,6},{3,7},{4,0},{5,1},{6,2},{7,3},{8,12},{9,13},{10,... | collective-permute-start | bytes 368648 | tf_op jit(solution)/shard_map/ppermute | solution.py:143
  17.9 0.1 collective-permute-start.5
  18.0 1.9 %collective-permute-done.3 = bf16[2,240,128]{2,1,0:T(8,128)(2,1)S(1)} collective-permute-done((bf16[2,240,128]{2,1,0:T(8,128)(2,1)S(1)}, bf16[2,240,128]{2,1,0:T(8,128)(2,1)S(1)}, u32[]{:S(2)}, u32[]{:S(2)}) %collective-permute-start.3) | collective-permute-done | bytes 122912 | tf_op jit(solution)/shard_map/ppermute | solution.py:143
  19.9 2.6 %collective-permute-done.4 = bf16[2,240,128]{2,1,0:T(8,128)(2,1)S(1)} collective-permute-done((bf16[2,240,128]{2,1,0:T(8,128)(2,1)S(1)}, bf16[2,240,128]{2,1,0:T(8,128)(2,1)S(1)}, u32[]{:S(2)}, u32[]{:S(2)}) %collective-permute-start.4) | collective-permute-done | bytes 122912 | tf_op jit(solution)/shard_map/ppermute | solution.py:143
  22.5 1.3 %collective-permute-done.5 = bf16[2,240,128]{2,1,0:T(8,128)(2,1)S(1)} collective-permute-done((bf16[2,240,128]{2,1,0:T(8,128)(2,1)S(1)}, bf16[2,240,128]{2,1,0:T(8,128)(2,1)S(1)}, u32[]{:S(2)}, u32[]{:S(2)}) %collective-permute-start.5) | collective-permute-done | bytes 122912 | tf_op jit(solution)/shard_map/ppermute | solution.py:143
  23.8 0.1 fusion.1
  23.9 2.8 %collective-permute-start.6 = (bf16[240,128]{1,0:T(8,128)(2,1)S(1)}, bf16[240,128]{1,0:T(8,128)(2,1)S(1)}, u32[]{:S(2)}, u32[]{:S(2)}) collective-permute-start(bf16[240,128]{1,0:T(8,128)(2,1)S(1)} %fusion.6), channel_id=1, source_target_pairs={{0,8},{1,9},{2,10},{3,11},{4,12},{5,13},{6,14},{7,15},{8,0},{9,1},... | collective-permute-start | bytes 184328 | tf_op jit(solution)/shard_map/ppermute | solution.py:143
  26.7 2.4 %collective-permute-done.6 = bf16[240,128]{1,0:T(8,128)(2,1)S(1)} collective-permute-done((bf16[240,128]{1,0:T(8,128)(2,1)S(1)}, bf16[240,128]{1,0:T(8,128)(2,1)S(1)}, u32[]{:S(2)}, u32[]{:S(2)}) %collective-permute-start.6) | collective-permute-done | bytes 61472 | tf_op jit(solution)/shard_map/ppermute | solution.py:143
  29.2 1.7 %collective-permute-start.7 = (bf16[240,128]{1,0:T(8,128)(2,1)S(1)}, bf16[240,128]{1,0:T(8,128)(2,1)S(1)}, u32[]{:S(2)}, u32[]{:S(2)}) collective-permute-start(bf16[240,128]{1,0:T(8,128)(2,1)S(1)} %fusion.5), channel_id=1, source_target_pairs={{0,16},{16,0},{1,17},{17,1},{2,18},{18,2},{3,19},{19,3},{4,20},{20... | collective-permute-start | bytes 184328 | tf_op jit(solution)/shard_map/ppermute | solution.py:139
  30.9 1.8 %shard_map.71 = bf16[2,4,8,8,128]{4,3,2,1,0:T(8,128)(2,1)} custom-call(bf16[6,8,16,128]{3,2,1,0:T(8,128)(2,1)S(1)} %get-tuple-element.23.slab_ref, bf16[3456,128]{1,0:T(8,128)(2,1)S(1)} %copy-done.1), custom_call_target="tpu_custom_call" | custom-call | flops 1000000000 | bytes 2097152 | tf_op jit(solution)/shard_map/pallas_call | solution.py:416
  32.6 0.8 %collective-permute-done.7 = bf16[240,128]{1,0:T(8,128)(2,1)S(1)} collective-permute-done((bf16[240,128]{1,0:T(8,128)(2,1)S(1)}, bf16[240,128]{1,0:T(8,128)(2,1)S(1)}, u32[]{:S(2)}, u32[]{:S(2)}) %collective-permute-start.7) | collective-permute-done | bytes 61472 | tf_op jit(solution)/shard_map/ppermute | solution.py:139
  33.5 0.7 %maximum_bitcast_fusion = f32[60416]{0:T(1024)} fusion(f32[232,128]{1,0:T(8,128)S(1)} %convert_multiply_fusion.1, f32[240,128]{1,0:T(8,128)S(1)} %convert_multiply_fusion), kind=kLoop, calls=%fused_computation.6 | loop fusion | flops 60416 | bytes 483328 | tf_op jit(solution)/shard_map/reshape | solution.py:488
  (8 shorter events, 0.1 us)
Async XLA Ops:
  0.6 7.5 %collective-permute-start.1 = (bf16[2,4,8,8,128]{4,3,2,1,0:T(8,128)(2,1)}, bf16[2,4,8,8,128]{4,3,2,1,0:T(8,128)(2,1)S(1)}, u32[]{:S(2)}, u32[]{:S(2)}) collective-permute-start(bf16[2,4,8,8,128]{4,3,2,1,0:T(8,128)(2,1)} %in_ref.1), channel_id=1, source_target_pairs={{0,16},{16,0},{1,17},{17,1},{2,18},{18,2},{3,19},{19,3},{4,20},{20... | collective-permute-start | bytes 393224 | tf_op jit(solution)/shard_map/ppermute | solution.py:139
  3.6 6.5 %collective-permute-start = (bf16[2,4,8,8,128]{4,3,2,1,0:T(8,128)(2,1)}, bf16[2,4,8,8,128]{4,3,2,1,0:T(8,128)(2,1)S(1)}, u32[]{:S(2)}, u32[]{:S(2)}) collective-permute-start(bf16[2,4,8,8,128]{4,3,2,1,0:T(8,128)(2,1)} %up_ref.1), channel_id=1, source_target_pairs={{0,16},{16,0},{1,17},{17,1},{2,18},{18,2},{3,19},{19,3},{4,20},{20... | collective-permute-start | bytes 393224 | tf_op jit(solution)/shard_map/ppermute | solution.py:139
  3.7 1.2 %copy-start = (bf16[3456,128]{1,0:T(8,128)(2,1)S(1)}, bf16[3456,128]{1,0:T(8,128)(2,1)}, u32[]{:S(2)}) copy-start(bf16[3456,128]{1,0:T(8,128)(2,1)} %w_ref.5) | copy-start | bytes 2654212
  4.9 0.9 %copy-start.4 = (bf16[2,4,8,8,128]{4,3,2,1,0:T(8,128)(2,1)S(1)}, bf16[2,4,8,8,128]{4,3,2,1,0:T(8,128)(2,1)}, u32[]{:S(2)}) copy-start(bf16[2,4,8,8,128]{4,3,2,1,0:T(8,128)(2,1)} %in_ref.1) | copy-start | bytes 393220
  5.8 2.4 %copy-start.1 = (bf16[3456,128]{1,0:T(8,128)(2,1)S(1)}, bf16[3456,128]{1,0:T(8,128)(2,1)}, u32[]{:S(2)}) copy-start(bf16[3456,128]{1,0:T(8,128)(2,1)} %w_ref.5) | copy-start | bytes 2654212
  5.8 2.4 %copy-start.2 = (bf16[1024,256]{1,0:T(8,128)(2,1)S(1)}, bf16[1024,256]{1,0:T(8,128)(2,1)}, u32[]{:S(2)}) copy-start(bf16[1024,256]{1,0:T(8,128)(2,1)} %w_down_ref.3) | copy-start | bytes 1572868
  5.8 2.4 %copy-start.3 = (bf16[2048,128]{1,0:T(8,128)(2,1)S(1)}, bf16[2048,128]{1,0:T(8,128)(2,1)}, u32[]{:S(2)}) copy-start(bf16[2048,128]{1,0:T(8,128)(2,1)} %w_up_ref.3) | copy-start | bytes 1572868
  5.8 2.4 %copy-start.5 = (bf16[2,4,8,8,128]{4,3,2,1,0:T(8,128)(2,1)S(1)}, bf16[2,4,8,8,128]{4,3,2,1,0:T(8,128)(2,1)}, u32[]{:S(2)}) copy-start(bf16[2,4,8,8,128]{4,3,2,1,0:T(8,128)(2,1)} %up_ref.1) | copy-start | bytes 393220
  12.4 1.9 %collective-permute-start.2 = (bf16[8,240,128]{2,1,0:T(8,128)(2,1)S(1)}, bf16[8,240,128]{2,1,0:T(8,128)(2,1)S(1)}, u32[]{:S(2)}, u32[]{:S(2)}) collective-permute-start(bf16[8,240,128]{2,1,0:T(8,128)(2,1)S(1)} %get-tuple-element.25), channel_id=1, source_target_pairs={{0,1},{1,0},{2,3},{3,2},{4,5},{5,4},{6,7},{7,6},{8,9},{9,8},{10,11... | collective-permute-start | bytes 1474568 | tf_op jit(solution)/shard_map/ppermute | solution.py:143
  14.5 5.5 %collective-permute-start.3 = (bf16[2,240,128]{2,1,0:T(8,128)(2,1)S(1)}, bf16[2,240,128]{2,1,0:T(8,128)(2,1)S(1)}, u32[]{:S(2)}, u32[]{:S(2)}) collective-permute-start(bf16[2,240,128]{2,1,0:T(8,128)(2,1)S(1)} %get-tuple-element.26), channel_id=1, source_target_pairs={{0,2},{1,3},{2,0},{3,1},{4,6},{5,7},{6,4},{7,5},{8,10},{9,11},{10,... | collective-permute-start | bytes 368648 | tf_op jit(solution)/shard_map/ppermute | solution.py:143
  16.3 6.2 %collective-permute-start.4 = (bf16[2,240,128]{2,1,0:T(8,128)(2,1)S(1)}, bf16[2,240,128]{2,1,0:T(8,128)(2,1)S(1)}, u32[]{:S(2)}, u32[]{:S(2)}) collective-permute-start(bf16[2,240,128]{2,1,0:T(8,128)(2,1)S(1)} %get-tuple-element.27), channel_id=1, source_target_pairs={{0,4},{1,5},{2,6},{3,7},{4,0},{5,1},{6,2},{7,3},{8,12},{9,13},{10,... | collective-permute-start | bytes 368648 | tf_op jit(solution)/shard_map/ppermute | solution.py:143
  17.9 5.9 %collective-permute-start.5 = (bf16[2,240,128]{2,1,0:T(8,128)(2,1)S(1)}, bf16[2,240,128]{2,1,0:T(8,128)(2,1)S(1)}, u32[]{:S(2)}, u32[]{:S(2)}) collective-permute-start(bf16[2,240,128]{2,1,0:T(8,128)(2,1)S(1)} %fusion.4), channel_id=1, source_target_pairs={{0,6},{1,7},{2,4},{3,5},{4,2},{5,3},{6,0},{7,1},{8,14},{9,15},{10,... | collective-permute-start | bytes 368648 | tf_op jit(solution)/shard_map/ppermute | solution.py:143
  23.9 5.2 %collective-permute-start.6 = (bf16[240,128]{1,0:T(8,128)(2,1)S(1)}, bf16[240,128]{1,0:T(8,128)(2,1)S(1)}, u32[]{:S(2)}, u32[]{:S(2)}) collective-permute-start(bf16[240,128]{1,0:T(8,128)(2,1)S(1)} %fusion.6), channel_id=1, source_target_pairs={{0,8},{1,9},{2,10},{3,11},{4,12},{5,13},{6,14},{7,15},{8,0},{9,1},... | collective-permute-start | bytes 184328 | tf_op jit(solution)/shard_map/ppermute | solution.py:143
  29.2 4.3 %collective-permute-start.7 = (bf16[240,128]{1,0:T(8,128)(2,1)S(1)}, bf16[240,128]{1,0:T(8,128)(2,1)S(1)}, u32[]{:S(2)}, u32[]{:S(2)}) collective-permute-start(bf16[240,128]{1,0:T(8,128)(2,1)S(1)} %fusion.5), channel_id=1, source_target_pairs={{0,16},{16,0},{1,17},{17,1},{2,18},{18,2},{3,19},{19,3},{4,20},{20... | collective-permute-start | bytes 184328 | tf_op jit(solution)/shard_map/ppermute | solution.py:139

commit v4 on v3

--- a/solution.py
+++ b/solution.py
@@ -1,3 +1,5 @@
+import functools
+
 import jax
 import jax.numpy as jnp
 from jax import lax
@@ -139,44 +141,53 @@
     return lax.ppermute(value, "sp", [(0, 1), (1, 0)])
 
 
-def swap_dp(value, mask):
-    return lax.ppermute(value, "dp", [(i, i ^ mask) for i in range(16)])
+def swap_dp(value, mask, odd_mask=None):
+    masks = (mask, mask if odd_mask is None else odd_mask)
+    return lax.ppermute(value, "dp", [(i, i ^ masks[i % 2]) for i in range(16)])
 
 
 def pick(value, dim, index):
     return lax.dynamic_index_in_dim(value, index, dim, keepdims=False)
 
 
-def sum_shares(mine, passed, scale):
-    at = lax.axis_index("dp")
+def square_sum(mine, passed):
+    here = (lax.axis_index("dp") >> 1) & 3
+
+    def chip_sum(index):
+        return pick(mine, 1, index).astype(jnp.float32) + pick(passed, 1, index).astype(
+            jnp.float32
+        )
+
+    core = lax.axis_index("dp") & 1
+    received = [
+        swap_dp(chip_sum(here ^ jnp.where(core == 0, even, odd)).astype(jnp.bfloat16), 2 * even, 2 * odd)
+        for even, odd in ((1, 3), (2, 1), (3, 2))
+    ]
+    total = chip_sum(here)
+    for part in received:
+        total += part.astype(jnp.float32)
+    return total
+
+
+def end_sum(square, scale, pieces):
+    far = (lax.axis_index("dp") >> 3) & 1
     side = lax.axis_index("sp")
-    row, near, far = (at >> 1) & 1, (at >> 2) & 1, (at >> 3) & 1
-
-    def chip_sum(z, y):
-        return pick(pick(mine, 1, z), 1, y).astype(jnp.float32) + pick(
-            pick(passed, 1, z), 1, y
-        ).astype(jnp.float32)
-
-    diagonal = swap_dp(chip_sum(1 - near, 1 - row).astype(jnp.bfloat16), 6)
-    along_y = swap_dp(chip_sum(near, 1 - row).astype(jnp.bfloat16), 2)
-    along_z = swap_dp(chip_sum(1 - near, row).astype(jnp.bfloat16), 4)
-    square = (
-        chip_sum(near, row)
-        + along_y.astype(jnp.float32)
-        + along_z.astype(jnp.float32)
-        + diagonal.astype(jnp.float32)
-    )
-    across = swap_dp(pick(square, 0, 1 - far).astype(jnp.bfloat16), 8)
-    total = (pick(square, 0, far) + across.astype(jnp.float32)).astype(jnp.bfloat16)
-    other = swap_x(total)
-    low = jnp.where(side == 0, total, other)
-    high = jnp.where(side == 0, other, total)
-    return low.astype(jnp.float32) * scale, high.astype(jnp.float32) * scale
+    sent = pick(square, 0, 1 - far).astype(jnp.bfloat16)
+    kept = pick(square, 0, far)
+    lows, highs = [], []
+    received = [swap_dp(sent[first:last], 8) for first, last in pieces]
+    for (first, last), part in zip(pieces, received):
+        total = (kept[first:last] + part.astype(jnp.float32)).astype(jnp.bfloat16)
+        other = swap_x(total)
+        lows.append(jnp.where(side == 0, total, other).astype(jnp.float32) * scale)
+        highs.append(jnp.where(side == 0, other, total).astype(jnp.float32) * scale)
+    return lows, highs
 
 
 LANES = 128
 VMEM = pl.BlockSpec(memory_space=pltpu.VMEM)
 BF16, F32 = jnp.bfloat16, jnp.float32
+CHUNK = 10
 PLACES = tuple((i, j, k) for i in range(2) for j in range(2) for k in range(2))
 
 
@@ -355,7 +366,7 @@
         pl.ds(side * (planes // 2), planes // 2 + 2), 1:9, :, LANES : 2 * LANES
     ]
 
-    deep = w_down_ref.shape[1]
+    deep = deep_act_ref.shape[0]
     grad_up = dot(deep_act_ref[...], upstream)
     down_at = 27 * LANES
     up_at = down_at + 8 * deep
@@ -368,26 +379,50 @@
         rows_ref[pl.ds(down_at + part, 8 * LANES, stride=deep // LANES), :] = grad_down[
             :, part * LANES : (part + 1) * LANES
         ]
-    turned = across([turned_ref[0], turned_ref[1]])
-    for i in range(3):
-        cells = across(
-            [
-                taps_ref[i : i + planes, j : j + 8].reshape(planes * 128, 3 * LANES)
-                for j in range(3)
-            ]
+    for half in range(2):
+        pl.when(side == half)(
+            functools.partial(
+                weight_rows,
+                half,
+                core,
+                turned_ref,
+                taps_ref,
+                rows_ref,
+                mine_ref,
+                passed_ref,
+            )
         )
-        sums = dot(turned, cells)
-        for tap in range(9):
-            at = (26 - 9 * i - tap) * LANES
-            rows_ref[at : at + LANES, :] = sums[:, tap * LANES : (tap + 1) * LANES]
+
+
+def weight_rows(side, core, turned_ref, taps_ref, rows_ref, mine_ref, passed_ref):
     share = rows_ref.shape[0] // 16
     half = mine_ref.shape[1]
+    starts = [at * share + side * (share - half) for at in range(16)]
+    kept = [
+        tap
+        for tap in range(27)
+        if any(at < (tap + 1) * LANES and tap * LANES < at + half for at in starts)
+    ]
+    turned = across([turned_ref[0], turned_ref[1]])
+    planes = taps_ref.shape[0] - 2
+    size = planes * 128
+    for first in range(0, len(kept), CHUNK):
+        group = kept[first : first + CHUNK]
+        cells = []
+        for tap in group:
+            i, j, k = (26 - tap) // 9, (26 - tap) // 3 % 3, (26 - tap) % 3
+            cells.append(
+                taps_ref[i : i + planes, j : j + 8, :, k * LANES : (k + 1) * LANES].reshape(
+                    size, LANES
+                )
+            )
+        sums = dot(turned, across(cells))
+        for at, tap in enumerate(group):
+            rows_ref[tap * LANES : (tap + 1) * LANES, :] = sums[:, at * LANES : (at + 1) * LANES]
     for pair in range(8):
-        at = 2 * pair * share + side * (share - half)
-        keep = pl.multiple_of(at + core * share, 8)
-        give = pl.multiple_of(at + (1 - core) * share, 8)
-        mine_ref[pair] = rows_ref[pl.ds(keep, half), :].astype(BF16)
-        passed_ref[pair] = rows_ref[pl.ds(give, half), :].astype(BF16)
+        for target, owner in ((mine_ref, core), (passed_ref, 1 - core)):
+            rows = pl.ds(pl.multiple_of(starts[2 * pair] + owner * share, 8), half)
+            target[pair] = rows_ref[rows, :].astype(BF16)
 
 
 def input_kernel(slab_ref, w_ref, out_ref, taps_ref, natural_ref):
@@ -480,12 +515,13 @@
         10**9,
     )
 
-    passed = swap_dp(passed, 1)
+    grid = (2, 4, half, LANES)
+    square = square_sum(mine.reshape(grid), swap_dp(passed, 1).reshape(grid))
     crop_total = inputs.shape[0] * lax.axis_size("dp")
     scale = 1.0 / jnp.sqrt(jnp.float32(crop_total * inputs.shape[2] ** 3))
-    grid = (2, 2, 2, half, LANES)
-    low, high = sum_shares(mine.reshape(grid), passed.reshape(grid), scale)
-    grad_share = jnp.concatenate([low, high[2 * half - per_share :]]).reshape(-1)
+    lows, highs = end_sum(square, scale, ((0, half),))
+    highs[0] = highs[0][2 * half - per_share :]
+    grad_share = jnp.concatenate(lows + highs).reshape(-1)
     return (grad_input, grad_share)
 
 

time: 34.4 us -> 34 us (0.988)
  no operation moved by 1% of the time
where the time goes in v4:
time: 34 us; the launch traced here: 33.8 us
  waiting for transfers between devices  13 us (38%)
  starting transfers between devices  11.1 us (33%)
  Pallas kernels  5.98 us (18%)
  local copies, waits for them, and re-layouts  2.1 us (6%)
  other arithmetic  0.95 us (3%)
  between operations  0.75 us (2%)
    ppermute x5, waiting for transfers between devices, swap_dp(): return lax.ppermute(value, 'dp', [(i, i ^ masks[i % 2]) for i in range(16)])  10 us
    ppermute x5, starting transfers between devices, swap_dp(): return lax.ppermute(value, 'dp', [(i, i ^ masks[i % 2]) for i in range(16)])  6.33 us
    pallas_call x4, Pallas kernels, run(): pl.pallas_call(body, out_shape=tuple((jax.ShapeDtypeStruct(shape, kind) f...  5.98 us
    ppermute x3, starting transfers between devices, swap_x(): return lax.ppermute(value, 'sp', [(0, 1), (1, 0)])  4.74 us
    ppermute x3, waiting for transfers between devices, swap_x(): return lax.ppermute(value, 'sp', [(0, 1), (1, 0)])  2.99 us
    unnamed x12, local copies, waits for them, and re-layouts  2.09 us
    reshape x1, other arithmetic, per_device_pairs(): grad_share = jnp.concatenate(lows + highs).reshape(-1)  0.71 us
  transfers between devices with their start and end apart: 8, of which 8 were waited for; matrix products, arithmetic and copies ran while one was open for 0% of the time, Pallas kernels for 12%

profile of v4, /device:TPU:0, one launch (start us, length us, event | category | flops | bytes accessed | tf_op | source)
XLA Modules:
  0.0 33.8 jit_solution(8408411760847356681)
XLA Ops:
  0.6 3.0 %collective-permute-start.1 = (bf16[2,4,8,8,128]{4,3,2,1,0:T(8,128)(2,1)}, bf16[2,4,8,8,128]{4,3,2,1,0:T(8,128)(2,1)S(1)}, u32[]{:S(2)}, u32[]{:S(2)}) collective-permute-start(bf16[2,4,8,8,128]{4,3,2,1,0:T(8,128)(2,1)} %in_ref.1), channel_id=1, source_target_pairs={{0,16},{16,0},{1,17},{17,1},{2,18},{18,2},{3,19},{19,3},{4,20},{20... | collective-permute-start | bytes 393224 | tf_op jit(solution)/shard_map/ppermute | solution.py:141
  3.6 0.1 collective-permute-start
  3.7 0.0 copy-start
  3.7 1.2 %copy-done = bf16[3456,128]{1,0:T(8,128)(2,1)S(1)} copy-done((bf16[3456,128]{1,0:T(8,128)(2,1)S(1)}, bf16[3456,128]{1,0:T(8,128)(2,1)}, u32[]{:S(2)}) %copy-start) | copy-done | bytes 884760
  4.9 0.0 copy-start.4
  4.9 0.9 %copy-done.4 = bf16[2,4,8,8,128]{4,3,2,1,0:T(8,128)(2,1)S(1)} copy-done((bf16[2,4,8,8,128]{4,3,2,1,0:T(8,128)(2,1)S(1)}, bf16[2,4,8,8,128]{4,3,2,1,0:T(8,128)(2,1)}, u32[]{:S(2)}) %copy-start.4) | copy-done | bytes 131096
  5.8 0.0 copy-start.1
  5.8 0.8 %shard_map.68 = (f32[6,128,128]{2,1,0:T(8,128)S(1)}, bf16[128,512]{1,0:T(8,128)(2,1)S(1)}) custom-call(bf16[2,4,8,8,128]{4,3,2,1,0:T(8,128)(2,1)S(1)} %copy-done.4, bf16[3456,128]{1,0:T(8,128)(2,1)S(1)} %copy-done), custom_call_target="tpu_custom_call" | custom-call | flops 1000000000 | bytes 2097152 | tf_op jit(solution)/shard_map/pallas_call | solution.py:451
  6.6 1.6 %collective-permute-done.1.in_ref = bf16[2,4,8,8,128]{4,3,2,1,0:T(8,128)(2,1)S(1)} collective-permute-done((bf16[2,4,8,8,128]{4,3,2,1,0:T(8,128)(2,1)}, bf16[2,4,8,8,128]{4,3,2,1,0:T(8,128)(2,1)S(1)}, u32[]{:S(2)}, u32[]{:S(2)}) %collective-permute-start.1) | collective-permute-done | bytes 131104 | tf_op jit(solution)/shard_map/ppermute | solution.py:141
  8.2 0.0 copy-done.1
  8.2 0.0 copy-done.2
  8.2 0.0 copy-done.3
  8.2 0.0 copy-done.5
  8.2 1.4 %shard_map.69 = (f32[4,2,4,2,2,8,128]{6,5,4,3,2,1,0:T(8,128)S(1)}, bf16[2,128,512]{2,1,0:T(8,128)(2,1)S(1)}, bf16[1024,128]{1,0:T(8,128)(2,1)S(1)}, bf16[256,128...) custom-call(bf16[2,4,8,8,128]{4,3,2,1,0:T(8,128)(2,1)S(1)} %collective-permute-, ...), custom_call_target="tpu_custom_call" | custom-call | flops 1000000000 | bytes 2097152 | tf_op jit(solution)/shard_map/pallas_call | solution.py:451
  9.6 0.6 %collective-permute-done.up_ref = bf16[2,4,8,8,128]{4,3,2,1,0:T(8,128)(2,1)S(1)} collective-permute-done((bf16[2,4,8,8,128]{4,3,2,1,0:T(8,128)(2,1)}, bf16[2,4,8,8,128]{4,3,2,1,0:T(8,128)(2,1)S(1)}, u32[]{:S(2)}, u32[]{:S(2)}) %collective-permute-start) | collective-permute-done | bytes 131104 | tf_op jit(solution)/shard_map/ppermute | solution.py:141
  10.2 2.0 %shard_map.70 = (bf16[8,240,128]{2,1,0:T(8,128)(2,1)S(1)}, bf16[8,240,128]{2,1,0:T(8,128)(2,1)S(1)}, bf16[6,8,16,128]{3,2,1,0:T(8,128)(2,1)S(1)}) custom-call(bf16[2,4,8,8,128]{4,3,2,1,0:T(8,128)(2,1)S(1)} %collective-permute-done.up_ref, f32[4,2,4,2,2,8,128]{6,5,4,3,2,1,0:T(8,128)S(1)} %get-tuple-element.16.slope_ref, ...), custom_call_target="tpu_custom_call" | custom-call | flops 1000000000 | bytes 2097152 | tf_op jit(solution)/shard_map/pallas_call | solution.py:451
  12.2 0.1 collective-permute-start.2
  12.3 1.8 %collective-permute-done.2 = bf16[8,240,128]{2,1,0:T(8,128)(2,1)S(1)} collective-permute-done((bf16[8,240,128]{2,1,0:T(8,128)(2,1)S(1)}, bf16[8,240,128]{2,1,0:T(8,128)(2,1)S(1)}, u32[]{:S(2)}, u32[]{:S(2)}) %collective-permute-start.2) | collective-permute-done | bytes 491552 | tf_op jit(solution)/shard_map/ppermute | solution.py:146
  14.1 0.1 fusion.2
  14.2 1.8 %collective-permute-start.3 = (bf16[2,240,128]{2,1,0:T(8,128)(2,1)S(1)}, bf16[2,240,128]{2,1,0:T(8,128)(2,1)S(1)}, u32[]{:S(2)}, u32[]{:S(2)}) collective-permute-start(bf16[2,240,128]{2,1,0:T(8,128)(2,1)S(1)} %get-tuple-element.26), channel_id=1, source_target_pairs={{0,2},{1,7},{2,0},{3,5},{4,6},{5,3},{6,4},{7,1},{8,10},{9,15},{10,... | collective-permute-start | bytes 368648 | tf_op jit(solution)/shard_map/ppermute | solution.py:146
  16.0 1.6 %collective-permute-start.4 = (bf16[2,240,128]{2,1,0:T(8,128)(2,1)S(1)}, bf16[2,240,128]{2,1,0:T(8,128)(2,1)S(1)}, u32[]{:S(2)}, u32[]{:S(2)}) collective-permute-start(bf16[2,240,128]{2,1,0:T(8,128)(2,1)S(1)} %get-tuple-element.27), channel_id=1, source_target_pairs={{0,4},{1,3},{2,6},{3,1},{4,0},{5,7},{6,2},{7,5},{8,12},{9,11},{10,... | collective-permute-start | bytes 368648 | tf_op jit(solution)/shard_map/ppermute | solution.py:146
  17.6 0.2 collective-permute-start.5
  17.8 3.5 %collective-permute-done.3 = bf16[2,240,128]{2,1,0:T(8,128)(2,1)S(1)} collective-permute-done((bf16[2,240,128]{2,1,0:T(8,128)(2,1)S(1)}, bf16[2,240,128]{2,1,0:T(8,128)(2,1)S(1)}, u32[]{:S(2)}, u32[]{:S(2)}) %collective-permute-start.3) | collective-permute-done | bytes 122912 | tf_op jit(solution)/shard_map/ppermute | solution.py:146
  21.3 0.6 %collective-permute-done.4 = bf16[2,240,128]{2,1,0:T(8,128)(2,1)S(1)} collective-permute-done((bf16[2,240,128]{2,1,0:T(8,128)(2,1)S(1)}, bf16[2,240,128]{2,1,0:T(8,128)(2,1)S(1)}, u32[]{:S(2)}, u32[]{:S(2)}) %collective-permute-start.4) | collective-permute-done | bytes 122912 | tf_op jit(solution)/shard_map/ppermute | solution.py:146
  22.0 1.5 %collective-permute-done.5 = bf16[2,240,128]{2,1,0:T(8,128)(2,1)S(1)} collective-permute-done((bf16[2,240,128]{2,1,0:T(8,128)(2,1)S(1)}, bf16[2,240,128]{2,1,0:T(8,128)(2,1)S(1)}, u32[]{:S(2)}, u32[]{:S(2)}) %collective-permute-start.5) | collective-permute-done | bytes 122912 | tf_op jit(solution)/shard_map/ppermute | solution.py:146
  23.5 0.1 fusion.1
  23.6 2.6 %collective-permute-start.6 = (bf16[240,128]{1,0:T(8,128)(2,1)S(1)}, bf16[240,128]{1,0:T(8,128)(2,1)S(1)}, u32[]{:S(2)}, u32[]{:S(2)}) collective-permute-start(bf16[240,128]{1,0:T(8,128)(2,1)S(1)} %fusion.6), channel_id=1, source_target_pairs={{0,8},{1,9},{2,10},{3,11},{4,12},{5,13},{6,14},{7,15},{8,0},{9,1},... | collective-permute-start | bytes 184328 | tf_op jit(solution)/shard_map/ppermute | solution.py:146
  26.2 2.5 %collective-permute-done.6 = bf16[240,128]{1,0:T(8,128)(2,1)S(1)} collective-permute-done((bf16[240,128]{1,0:T(8,128)(2,1)S(1)}, bf16[240,128]{1,0:T(8,128)(2,1)S(1)}, u32[]{:S(2)}, u32[]{:S(2)}) %collective-permute-start.6) | collective-permute-done | bytes 61472 | tf_op jit(solution)/shard_map/ppermute | solution.py:146
  28.8 1.7 %collective-permute-start.7 = (bf16[240,128]{1,0:T(8,128)(2,1)S(1)}, bf16[240,128]{1,0:T(8,128)(2,1)S(1)}, u32[]{:S(2)}, u32[]{:S(2)}) collective-permute-start(bf16[240,128]{1,0:T(8,128)(2,1)S(1)} %fusion.5), channel_id=1, source_target_pairs={{0,16},{16,0},{1,17},{17,1},{2,18},{18,2},{3,19},{19,3},{4,20},{20... | collective-permute-start | bytes 184328 | tf_op jit(solution)/shard_map/ppermute | solution.py:141
  30.5 1.8 %shard_map.71 = bf16[2,4,8,8,128]{4,3,2,1,0:T(8,128)(2,1)} custom-call(bf16[6,8,16,128]{3,2,1,0:T(8,128)(2,1)S(1)} %get-tuple-element.23.slab_ref, bf16[3456,128]{1,0:T(8,128)(2,1)S(1)} %copy-done.1), custom_call_target="tpu_custom_call" | custom-call | flops 1000000000 | bytes 2097152 | tf_op jit(solution)/shard_map/pallas_call | solution.py:451
  32.2 0.8 %collective-permute-done.7 = bf16[240,128]{1,0:T(8,128)(2,1)S(1)} collective-permute-done((bf16[240,128]{1,0:T(8,128)(2,1)S(1)}, bf16[240,128]{1,0:T(8,128)(2,1)S(1)}, u32[]{:S(2)}, u32[]{:S(2)}) %collective-permute-start.7) | collective-permute-done | bytes 61472 | tf_op jit(solution)/shard_map/ppermute | solution.py:141
  33.1 0.7 %maximum_bitcast_fusion = f32[60416]{0:T(1024)} fusion(f32[232,128]{1,0:T(8,128)S(1)} %convert_multiply_fusion.1, f32[240,128]{1,0:T(8,128)S(1)} %convert_multiply_fusion), kind=kLoop, calls=%fused_computation.6 | loop fusion | flops 60416 | bytes 483328 | tf_op jit(solution)/shard_map/reshape | solution.py:524
  (8 shorter events, 0.1 us)
Async XLA Ops:
  0.6 7.5 %collective-permute-start.1 = (bf16[2,4,8,8,128]{4,3,2,1,0:T(8,128)(2,1)}, bf16[2,4,8,8,128]{4,3,2,1,0:T(8,128)(2,1)S(1)}, u32[]{:S(2)}, u32[]{:S(2)}) collective-permute-start(bf16[2,4,8,8,128]{4,3,2,1,0:T(8,128)(2,1)} %in_ref.1), channel_id=1, source_target_pairs={{0,16},{16,0},{1,17},{17,1},{2,18},{18,2},{3,19},{19,3},{4,20},{20... | collective-permute-start | bytes 393224 | tf_op jit(solution)/shard_map/ppermute | solution.py:141
  3.6 6.5 %collective-permute-start = (bf16[2,4,8,8,128]{4,3,2,1,0:T(8,128)(2,1)}, bf16[2,4,8,8,128]{4,3,2,1,0:T(8,128)(2,1)S(1)}, u32[]{:S(2)}, u32[]{:S(2)}) collective-permute-start(bf16[2,4,8,8,128]{4,3,2,1,0:T(8,128)(2,1)} %up_ref.1), channel_id=1, source_target_pairs={{0,16},{16,0},{1,17},{17,1},{2,18},{18,2},{3,19},{19,3},{4,20},{20... | collective-permute-start | bytes 393224 | tf_op jit(solution)/shard_map/ppermute | solution.py:141
  3.7 1.2 %copy-start = (bf16[3456,128]{1,0:T(8,128)(2,1)S(1)}, bf16[3456,128]{1,0:T(8,128)(2,1)}, u32[]{:S(2)}) copy-start(bf16[3456,128]{1,0:T(8,128)(2,1)} %w_ref.5) | copy-start | bytes 2654212
  4.9 0.9 %copy-start.4 = (bf16[2,4,8,8,128]{4,3,2,1,0:T(8,128)(2,1)S(1)}, bf16[2,4,8,8,128]{4,3,2,1,0:T(8,128)(2,1)}, u32[]{:S(2)}) copy-start(bf16[2,4,8,8,128]{4,3,2,1,0:T(8,128)(2,1)} %in_ref.1) | copy-start | bytes 393220
  5.8 2.4 %copy-start.1 = (bf16[3456,128]{1,0:T(8,128)(2,1)S(1)}, bf16[3456,128]{1,0:T(8,128)(2,1)}, u32[]{:S(2)}) copy-start(bf16[3456,128]{1,0:T(8,128)(2,1)} %w_ref.5) | copy-start | bytes 2654212
  5.8 2.4 %copy-start.2 = (bf16[1024,256]{1,0:T(8,128)(2,1)S(1)}, bf16[1024,256]{1,0:T(8,128)(2,1)}, u32[]{:S(2)}) copy-start(bf16[1024,256]{1,0:T(8,128)(2,1)} %w_down_ref.3) | copy-start | bytes 1572868
  5.8 2.4 %copy-start.3 = (bf16[2048,128]{1,0:T(8,128)(2,1)S(1)}, bf16[2048,128]{1,0:T(8,128)(2,1)}, u32[]{:S(2)}) copy-start(bf16[2048,128]{1,0:T(8,128)(2,1)} %w_up_ref.3) | copy-start | bytes 1572868
  5.8 2.4 %copy-start.5 = (bf16[2,4,8,8,128]{4,3,2,1,0:T(8,128)(2,1)S(1)}, bf16[2,4,8,8,128]{4,3,2,1,0:T(8,128)(2,1)}, u32[]{:S(2)}) copy-start(bf16[2,4,8,8,128]{4,3,2,1,0:T(8,128)(2,1)} %up_ref.1) | copy-start | bytes 393220
  12.2 1.9 %collective-permute-start.2 = (bf16[8,240,128]{2,1,0:T(8,128)(2,1)S(1)}, bf16[8,240,128]{2,1,0:T(8,128)(2,1)S(1)}, u32[]{:S(2)}, u32[]{:S(2)}) collective-permute-start(bf16[8,240,128]{2,1,0:T(8,128)(2,1)S(1)} %get-tuple-element.25), channel_id=1, source_target_pairs={{0,1},{1,0},{2,3},{3,2},{4,5},{5,4},{6,7},{7,6},{8,9},{9,8},{10,11... | collective-permute-start | bytes 1474568 | tf_op jit(solution)/shard_map/ppermute | solution.py:146
  14.2 7.2 %collective-permute-start.3 = (bf16[2,240,128]{2,1,0:T(8,128)(2,1)S(1)}, bf16[2,240,128]{2,1,0:T(8,128)(2,1)S(1)}, u32[]{:S(2)}, u32[]{:S(2)}) collective-permute-start(bf16[2,240,128]{2,1,0:T(8,128)(2,1)S(1)} %get-tuple-element.26), channel_id=1, source_target_pairs={{0,2},{1,7},{2,0},{3,5},{4,6},{5,3},{6,4},{7,1},{8,10},{9,15},{10,... | collective-permute-start | bytes 368648 | tf_op jit(solution)/shard_map/ppermute | solution.py:146
  16.0 6.0 %collective-permute-start.4 = (bf16[2,240,128]{2,1,0:T(8,128)(2,1)S(1)}, bf16[2,240,128]{2,1,0:T(8,128)(2,1)S(1)}, u32[]{:S(2)}, u32[]{:S(2)}) collective-permute-start(bf16[2,240,128]{2,1,0:T(8,128)(2,1)S(1)} %get-tuple-element.27), channel_id=1, source_target_pairs={{0,4},{1,3},{2,6},{3,1},{4,0},{5,7},{6,2},{7,5},{8,12},{9,11},{10,... | collective-permute-start | bytes 368648 | tf_op jit(solution)/shard_map/ppermute | solution.py:146
  17.6 5.8 %collective-permute-start.5 = (bf16[2,240,128]{2,1,0:T(8,128)(2,1)S(1)}, bf16[2,240,128]{2,1,0:T(8,128)(2,1)S(1)}, u32[]{:S(2)}, u32[]{:S(2)}) collective-permute-start(bf16[2,240,128]{2,1,0:T(8,128)(2,1)S(1)} %fusion.4), channel_id=1, source_target_pairs={{0,6},{1,5},{2,4},{3,7},{4,2},{5,1},{6,0},{7,3},{8,14},{9,13},{10,... | collective-permute-start | bytes 368648 | tf_op jit(solution)/shard_map/ppermute | solution.py:146
  23.6 5.2 %collective-permute-start.6 = (bf16[240,128]{1,0:T(8,128)(2,1)S(1)}, bf16[240,128]{1,0:T(8,128)(2,1)S(1)}, u32[]{:S(2)}, u32[]{:S(2)}) collective-permute-start(bf16[240,128]{1,0:T(8,128)(2,1)S(1)} %fusion.6), channel_id=1, source_target_pairs={{0,8},{1,9},{2,10},{3,11},{4,12},{5,13},{6,14},{7,15},{8,0},{9,1},... | collective-permute-start | bytes 184328 | tf_op jit(solution)/shard_map/ppermute | solution.py:146
  28.8 4.3 %collective-permute-start.7 = (bf16[240,128]{1,0:T(8,128)(2,1)S(1)}, bf16[240,128]{1,0:T(8,128)(2,1)S(1)}, u32[]{:S(2)}, u32[]{:S(2)}) collective-permute-start(bf16[240,128]{1,0:T(8,128)(2,1)S(1)} %fusion.5), channel_id=1, source_target_pairs={{0,16},{16,0},{1,17},{17,1},{2,18},{18,2},{3,19},{19,3},{4,20},{20... | collective-permute-start | bytes 184328 | tf_op jit(solution)/shard_map/ppermute | solution.py:141

commit v5 on v4

--- a/solution.py
+++ b/solution.py
@@ -150,23 +150,16 @@
     return lax.dynamic_index_in_dim(value, index, dim, keepdims=False)
 
 
-def square_sum(mine, passed):
-    here = (lax.axis_index("dp") >> 1) & 3
-
-    def chip_sum(index):
-        return pick(mine, 1, index).astype(jnp.float32) + pick(passed, 1, index).astype(
-            jnp.float32
-        )
-
-    core = lax.axis_index("dp") & 1
+ORDER = ((1, 3), (2, 1), (3, 2))
+
+
+def square_sum(pieces, own):
     received = [
-        swap_dp(chip_sum(here ^ jnp.where(core == 0, even, odd)).astype(jnp.bfloat16), 2 * even, 2 * odd)
-        for even, odd in ((1, 3), (2, 1), (3, 2))
+        swap_dp(piece, 2 * even, 2 * odd) for piece, (even, odd) in zip(pieces, ORDER)
     ]
-    total = chip_sum(here)
     for part in received:
-        total += part.astype(jnp.float32)
-    return total
+        own += part.astype(jnp.float32)
+    return own
 
 
 def end_sum(square, scale, pieces):
@@ -187,7 +180,8 @@
 LANES = 128
 VMEM = pl.BlockSpec(memory_space=pltpu.VMEM)
 BF16, F32 = jnp.bfloat16, jnp.float32
-CHUNK = 10
+SHARE = 472
+HALF = 240
 PLACES = tuple((i, j, k) for i in range(2) for j in range(2) for k in range(2))
 
 
@@ -332,11 +326,12 @@
     mine_ref,
     passed_ref,
     slab_ref,
+    taps_ref,
+    down_ref,
     natural_ref,
     blocks_ref,
     act_ref,
     folded_ref,
-    taps_ref,
     rows_ref,
 ):
     side = lax.axis_index("sp")
@@ -379,50 +374,79 @@
         rows_ref[pl.ds(down_at + part, 8 * LANES, stride=deep // LANES), :] = grad_down[
             :, part * LANES : (part + 1) * LANES
         ]
-    for half in range(2):
-        pl.when(side == half)(
-            functools.partial(
-                weight_rows,
-                half,
-                core,
-                turned_ref,
-                taps_ref,
-                rows_ref,
-                mine_ref,
-                passed_ref,
+    down_ref[...] = rows_ref[down_at : down_at + down_ref.shape[0], :]
+
+    def give(own_side, other):
+        conv_rows(own_side, other, turned_ref, taps_ref, rows_ref)
+        keep_rows(own_side, other, range(8), rows_ref, passed_ref)
+        keep_rows(own_side, 1 - other, range(4, 8), rows_ref, mine_ref)
+
+    for_place(side, 1 - core, give)
+
+
+def for_place(side, owner, body):
+    for own_side in range(2):
+        for own_owner in range(2):
+            pl.when((side == own_side) & (owner == own_owner))(
+                functools.partial(body, own_side, own_owner)
             )
-        )
-
-
-def weight_rows(side, core, turned_ref, taps_ref, rows_ref, mine_ref, passed_ref):
-    share = rows_ref.shape[0] // 16
-    half = mine_ref.shape[1]
-    starts = [at * share + side * (share - half) for at in range(16)]
+
+
+def window(side, owner, pair):
+    return (2 * pair + owner) * SHARE + side * (SHARE - HALF)
+
+
+def conv_rows(side, owner, turned_ref, taps_ref, rows_ref):
+    starts = [window(side, owner, pair) for pair in range(8)]
     kept = [
         tap
         for tap in range(27)
-        if any(at < (tap + 1) * LANES and tap * LANES < at + half for at in starts)
+        if any(at < (tap + 1) * LANES and tap * LANES < at + HALF for at in starts)
     ]
     turned = across([turned_ref[0], turned_ref[1]])
     planes = taps_ref.shape[0] - 2
     size = planes * 128
-    for first in range(0, len(kept), CHUNK):
-        group = kept[first : first + CHUNK]
-        cells = []
-        for tap in group:
-            i, j, k = (26 - tap) // 9, (26 - tap) // 3 % 3, (26 - tap) % 3
-            cells.append(
-                taps_ref[i : i + planes, j : j + 8, :, k * LANES : (k + 1) * LANES].reshape(
-                    size, LANES
-                )
-            )
-        sums = dot(turned, across(cells))
-        for at, tap in enumerate(group):
-            rows_ref[tap * LANES : (tap + 1) * LANES, :] = sums[:, at * LANES : (at + 1) * LANES]
-    for pair in range(8):
-        for target, owner in ((mine_ref, core), (passed_ref, 1 - core)):
-            rows = pl.ds(pl.multiple_of(starts[2 * pair] + owner * share, 8), half)
-            target[pair] = rows_ref[rows, :].astype(BF16)
+    cells = []
+    for tap in kept:
+        i, j, k = (26 - tap) // 9, (26 - tap) // 3 % 3, (26 - tap) % 3
+        cells.append(
+            taps_ref[i : i + planes, j : j + 8, :, k * LANES : (k + 1) * LANES].reshape(size, LANES)
+        )
+    sums = dot(turned, across(cells))
+    for at, tap in enumerate(kept):
+        rows_ref[tap * LANES : (tap + 1) * LANES, :] = sums[:, at * LANES : (at + 1) * LANES]
+
+
+def keep_rows(side, owner, pairs, rows_ref, target_ref):
+    for at, pair in enumerate(pairs):
+        first = window(side, owner, pair)
+        target_ref[at] = rows_ref[first : first + HALF, :].astype(BF16)
+
+
+def own_rows_kernel(taps_ref, turned_ref, down_ref, mine_ref, rows_ref):
+    rows_ref[27 * LANES :, :] = down_ref[...]
+
+    def give(own_side, own_core):
+        conv_rows(own_side, own_core, turned_ref, taps_ref, rows_ref)
+        keep_rows(own_side, own_core, range(4), rows_ref, mine_ref)
+
+    for_place(lax.axis_index("sp"), lax.axis_index("dp") % 2, give)
+
+
+def chip_kernel(late_ref, early_ref, passed_ref, first_ref, second_ref, third_ref, own_ref):
+    at = lax.axis_index("dp")
+    here = (at >> 1) & 3
+    odd_core = at & 1
+
+    def chip_sum(far, index):
+        mine = (late_ref, early_ref)[far][index]
+        return mine.astype(F32) + passed_ref[4 * far + index].astype(F32)
+
+    for far in range(2):
+        for target, (even, odd) in zip((first_ref, second_ref, third_ref), ORDER):
+            index = here ^ (even + odd_core * (odd - even))
+            target[far] = chip_sum(far, index).astype(BF16)
+        own_ref[far] = chip_sum(far, here)
 
 
 def input_kernel(slab_ref, w_ref, out_ref, taps_ref, natural_ref):
@@ -491,20 +515,28 @@
         10**9,
     )
     total_rows = (w_conv.size + w_down.size + w_up.size) // LANES
-    per_share = total_rows // 16
-    half = -(-per_share // 32) * 16
-    mine, passed, slab = run(
+    conv_count = w_conv.size // LANES
+    taps = ((10, 10, 16, 3 * LANES), BF16)
+    given = ((4, HALF, LANES), BF16)
+    down = ((8 * SHARE - conv_count, LANES), F32)
+    early_mine, passed, slab, grad_taps, down_rows = run(
         backward_kernel,
         (other_up, *saved, w_down, w_up),
-        [((8, half, LANES), BF16), ((8, half, LANES), BF16), ((6, 8, 16, LANES), BF16)],
+        [given, ((8, HALF, LANES), BF16), ((6, 8, 16, LANES), BF16), taps, down],
         [
             natural,
             ((2, *blocked[0]), BF16),
             ((2, *act[0]), F32),
             folded,
-            ((10, 10, 16, 3 * LANES), BF16),
             ((total_rows, LANES), F32),
         ],
+        10**9,
+    )
+    (late_mine,) = run(
+        own_rows_kernel,
+        (grad_taps, saved[1], down_rows),
+        [given],
+        [((8 * SHARE, LANES), F32)],
         10**9,
     )
     (grad_input,) = run(
@@ -515,12 +547,19 @@
         10**9,
     )
 
-    grid = (2, 4, half, LANES)
-    square = square_sum(mine.reshape(grid), swap_dp(passed, 1).reshape(grid))
+    piece = ((2, HALF, LANES), BF16)
+    *pieces, own = run(
+        chip_kernel,
+        (late_mine, early_mine, swap_dp(passed, 1)),
+        [piece, piece, piece, (piece[0], F32)],
+        [],
+        10**6,
+    )
+    square = square_sum(pieces, own)
     crop_total = inputs.shape[0] * lax.axis_size("dp")
     scale = 1.0 / jnp.sqrt(jnp.float32(crop_total * inputs.shape[2] ** 3))
-    lows, highs = end_sum(square, scale, ((0, half),))
-    highs[0] = highs[0][2 * half - per_share :]
+    lows, highs = end_sum(square, scale, ((0, HALF),))
+    highs[0] = highs[0][2 * HALF - SHARE :]
     grad_share = jnp.concatenate(lows + highs).reshape(-1)
     return (grad_input, grad_share)
 

time: 34 us -> 33.5 us (0.985)
  waiting for transfers between devices: 13 us -> 12.4 us
    ppermute x5, waiting for transfers between devices: 10 us -> 9.37 us  [swap_dp(): return lax.ppermute(value, 'dp', [(i, i ^ masks[i % 2]) for i in range(16)])]
    pallas_call x4 -> x6, Pallas kernels: 5.98 us -> 6.23 us  [run(): pl.pallas_call(body, out_shape=tuple((jax.ShapeDtypeStruct(shape, kind) f...]
  transfers between devices with their start and end apart: 8 -> 8, of which waited for: 8 -> 8; matrix products, arithmetic and copies ran while one was open for 0% -> 0% of each run, Pallas kernels for 12% -> 13%
where the time goes in v5:
time: 33.5 us; the launch traced here: 33.4 us
  waiting for transfers between devices  12.4 us (37%)
  starting transfers between devices  11.1 us (33%)
  Pallas kernels  6.23 us (19%)
  local copies, waits for them, and re-layouts  2.1 us (6%)
  other arithmetic  0.83 us (2%)
  between operations  0.72 us (2%)
    ppermute x5, waiting for transfers between devices, swap_dp(): return lax.ppermute(value, 'dp', [(i, i ^ masks[i % 2]) for i in range(16)])  9.37 us
    ppermute x5, starting transfers between devices, swap_dp(): return lax.ppermute(value, 'dp', [(i, i ^ masks[i % 2]) for i in range(16)])  6.38 us
    pallas_call x6, Pallas kernels, run(): pl.pallas_call(body, out_shape=tuple((jax.ShapeDtypeStruct(shape, kind) f...  6.23 us
    ppermute x3, starting transfers between devices, swap_x(): return lax.ppermute(value, 'sp', [(0, 1), (1, 0)])  4.72 us
    ppermute x3, waiting for transfers between devices, swap_x(): return lax.ppermute(value, 'sp', [(0, 1), (1, 0)])  3.01 us
    unnamed x12, local copies, waits for them, and re-layouts  2.09 us
    reshape x1, other arithmetic, per_device_pairs(): grad_share = jnp.concatenate(lows + highs).reshape(-1)  0.71 us
  transfers between devices with their start and end apart: 8, of which 8 were waited for; matrix products, arithmetic and copies ran while one was open for 0% of the time, Pallas kernels for 13%

profile of v5, /device:TPU:0, one launch (start us, length us, event | category | flops | bytes accessed | tf_op | source)
XLA Modules:
  0.0 33.4 jit_solution(5018800113838579076)
XLA Ops:
  0.6 3.0 %collective-permute-start.1 = (bf16[2,4,8,8,128]{4,3,2,1,0:T(8,128)(2,1)}, bf16[2,4,8,8,128]{4,3,2,1,0:T(8,128)(2,1)S(1)}, u32[]{:S(2)}, u32[]{:S(2)}) collective-permute-start(bf16[2,4,8,8,128]{4,3,2,1,0:T(8,128)(2,1)} %in_ref.1), channel_id=1, source_target_pairs={{0,16},{16,0},{1,17},{17,1},{2,18},{18,2},{3,19},{19,3},{4,20},{20... | collective-permute-start | bytes 393224 | tf_op jit(solution)/shard_map/ppermute | solution.py:141
  3.6 0.1 collective-permute-start
  3.7 0.0 copy-start
  3.7 1.2 %copy-done = bf16[3456,128]{1,0:T(8,128)(2,1)S(1)} copy-done((bf16[3456,128]{1,0:T(8,128)(2,1)S(1)}, bf16[3456,128]{1,0:T(8,128)(2,1)}, u32[]{:S(2)}) %copy-start) | copy-done | bytes 884760
  4.9 0.0 copy-start.4
  4.9 0.9 %copy-done.4 = bf16[2,4,8,8,128]{4,3,2,1,0:T(8,128)(2,1)S(1)} copy-done((bf16[2,4,8,8,128]{4,3,2,1,0:T(8,128)(2,1)S(1)}, bf16[2,4,8,8,128]{4,3,2,1,0:T(8,128)(2,1)}, u32[]{:S(2)}) %copy-start.4) | copy-done | bytes 131096
  5.8 0.8 %shard_map.68 = (f32[6,128,128]{2,1,0:T(8,128)S(1)}, bf16[128,512]{1,0:T(8,128)(2,1)S(1)}) custom-call(bf16[2,4,8,8,128]{4,3,2,1,0:T(8,128)(2,1)S(1)} %copy-done.4, bf16[3456,128]{1,0:T(8,128)(2,1)S(1)} %copy-done), custom_call_target="tpu_custom_call" | custom-call | flops 1000000000 | bytes 2097152 | tf_op jit(solution)/shard_map/pallas_call | solution.py:475
  6.6 1.6 %collective-permute-done.1.in_ref = bf16[2,4,8,8,128]{4,3,2,1,0:T(8,128)(2,1)S(1)} collective-permute-done((bf16[2,4,8,8,128]{4,3,2,1,0:T(8,128)(2,1)}, bf16[2,4,8,8,128]{4,3,2,1,0:T(8,128)(2,1)S(1)}, u32[]{:S(2)}, u32[]{:S(2)}) %collective-permute-start.1) | collective-permute-done | bytes 131104 | tf_op jit(solution)/shard_map/ppermute | solution.py:141
  8.2 0.0 copy-done.1
  8.2 0.0 copy-done.2
  8.2 0.0 copy-done.3
  8.2 0.0 copy-done.5
  8.2 1.4 %shard_map.69 = (f32[4,2,4,2,2,8,128]{6,5,4,3,2,1,0:T(8,128)S(1)}, bf16[2,128,512]{2,1,0:T(8,128)(2,1)S(1)}, bf16[1024,128]{1,0:T(8,128)(2,1)S(1)}, bf16[256,128...) custom-call(bf16[2,4,8,8,128]{4,3,2,1,0:T(8,128)(2,1)S(1)} %collective-permute-, ...), custom_call_target="tpu_custom_call" | custom-call | flops 1000000000 | bytes 2097152 | tf_op jit(solution)/shard_map/pallas_call | solution.py:475
  9.6 0.6 %collective-permute-done.up_ref = bf16[2,4,8,8,128]{4,3,2,1,0:T(8,128)(2,1)S(1)} collective-permute-done((bf16[2,4,8,8,128]{4,3,2,1,0:T(8,128)(2,1)}, bf16[2,4,8,8,128]{4,3,2,1,0:T(8,128)(2,1)S(1)}, u32[]{:S(2)}, u32[]{:S(2)}) %collective-permute-start) | collective-permute-done | bytes 131104 | tf_op jit(solution)/shard_map/ppermute | solution.py:141
  10.2 1.6 %shard_map.70 = (bf16[4,240,128]{2,1,0:T(8,128)(2,1)S(1)}, bf16[8,240,128]{2,1,0:T(8,128)(2,1)S(1)}, bf16[6,8,16,128]{3,2,1,0:T(8,128)(2,1)S(1)}, bf16[10,10,16,384]{3,2,1,0:T(8,128)(2,1)S(1)}, f32[320,128]{1,0:T(8,128)S(1)}) custom-call(bf16[2,4,8,8,128]{4,3,2,1,0:T(8,128)(2,1)S(1)} %collective-permute-done.up_ref, ...), custom_call_target="tpu_custom_call" | custom-call | flops 1000000000 | bytes 2097152 | tf_op jit(solution)/shard_map/pallas_call | solution.py:475
  11.8 0.1 collective-permute-start.2
  11.9 0.5 %shard_map.72.late_ref = bf16[4,240,128]{2,1,0:T(8,128)(2,1)S(1)} custom-call(bf16[10,10,16,384]{3,2,1,0:T(8,128)(2,1)S(1)} %get-tuple-element.30.taps_ref, bf16[2,128,512]{2,1,0:T(8,128)(2,1)S(1)} %get-tuple-element.23.turned_ref, f32[320,128]{1,0:T(8,128)S(1)} %get-tuple-element.31.down_ref), custom_call_target="tpu_custom_call" | custom-call | flops 1000000000 | bytes 2097152 | tf_op jit(solution)/shard_map/pallas_call | solution.py:475
  12.4 1.3 %collective-permute-done.2.passed_ref = bf16[8,240,128]{2,1,0:T(8,128)(2,1)S(1)} collective-permute-done((bf16[8,240,128]{2,1,0:T(8,128)(2,1)S(1)}, bf16[8,240,128]{2,1,0:T(8,128)(2,1)S(1)}, u32[]{:S(2)}, u32[]{:S(2)}) %collective-permute-start.2) | collective-permute-done | bytes 491552 | tf_op jit(solution)/shard_map/ppermute | solution.py:146
  13.7 0.1 shard_map.73
  13.8 1.8 %collective-permute-start.3 = (bf16[2,240,128]{2,1,0:T(8,128)(2,1)S(1)}, bf16[2,240,128]{2,1,0:T(8,128)(2,1)S(1)}, u32[]{:S(2)}, u32[]{:S(2)}) collective-permute-start(bf16[2,240,128]{2,1,0:T(8,128)(2,1)S(1)} %get-tuple-element.35), channel_id=1, source_target_pairs={{0,2},{1,7},{2,0},{3,5},{4,6},{5,3},{6,4},{7,1},{8,10},{9,15},{10,... | collective-permute-start | bytes 368648 | tf_op jit(solution)/shard_map/ppermute | solution.py:146
  15.7 1.6 %collective-permute-start.4 = (bf16[2,240,128]{2,1,0:T(8,128)(2,1)S(1)}, bf16[2,240,128]{2,1,0:T(8,128)(2,1)S(1)}, u32[]{:S(2)}, u32[]{:S(2)}) collective-permute-start(bf16[2,240,128]{2,1,0:T(8,128)(2,1)S(1)} %get-tuple-element.36), channel_id=1, source_target_pairs={{0,4},{1,3},{2,6},{3,1},{4,0},{5,7},{6,2},{7,5},{8,12},{9,11},{10,... | collective-permute-start | bytes 368648 | tf_op jit(solution)/shard_map/ppermute | solution.py:146
  17.2 0.1 collective-permute-start.5
  17.4 3.6 %collective-permute-done.3 = bf16[2,240,128]{2,1,0:T(8,128)(2,1)S(1)} collective-permute-done((bf16[2,240,128]{2,1,0:T(8,128)(2,1)S(1)}, bf16[2,240,128]{2,1,0:T(8,128)(2,1)S(1)}, u32[]{:S(2)}, u32[]{:S(2)}) %collective-permute-start.3) | collective-permute-done | bytes 122912 | tf_op jit(solution)/shard_map/ppermute | solution.py:146
  21.0 0.8 %collective-permute-done.4 = bf16[2,240,128]{2,1,0:T(8,128)(2,1)S(1)} collective-permute-done((bf16[2,240,128]{2,1,0:T(8,128)(2,1)S(1)}, bf16[2,240,128]{2,1,0:T(8,128)(2,1)S(1)}, u32[]{:S(2)}, u32[]{:S(2)}) %collective-permute-start.4) | collective-permute-done | bytes 122912 | tf_op jit(solution)/shard_map/ppermute | solution.py:146
  21.7 1.3 %collective-permute-done.5 = bf16[2,240,128]{2,1,0:T(8,128)(2,1)S(1)} collective-permute-done((bf16[2,240,128]{2,1,0:T(8,128)(2,1)S(1)}, bf16[2,240,128]{2,1,0:T(8,128)(2,1)S(1)}, u32[]{:S(2)}, u32[]{:S(2)}) %collective-permute-start.5) | collective-permute-done | bytes 122912 | tf_op jit(solution)/shard_map/ppermute | solution.py:146
  23.0 0.1 convert_add_fusion
  23.1 2.8 %collective-permute-start.6 = (bf16[240,128]{1,0:T(8,128)(2,1)S(1)}, bf16[240,128]{1,0:T(8,128)(2,1)S(1)}, u32[]{:S(2)}, u32[]{:S(2)}) collective-permute-start(bf16[240,128]{1,0:T(8,128)(2,1)S(1)} %fusion.1), channel_id=1, source_target_pairs={{0,8},{1,9},{2,10},{3,11},{4,12},{5,13},{6,14},{7,15},{8,0},{9,1},... | collective-permute-start | bytes 184328 | tf_op jit(solution)/shard_map/ppermute | solution.py:146
  25.9 2.4 %collective-permute-done.6 = bf16[240,128]{1,0:T(8,128)(2,1)S(1)} collective-permute-done((bf16[240,128]{1,0:T(8,128)(2,1)S(1)}, bf16[240,128]{1,0:T(8,128)(2,1)S(1)}, u32[]{:S(2)}, u32[]{:S(2)}) %collective-permute-start.6) | collective-permute-done | bytes 61472 | tf_op jit(solution)/shard_map/ppermute | solution.py:146
  28.3 1.6 %collective-permute-start.7 = (bf16[240,128]{1,0:T(8,128)(2,1)S(1)}, bf16[240,128]{1,0:T(8,128)(2,1)S(1)}, u32[]{:S(2)}, u32[]{:S(2)}) collective-permute-start(bf16[240,128]{1,0:T(8,128)(2,1)S(1)} %fusion), channel_id=1, source_target_pairs={{0,16},{16,0},{1,17},{17,1},{2,18},{18,2},{3,19},{19,3},{4,20},{20... | collective-permute-start | bytes 184328 | tf_op jit(solution)/shard_map/ppermute | solution.py:141
  30.0 1.8 %shard_map.71 = bf16[2,4,8,8,128]{4,3,2,1,0:T(8,128)(2,1)} custom-call(bf16[6,8,16,128]{3,2,1,0:T(8,128)(2,1)S(1)} %get-tuple-element.29.slab_ref, bf16[3456,128]{1,0:T(8,128)(2,1)S(1)} %copy-done.1), custom_call_target="tpu_custom_call" | custom-call | flops 1000000000 | bytes 2097152 | tf_op jit(solution)/shard_map/pallas_call | solution.py:475
  31.7 0.9 %collective-permute-done.7 = bf16[240,128]{1,0:T(8,128)(2,1)S(1)} collective-permute-done((bf16[240,128]{1,0:T(8,128)(2,1)S(1)}, bf16[240,128]{1,0:T(8,128)(2,1)S(1)}, u32[]{:S(2)}, u32[]{:S(2)}) %collective-permute-start.7) | collective-permute-done | bytes 61472 | tf_op jit(solution)/shard_map/ppermute | solution.py:141
  32.7 0.7 %maximum_bitcast_fusion = f32[60416]{0:T(1024)} fusion(f32[232,128]{1,0:T(8,128)S(1)} %convert_multiply_fusion.1, f32[240,128]{1,0:T(8,128)S(1)} %convert_multiply_fusion), kind=kLoop, calls=%fused_computation.1 | loop fusion | flops 60416 | bytes 483328 | tf_op jit(solution)/shard_map/reshape | solution.py:563
  (8 shorter events, 0.1 us)
Async XLA Ops:
  0.6 7.5 %collective-permute-start.1 = (bf16[2,4,8,8,128]{4,3,2,1,0:T(8,128)(2,1)}, bf16[2,4,8,8,128]{4,3,2,1,0:T(8,128)(2,1)S(1)}, u32[]{:S(2)}, u32[]{:S(2)}) collective-permute-start(bf16[2,4,8,8,128]{4,3,2,1,0:T(8,128)(2,1)} %in_ref.1), channel_id=1, source_target_pairs={{0,16},{16,0},{1,17},{17,1},{2,18},{18,2},{3,19},{19,3},{4,20},{20... | collective-permute-start | bytes 393224 | tf_op jit(solution)/shard_map/ppermute | solution.py:141
  3.6 6.5 %collective-permute-start = (bf16[2,4,8,8,128]{4,3,2,1,0:T(8,128)(2,1)}, bf16[2,4,8,8,128]{4,3,2,1,0:T(8,128)(2,1)S(1)}, u32[]{:S(2)}, u32[]{:S(2)}) collective-permute-start(bf16[2,4,8,8,128]{4,3,2,1,0:T(8,128)(2,1)} %up_ref.1), channel_id=1, source_target_pairs={{0,16},{16,0},{1,17},{17,1},{2,18},{18,2},{3,19},{19,3},{4,20},{20... | collective-permute-start | bytes 393224 | tf_op jit(solution)/shard_map/ppermute | solution.py:141
  3.7 1.2 %copy-start = (bf16[3456,128]{1,0:T(8,128)(2,1)S(1)}, bf16[3456,128]{1,0:T(8,128)(2,1)}, u32[]{:S(2)}) copy-start(bf16[3456,128]{1,0:T(8,128)(2,1)} %w_ref.5) | copy-start | bytes 2654212
  4.9 0.9 %copy-start.4 = (bf16[2,4,8,8,128]{4,3,2,1,0:T(8,128)(2,1)S(1)}, bf16[2,4,8,8,128]{4,3,2,1,0:T(8,128)(2,1)}, u32[]{:S(2)}) copy-start(bf16[2,4,8,8,128]{4,3,2,1,0:T(8,128)(2,1)} %in_ref.1) | copy-start | bytes 393220
  5.8 2.4 %copy-start.1 = (bf16[3456,128]{1,0:T(8,128)(2,1)S(1)}, bf16[3456,128]{1,0:T(8,128)(2,1)}, u32[]{:S(2)}) copy-start(bf16[3456,128]{1,0:T(8,128)(2,1)} %w_ref.5) | copy-start | bytes 2654212
  5.8 2.4 %copy-start.2 = (bf16[1024,256]{1,0:T(8,128)(2,1)S(1)}, bf16[1024,256]{1,0:T(8,128)(2,1)}, u32[]{:S(2)}) copy-start(bf16[1024,256]{1,0:T(8,128)(2,1)} %w_down_ref.3) | copy-start | bytes 1572868
  5.8 2.4 %copy-start.3 = (bf16[2048,128]{1,0:T(8,128)(2,1)S(1)}, bf16[2048,128]{1,0:T(8,128)(2,1)}, u32[]{:S(2)}) copy-start(bf16[2048,128]{1,0:T(8,128)(2,1)} %w_up_ref.3) | copy-start | bytes 1572868
  5.8 2.4 %copy-start.5 = (bf16[2,4,8,8,128]{4,3,2,1,0:T(8,128)(2,1)S(1)}, bf16[2,4,8,8,128]{4,3,2,1,0:T(8,128)(2,1)}, u32[]{:S(2)}) copy-start(bf16[2,4,8,8,128]{4,3,2,1,0:T(8,128)(2,1)} %up_ref.1) | copy-start | bytes 393220
  11.8 1.9 %collective-permute-start.2 = (bf16[8,240,128]{2,1,0:T(8,128)(2,1)S(1)}, bf16[8,240,128]{2,1,0:T(8,128)(2,1)S(1)}, u32[]{:S(2)}, u32[]{:S(2)}) collective-permute-start(bf16[8,240,128]{2,1,0:T(8,128)(2,1)S(1)} %get-tuple-element.33), channel_id=1, source_target_pairs={{0,1},{1,0},{2,3},{3,2},{4,5},{5,4},{6,7},{7,6},{8,9},{9,8},{10,11... | collective-permute-start | bytes 1474568 | tf_op jit(solution)/shard_map/ppermute | solution.py:146
  13.8 7.2 %collective-permute-start.3 = (bf16[2,240,128]{2,1,0:T(8,128)(2,1)S(1)}, bf16[2,240,128]{2,1,0:T(8,128)(2,1)S(1)}, u32[]{:S(2)}, u32[]{:S(2)}) collective-permute-start(bf16[2,240,128]{2,1,0:T(8,128)(2,1)S(1)} %get-tuple-element.35), channel_id=1, source_target_pairs={{0,2},{1,7},{2,0},{3,5},{4,6},{5,3},{6,4},{7,1},{8,10},{9,15},{10,... | collective-permute-start | bytes 368648 | tf_op jit(solution)/shard_map/ppermute | solution.py:146
  15.7 6.1 %collective-permute-start.4 = (bf16[2,240,128]{2,1,0:T(8,128)(2,1)S(1)}, bf16[2,240,128]{2,1,0:T(8,128)(2,1)S(1)}, u32[]{:S(2)}, u32[]{:S(2)}) collective-permute-start(bf16[2,240,128]{2,1,0:T(8,128)(2,1)S(1)} %get-tuple-element.36), channel_id=1, source_target_pairs={{0,4},{1,3},{2,6},{3,1},{4,0},{5,7},{6,2},{7,5},{8,12},{9,11},{10,... | collective-permute-start | bytes 368648 | tf_op jit(solution)/shard_map/ppermute | solution.py:146
  17.2 5.8 %collective-permute-start.5 = (bf16[2,240,128]{2,1,0:T(8,128)(2,1)S(1)}, bf16[2,240,128]{2,1,0:T(8,128)(2,1)S(1)}, u32[]{:S(2)}, u32[]{:S(2)}) collective-permute-start(bf16[2,240,128]{2,1,0:T(8,128)(2,1)S(1)} %get-tuple-element.37), channel_id=1, source_target_pairs={{0,6},{1,5},{2,4},{3,7},{4,2},{5,1},{6,0},{7,3},{8,14},{9,13},{10,... | collective-permute-start | bytes 368648 | tf_op jit(solution)/shard_map/ppermute | solution.py:146
  23.1 5.2 %collective-permute-start.6 = (bf16[240,128]{1,0:T(8,128)(2,1)S(1)}, bf16[240,128]{1,0:T(8,128)(2,1)S(1)}, u32[]{:S(2)}, u32[]{:S(2)}) collective-permute-start(bf16[240,128]{1,0:T(8,128)(2,1)S(1)} %fusion.1), channel_id=1, source_target_pairs={{0,8},{1,9},{2,10},{3,11},{4,12},{5,13},{6,14},{7,15},{8,0},{9,1},... | collective-permute-start | bytes 184328 | tf_op jit(solution)/shard_map/ppermute | solution.py:146
  28.3 4.3 %collective-permute-start.7 = (bf16[240,128]{1,0:T(8,128)(2,1)S(1)}, bf16[240,128]{1,0:T(8,128)(2,1)S(1)}, u32[]{:S(2)}, u32[]{:S(2)}) collective-permute-start(bf16[240,128]{1,0:T(8,128)(2,1)S(1)} %fusion), channel_id=1, source_target_pairs={{0,16},{16,0},{1,17},{17,1},{2,18},{18,2},{3,19},{19,3},{4,20},{20... | collective-permute-start | bytes 184328 | tf_op jit(solution)/shard_map/ppermute | solution.py:141

commit v6 on v5

--- a/solution.py
+++ b/solution.py
@@ -182,6 +182,7 @@
 BF16, F32 = jnp.bfloat16, jnp.float32
 SHARE = 472
 HALF = 240
+EARLY = 2
 PLACES = tuple((i, j, k) for i in range(2) for j in range(2) for k in range(2))
 
 
@@ -324,7 +325,8 @@
     w_down_ref,
     w_up_ref,
     mine_ref,
-    passed_ref,
+    first_ref,
+    rest_ref,
     slab_ref,
     taps_ref,
     down_ref,
@@ -375,10 +377,18 @@
             :, part * LANES : (part + 1) * LANES
         ]
     down_ref[...] = rows_ref[down_at : down_at + down_ref.shape[0], :]
+    here = (lax.axis_index("dp") >> 1) & 3
 
     def give(own_side, other):
         conv_rows(own_side, other, turned_ref, taps_ref, rows_ref)
-        keep_rows(own_side, other, range(8), rows_ref, passed_ref)
+        steps = [step[other] for step in ORDER] + [0]
+        for far in range(2):
+            for place, step in enumerate(steps):
+                start = window(own_side, other, 4 * far + (here ^ step))
+                target, slot = (first_ref, place) if place < EARLY else (rest_ref, place - EARLY)
+                target[2 * slot + far] = rows_ref[
+                    pl.ds(pl.multiple_of(start, 8), HALF), :
+                ].astype(BF16)
         keep_rows(own_side, 1 - other, range(4, 8), rows_ref, mine_ref)
 
     for_place(side, 1 - core, give)
@@ -433,20 +443,13 @@
     for_place(lax.axis_index("sp"), lax.axis_index("dp") % 2, give)
 
 
-def chip_kernel(late_ref, early_ref, passed_ref, first_ref, second_ref, third_ref, own_ref):
+def chip_kernel(steps, late_ref, early_ref, passed_ref, *targets):
     at = lax.axis_index("dp")
-    here = (at >> 1) & 3
-    odd_core = at & 1
-
-    def chip_sum(far, index):
-        mine = (late_ref, early_ref)[far][index]
-        return mine.astype(F32) + passed_ref[4 * far + index].astype(F32)
-
-    for far in range(2):
-        for target, (even, odd) in zip((first_ref, second_ref, third_ref), ORDER):
-            index = here ^ (even + odd_core * (odd - even))
-            target[far] = chip_sum(far, index).astype(BF16)
-        own_ref[far] = chip_sum(far, here)
+    for place, ((even, odd), target) in enumerate(zip(steps, targets)):
+        index = ((at >> 1) & 3) ^ (even + (at & 1) * (odd - even))
+        for far, mine_ref in enumerate((late_ref, early_ref)):
+            total = mine_ref[index].astype(F32) + passed_ref[2 * place + far].astype(F32)
+            target[far] = total.astype(target.dtype)
 
 
 def input_kernel(slab_ref, w_ref, out_ref, taps_ref, natural_ref):
@@ -478,7 +481,7 @@
         in_specs=[VMEM] * len(operands),
         out_specs=(VMEM,) * len(outs),
         scratch_shapes=[pltpu.VMEM(shape, kind) for shape, kind in scratch],
-        compiler_params=pltpu.CompilerParams(vmem_limit_bytes=40 << 20),
+        compiler_params=pltpu.CompilerParams(vmem_limit_bytes=24 << 20),
         cost_estimate=pl.CostEstimate(flops=flops, bytes_accessed=1 << 21, transcendentals=0),
     )(*operands)
 
@@ -519,10 +522,17 @@
     taps = ((10, 10, 16, 3 * LANES), BF16)
     given = ((4, HALF, LANES), BF16)
     down = ((8 * SHARE - conv_count, LANES), F32)
-    early_mine, passed, slab, grad_taps, down_rows = run(
+    early_mine, first, rest, slab, grad_taps, down_rows = run(
         backward_kernel,
         (other_up, *saved, w_down, w_up),
-        [given, ((8, HALF, LANES), BF16), ((6, 8, 16, LANES), BF16), taps, down],
+        [
+            given,
+            ((2 * EARLY, HALF, LANES), BF16),
+            ((8 - 2 * EARLY, HALF, LANES), BF16),
+            ((6, 8, 16, LANES), BF16),
+            taps,
+            down,
+        ],
         [
             natural,
             ((2, *blocked[0]), BF16),
@@ -547,13 +557,19 @@
         10**9,
     )
 
-    piece = ((2, HALF, LANES), BF16)
-    *pieces, own = run(
-        chip_kernel,
-        (late_mine, early_mine, swap_dp(passed, 1)),
-        [piece, piece, piece, (piece[0], F32)],
-        [],
-        10**6,
+    first, rest = swap_dp(first, 1), swap_dp(rest, 1)
+    sums = [((2, HALF, LANES), BF16)] * 3 + [((2, HALF, LANES), F32)]
+    steps = (*ORDER, (0, 0))
+    *pieces, own = (
+        part
+        for passed, places in ((first, slice(0, EARLY)), (rest, slice(EARLY, 4)))
+        for part in run(
+            functools.partial(chip_kernel, steps[places]),
+            (late_mine, early_mine, passed),
+            sums[places],
+            [],
+            10**6,
+        )
     )
     square = square_sum(pieces, own)
     crop_total = inputs.shape[0] * lax.axis_size("dp")

time: 33.5 us -> 33.3 us (level)
  waiting for transfers between devices: 12.4 us -> 11.8 us
  starting transfers between devices: 11.1 us -> 11.5 us
    ppermute x5 -> x6, waiting for transfers between devices: 9.37 us -> 8.63 us  [swap_dp(): return lax.ppermute(value, 'dp', [(i, i ^ masks[i % 2]) for i in range(16)])]
    ppermute x5 -> x6, starting transfers between devices: 6.38 us -> 6.84 us  [swap_dp(): return lax.ppermute(value, 'dp', [(i, i ^ masks[i % 2]) for i in range(16)])]
    pallas_call x6 -> x7, Pallas kernels: 6.23 us -> 6.31 us  [run(): pl.pallas_call(body, out_shape=tuple((jax.ShapeDtypeStruct(shape, kind) f...]
  transfers between devices with their start and end apart: 8 -> 9, of which waited for: 8 -> 8; matrix products, arithmetic and copies ran while one was open for 0% -> 0% of each run, Pallas kernels for 13% -> 14%
where the time goes in v6:
time: 33.3 us; the launch traced here: 33.2 us
  waiting for transfers between devices  11.8 us (35%)
  starting transfers between devices  11.5 us (35%)
  Pallas kernels  6.31 us (19%)
  local copies, waits for them, and re-layouts  2.1 us (6%)
  other arithmetic  0.83 us (2%)
  between operations  0.73 us (2%)
    ppermute x6, waiting for transfers between devices, swap_dp(): return lax.ppermute(value, 'dp', [(i, i ^ masks[i % 2]) for i in range(16)])  8.63 us
    ppermute x6, starting transfers between devices, swap_dp(): return lax.ppermute(value, 'dp', [(i, i ^ masks[i % 2]) for i in range(16)])  6.84 us
    pallas_call x7, Pallas kernels, run(): pl.pallas_call(body, out_shape=tuple((jax.ShapeDtypeStruct(shape, kind) f...  6.31 us
    ppermute x3, starting transfers between devices, swap_x(): return lax.ppermute(value, 'sp', [(0, 1), (1, 0)])  4.61 us
    ppermute x3, waiting for transfers between devices, swap_x(): return lax.ppermute(value, 'sp', [(0, 1), (1, 0)])  3.13 us
    unnamed x12, local copies, waits for them, and re-layouts  2.09 us
    reshape x1, other arithmetic, per_device_pairs(): grad_share = jnp.concatenate(lows + highs).reshape(-1)  0.71 us
  transfers between devices with their start and end apart: 9, of which 8 were waited for; matrix products, arithmetic and copies ran while one was open for 0% of the time, Pallas kernels for 14%

profile of v6, /device:TPU:0, one launch (start us, length us, event | category | flops | bytes accessed | tf_op | source)
XLA Modules:
  0.0 33.2 jit_solution(562360920938239959)
XLA Ops:
  0.6 3.0 %collective-permute-start.1 = (bf16[2,4,8,8,128]{4,3,2,1,0:T(8,128)(2,1)}, bf16[2,4,8,8,128]{4,3,2,1,0:T(8,128)(2,1)S(1)}, u32[]{:S(2)}, u32[]{:S(2)}) collective-permute-start(bf16[2,4,8,8,128]{4,3,2,1,0:T(8,128)(2,1)} %in_ref.1), channel_id=1, source_target_pairs={{0,16},{16,0},{1,17},{17,1},{2,18},{18,2},{3,19},{19,3},{4,20},{20... | collective-permute-start | bytes 393224 | tf_op jit(solution)/shard_map/ppermute | solution.py:141
  3.6 0.1 collective-permute-start
  3.7 1.2 %copy-done = bf16[3456,128]{1,0:T(8,128)(2,1)S(1)} copy-done((bf16[3456,128]{1,0:T(8,128)(2,1)S(1)}, bf16[3456,128]{1,0:T(8,128)(2,1)}, u32[]{:S(2)}) %copy-start) | copy-done | bytes 884760
  4.9 0.9 %copy-done.4 = bf16[2,4,8,8,128]{4,3,2,1,0:T(8,128)(2,1)S(1)} copy-done((bf16[2,4,8,8,128]{4,3,2,1,0:T(8,128)(2,1)S(1)}, bf16[2,4,8,8,128]{4,3,2,1,0:T(8,128)(2,1)}, u32[]{:S(2)}) %copy-start.4) | copy-done | bytes 131096
  5.8 0.8 %shard_map.68 = (f32[6,128,128]{2,1,0:T(8,128)S(1)}, bf16[128,512]{1,0:T(8,128)(2,1)S(1)}) custom-call(bf16[2,4,8,8,128]{4,3,2,1,0:T(8,128)(2,1)S(1)} %copy-done.4, bf16[3456,128]{1,0:T(8,128)(2,1)S(1)} %copy-done), custom_call_target="tpu_custom_call" | custom-call | flops 1000000000 | bytes 2097152 | tf_op jit(solution)/shard_map/pallas_call | solution.py:478
  6.6 1.6 %collective-permute-done.1.in_ref = bf16[2,4,8,8,128]{4,3,2,1,0:T(8,128)(2,1)S(1)} collective-permute-done((bf16[2,4,8,8,128]{4,3,2,1,0:T(8,128)(2,1)}, bf16[2,4,8,8,128]{4,3,2,1,0:T(8,128)(2,1)S(1)}, u32[]{:S(2)}, u32[]{:S(2)}) %collective-permute-start.1) | collective-permute-done | bytes 131104 | tf_op jit(solution)/shard_map/ppermute | solution.py:141
  8.2 0.0 copy-done.1
  8.2 0.0 copy-done.2
  8.2 0.0 copy-done.3
  8.2 1.4 %shard_map.69 = (f32[4,2,4,2,2,8,128]{6,5,4,3,2,1,0:T(8,128)S(1)}, bf16[2,128,512]{2,1,0:T(8,128)(2,1)S(1)}, bf16[1024,128]{1,0:T(8,128)(2,1)S(1)}, bf16[256,128...) custom-call(bf16[2,4,8,8,128]{4,3,2,1,0:T(8,128)(2,1)S(1)} %collective-permute-, ...), custom_call_target="tpu_custom_call" | custom-call | flops 1000000000 | bytes 2097152 | tf_op jit(solution)/shard_map/pallas_call | solution.py:478
  9.6 0.6 %collective-permute-done.up_ref = bf16[2,4,8,8,128]{4,3,2,1,0:T(8,128)(2,1)S(1)} collective-permute-done((bf16[2,4,8,8,128]{4,3,2,1,0:T(8,128)(2,1)}, bf16[2,4,8,8,128]{4,3,2,1,0:T(8,128)(2,1)S(1)}, u32[]{:S(2)}, u32[]{:S(2)}) %collective-permute-start) | collective-permute-done | bytes 131104 | tf_op jit(solution)/shard_map/ppermute | solution.py:141
  10.2 1.7 %shard_map.70 = (bf16[4,240,128]{2,1,0:T(8,128)(2,1)S(1)}, bf16[4,240,128]{2,1,0:T(8,128)(2,1)S(1)}, bf16[4,240,128]{2,1,0:T(8,128)(2,1)S(1)}, bf16[6,8,16,128]{...) custom-call(bf16[2,4,8,8,128]{4,3,2,1,0:T(8,128)(2,1)S(1)} %collective-permute-done.up_ref, ...), custom_call_target="tpu_custom_call" | custom-call | flops 1000000000 | bytes 2097152 | tf_op jit(solution)/shard_map/pallas_call | solution.py:478
  11.8 0.1 collective-permute-start.3
  11.9 0.5 %collective-permute-start.2 = (bf16[4,240,128]{2,1,0:T(8,128)(2,1)S(1)}, bf16[4,240,128]{2,1,0:T(8,128)(2,1)S(1)}, u32[]{:S(2)}, u32[]{:S(2)}) collective-permute-start(bf16[4,240,128]{2,1,0:T(8,128)(2,1)S(1)} %get-tuple-element.34), channel_id=1, source_target_pairs={{0,1},{1,0},{2,3},{3,2},{4,5},{5,4},{6,7},{7,6},{8,9},{9,8},{10,11... | collective-permute-start | bytes 737288 | tf_op jit(solution)/shard_map/ppermute | solution.py:146
  12.4 0.5 %shard_map.72.late_ref = bf16[4,240,128]{2,1,0:T(8,128)(2,1)S(1)} custom-call(bf16[10,10,16,384]{3,2,1,0:T(8,128)(2,1)S(1)} %get-tuple-element.31.taps_ref, bf16[2,128,512]{2,1,0:T(8,128)(2,1)S(1)} %get-tuple-element.24.turned_ref, f32[320,128]{1,0:T(8,128)S(1)} %get-tuple-element.32.down_ref), custom_call_target="tpu_custom_call" | custom-call | flops 1000000000 | bytes 2097152 | tf_op jit(solution)/shard_map/pallas_call | solution.py:478
  13.0 0.5 %collective-permute-done.3.passed_ref = bf16[4,240,128]{2,1,0:T(8,128)(2,1)S(1)} collective-permute-done((bf16[4,240,128]{2,1,0:T(8,128)(2,1)S(1)}, bf16[4,240,128]{2,1,0:T(8,128)(2,1)S(1)}, u32[]{:S(2)}, u32[]{:S(2)}) %collective-permute-start.3) | collective-permute-done | bytes 245792 | tf_op jit(solution)/shard_map/ppermute | solution.py:146
  13.4 0.1 shard_map.74
  13.5 1.8 %collective-permute-start.4 = (bf16[2,240,128]{2,1,0:T(8,128)(2,1)S(1)}, bf16[2,240,128]{2,1,0:T(8,128)(2,1)S(1)}, u32[]{:S(2)}, u32[]{:S(2)}) collective-permute-start(bf16[2,240,128]{2,1,0:T(8,128)(2,1)S(1)} %get-tuple-element.37), channel_id=1, source_target_pairs={{0,2},{1,7},{2,0},{3,5},{4,6},{5,3},{6,4},{7,1},{8,10},{9,15},{10,... | collective-permute-start | bytes 368648 | tf_op jit(solution)/shard_map/ppermute | solution.py:146
  15.3 1.6 %collective-permute-start.5 = (bf16[2,240,128]{2,1,0:T(8,128)(2,1)S(1)}, bf16[2,240,128]{2,1,0:T(8,128)(2,1)S(1)}, u32[]{:S(2)}, u32[]{:S(2)}) collective-permute-start(bf16[2,240,128]{2,1,0:T(8,128)(2,1)S(1)} %get-tuple-element.38), channel_id=1, source_target_pairs={{0,4},{1,3},{2,6},{3,1},{4,0},{5,7},{6,2},{7,5},{8,12},{9,11},{10,... | collective-permute-start | bytes 368648 | tf_op jit(solution)/shard_map/ppermute | solution.py:146
  16.9 0.0 collective-permute-done.2.passed_ref
  16.9 0.1 shard_map.73
  17.0 0.2 collective-permute-start.6
  17.2 3.5 %collective-permute-done.4 = bf16[2,240,128]{2,1,0:T(8,128)(2,1)S(1)} collective-permute-done((bf16[2,240,128]{2,1,0:T(8,128)(2,1)S(1)}, bf16[2,240,128]{2,1,0:T(8,128)(2,1)S(1)}, u32[]{:S(2)}, u32[]{:S(2)}) %collective-permute-start.4) | collective-permute-done | bytes 122912 | tf_op jit(solution)/shard_map/ppermute | solution.py:146
  20.6 0.6 %collective-permute-done.5 = bf16[2,240,128]{2,1,0:T(8,128)(2,1)S(1)} collective-permute-done((bf16[2,240,128]{2,1,0:T(8,128)(2,1)S(1)}, bf16[2,240,128]{2,1,0:T(8,128)(2,1)S(1)}, u32[]{:S(2)}, u32[]{:S(2)}) %collective-permute-start.5) | collective-permute-done | bytes 122912 | tf_op jit(solution)/shard_map/ppermute | solution.py:146
  21.3 1.6 %collective-permute-done.6 = bf16[2,240,128]{2,1,0:T(8,128)(2,1)S(1)} collective-permute-done((bf16[2,240,128]{2,1,0:T(8,128)(2,1)S(1)}, bf16[2,240,128]{2,1,0:T(8,128)(2,1)S(1)}, u32[]{:S(2)}, u32[]{:S(2)}) %collective-permute-start.6) | collective-permute-done | bytes 122912 | tf_op jit(solution)/shard_map/ppermute | solution.py:146
  22.8 0.1 convert_add_fusion
  22.9 2.7 %collective-permute-start.7 = (bf16[240,128]{1,0:T(8,128)(2,1)S(1)}, bf16[240,128]{1,0:T(8,128)(2,1)S(1)}, u32[]{:S(2)}, u32[]{:S(2)}) collective-permute-start(bf16[240,128]{1,0:T(8,128)(2,1)S(1)} %fusion.1), channel_id=1, source_target_pairs={{0,8},{1,9},{2,10},{3,11},{4,12},{5,13},{6,14},{7,15},{8,0},{9,1},... | collective-permute-start | bytes 184328 | tf_op jit(solution)/shard_map/ppermute | solution.py:146
  25.6 2.5 %collective-permute-done.7 = bf16[240,128]{1,0:T(8,128)(2,1)S(1)} collective-permute-done((bf16[240,128]{1,0:T(8,128)(2,1)S(1)}, bf16[240,128]{1,0:T(8,128)(2,1)S(1)}, u32[]{:S(2)}, u32[]{:S(2)}) %collective-permute-start.7) | collective-permute-done | bytes 61472 | tf_op jit(solution)/shard_map/ppermute | solution.py:146
  28.1 1.5 %collective-permute-start.8 = (bf16[240,128]{1,0:T(8,128)(2,1)S(1)}, bf16[240,128]{1,0:T(8,128)(2,1)S(1)}, u32[]{:S(2)}, u32[]{:S(2)}) collective-permute-start(bf16[240,128]{1,0:T(8,128)(2,1)S(1)} %fusion), channel_id=1, source_target_pairs={{0,16},{16,0},{1,17},{17,1},{2,18},{18,2},{3,19},{19,3},{4,20},{20... | collective-permute-start | bytes 184328 | tf_op jit(solution)/shard_map/ppermute | solution.py:141
  29.6 1.8 %shard_map.71 = bf16[2,4,8,8,128]{4,3,2,1,0:T(8,128)(2,1)} custom-call(bf16[6,8,16,128]{3,2,1,0:T(8,128)(2,1)S(1)} %get-tuple-element.30.slab_ref, bf16[3456,128]{1,0:T(8,128)(2,1)S(1)} %copy-done.1), custom_call_target="tpu_custom_call" | custom-call | flops 1000000000 | bytes 2097152 | tf_op jit(solution)/shard_map/pallas_call | solution.py:478
  31.4 1.0 %collective-permute-done.8 = bf16[240,128]{1,0:T(8,128)(2,1)S(1)} collective-permute-done((bf16[240,128]{1,0:T(8,128)(2,1)S(1)}, bf16[240,128]{1,0:T(8,128)(2,1)S(1)}, u32[]{:S(2)}, u32[]{:S(2)}) %collective-permute-start.8) | collective-permute-done | bytes 61472 | tf_op jit(solution)/shard_map/ppermute | solution.py:141
  32.5 0.7 %maximum_bitcast_fusion = f32[60416]{0:T(1024)} fusion(f32[232,128]{1,0:T(8,128)S(1)} %convert_multiply_fusion.1, f32[240,128]{1,0:T(8,128)S(1)} %convert_multiply_fusion), kind=kLoop, calls=%fused_computation.1 | loop fusion | flops 60416 | bytes 483328 | tf_op jit(solution)/shard_map/reshape | solution.py:579
  (11 shorter events, 0.1 us)
Async XLA Ops:
  0.6 7.5 %collective-permute-start.1 = (bf16[2,4,8,8,128]{4,3,2,1,0:T(8,128)(2,1)}, bf16[2,4,8,8,128]{4,3,2,1,0:T(8,128)(2,1)S(1)}, u32[]{:S(2)}, u32[]{:S(2)}) collective-permute-start(bf16[2,4,8,8,128]{4,3,2,1,0:T(8,128)(2,1)} %in_ref.1), channel_id=1, source_target_pairs={{0,16},{16,0},{1,17},{17,1},{2,18},{18,2},{3,19},{19,3},{4,20},{20... | collective-permute-start | bytes 393224 | tf_op jit(solution)/shard_map/ppermute | solution.py:141
  3.6 6.5 %collective-permute-start = (bf16[2,4,8,8,128]{4,3,2,1,0:T(8,128)(2,1)}, bf16[2,4,8,8,128]{4,3,2,1,0:T(8,128)(2,1)S(1)}, u32[]{:S(2)}, u32[]{:S(2)}) collective-permute-start(bf16[2,4,8,8,128]{4,3,2,1,0:T(8,128)(2,1)} %up_ref.1), channel_id=1, source_target_pairs={{0,16},{16,0},{1,17},{17,1},{2,18},{18,2},{3,19},{19,3},{4,20},{20... | collective-permute-start | bytes 393224 | tf_op jit(solution)/shard_map/ppermute | solution.py:141
  3.7 1.2 %copy-start = (bf16[3456,128]{1,0:T(8,128)(2,1)S(1)}, bf16[3456,128]{1,0:T(8,128)(2,1)}, u32[]{:S(2)}) copy-start(bf16[3456,128]{1,0:T(8,128)(2,1)} %w_ref.5) | copy-start | bytes 2654212
  4.9 0.9 %copy-start.4 = (bf16[2,4,8,8,128]{4,3,2,1,0:T(8,128)(2,1)S(1)}, bf16[2,4,8,8,128]{4,3,2,1,0:T(8,128)(2,1)}, u32[]{:S(2)}) copy-start(bf16[2,4,8,8,128]{4,3,2,1,0:T(8,128)(2,1)} %in_ref.1) | copy-start | bytes 393220
  5.8 2.4 %copy-start.1 = (bf16[3456,128]{1,0:T(8,128)(2,1)S(1)}, bf16[3456,128]{1,0:T(8,128)(2,1)}, u32[]{:S(2)}) copy-start(bf16[3456,128]{1,0:T(8,128)(2,1)} %w_ref.5) | copy-start | bytes 2654212
  5.8 2.4 %copy-start.2 = (bf16[1024,256]{1,0:T(8,128)(2,1)S(1)}, bf16[1024,256]{1,0:T(8,128)(2,1)}, u32[]{:S(2)}) copy-start(bf16[1024,256]{1,0:T(8,128)(2,1)} %w_down_ref.3) | copy-start | bytes 1572868
  5.8 2.4 %copy-start.3 = (bf16[2048,128]{1,0:T(8,128)(2,1)S(1)}, bf16[2048,128]{1,0:T(8,128)(2,1)}, u32[]{:S(2)}) copy-start(bf16[2048,128]{1,0:T(8,128)(2,1)} %w_up_ref.3) | copy-start | bytes 1572868
  5.8 2.4 %copy-start.5 = (bf16[2,4,8,8,128]{4,3,2,1,0:T(8,128)(2,1)S(1)}, bf16[2,4,8,8,128]{4,3,2,1,0:T(8,128)(2,1)}, u32[]{:S(2)}) copy-start(bf16[2,4,8,8,128]{4,3,2,1,0:T(8,128)(2,1)} %up_ref.1) | copy-start | bytes 393220
  11.8 1.6 %collective-permute-start.3 = (bf16[4,240,128]{2,1,0:T(8,128)(2,1)S(1)}, bf16[4,240,128]{2,1,0:T(8,128)(2,1)S(1)}, u32[]{:S(2)}, u32[]{:S(2)}) collective-permute-start(bf16[4,240,128]{2,1,0:T(8,128)(2,1)S(1)} %get-tuple-element.36), channel_id=1, source_target_pairs={{0,1},{1,0},{2,3},{3,2},{4,5},{5,4},{6,7},{7,6},{8,9},{9,8},{10,11... | collective-permute-start | bytes 737288 | tf_op jit(solution)/shard_map/ppermute | solution.py:146
  11.9 5.0 %collective-permute-start.2 = (bf16[4,240,128]{2,1,0:T(8,128)(2,1)S(1)}, bf16[4,240,128]{2,1,0:T(8,128)(2,1)S(1)}, u32[]{:S(2)}, u32[]{:S(2)}) collective-permute-start(bf16[4,240,128]{2,1,0:T(8,128)(2,1)S(1)} %get-tuple-element.34), channel_id=1, source_target_pairs={{0,1},{1,0},{2,3},{3,2},{4,5},{5,4},{6,7},{7,6},{8,9},{9,8},{10,11... | collective-permute-start | bytes 737288 | tf_op jit(solution)/shard_map/ppermute | solution.py:146
  13.5 7.2 %collective-permute-start.4 = (bf16[2,240,128]{2,1,0:T(8,128)(2,1)S(1)}, bf16[2,240,128]{2,1,0:T(8,128)(2,1)S(1)}, u32[]{:S(2)}, u32[]{:S(2)}) collective-permute-start(bf16[2,240,128]{2,1,0:T(8,128)(2,1)S(1)} %get-tuple-element.37), channel_id=1, source_target_pairs={{0,2},{1,7},{2,0},{3,5},{4,6},{5,3},{6,4},{7,1},{8,10},{9,15},{10,... | collective-permute-start | bytes 368648 | tf_op jit(solution)/shard_map/ppermute | solution.py:146
  15.3 5.9 %collective-permute-start.5 = (bf16[2,240,128]{2,1,0:T(8,128)(2,1)S(1)}, bf16[2,240,128]{2,1,0:T(8,128)(2,1)S(1)}, u32[]{:S(2)}, u32[]{:S(2)}) collective-permute-start(bf16[2,240,128]{2,1,0:T(8,128)(2,1)S(1)} %get-tuple-element.38), channel_id=1, source_target_pairs={{0,4},{1,3},{2,6},{3,1},{4,0},{5,7},{6,2},{7,5},{8,12},{9,11},{10,... | collective-permute-start | bytes 368648 | tf_op jit(solution)/shard_map/ppermute | solution.py:146
  17.0 5.8 %collective-permute-start.6 = (bf16[2,240,128]{2,1,0:T(8,128)(2,1)S(1)}, bf16[2,240,128]{2,1,0:T(8,128)(2,1)S(1)}, u32[]{:S(2)}, u32[]{:S(2)}) collective-permute-start(bf16[2,240,128]{2,1,0:T(8,128)(2,1)S(1)} %get-tuple-element.39), channel_id=1, source_target_pairs={{0,6},{1,5},{2,4},{3,7},{4,2},{5,1},{6,0},{7,3},{8,14},{9,13},{10,... | collective-permute-start | bytes 368648 | tf_op jit(solution)/shard_map/ppermute | solution.py:146
  22.9 5.2 %collective-permute-start.7 = (bf16[240,128]{1,0:T(8,128)(2,1)S(1)}, bf16[240,128]{1,0:T(8,128)(2,1)S(1)}, u32[]{:S(2)}, u32[]{:S(2)}) collective-permute-start(bf16[240,128]{1,0:T(8,128)(2,1)S(1)} %fusion.1), channel_id=1, source_target_pairs={{0,8},{1,9},{2,10},{3,11},{4,12},{5,13},{6,14},{7,15},{8,0},{9,1},... | collective-permute-start | bytes 184328 | tf_op jit(solution)/shard_map/ppermute | solution.py:146
  28.1 4.3 %collective-permute-start.8 = (bf16[240,128]{1,0:T(8,128)(2,1)S(1)}, bf16[240,128]{1,0:T(8,128)(2,1)S(1)}, u32[]{:S(2)}, u32[]{:S(2)}) collective-permute-start(bf16[240,128]{1,0:T(8,128)(2,1)S(1)} %fusion), channel_id=1, source_target_pairs={{0,16},{16,0},{1,17},{17,1},{2,18},{18,2},{3,19},{19,3},{4,20},{20... | collective-permute-start | bytes 184328 | tf_op jit(solution)/shard_map/ppermute | solution.py:141

commit v7 on v6

--- a/solution.py
+++ b/solution.py
@@ -327,7 +327,6 @@
     mine_ref,
     first_ref,
     rest_ref,
-    slab_ref,
     taps_ref,
     down_ref,
     natural_ref,
@@ -359,9 +358,6 @@
         folded_ref[:, :, :, :, 0].reshape(whole),
         folded_ref[:, :, :, :, 1].reshape(whole),
     )
-    slab_ref[...] = taps_ref[
-        pl.ds(side * (planes // 2), planes // 2 + 2), 1:9, :, LANES : 2 * LANES
-    ]
 
     deep = deep_act_ref.shape[0]
     grad_up = dot(deep_act_ref[...], upstream)
@@ -452,12 +448,10 @@
             target[far] = total.astype(target.dtype)
 
 
-def input_kernel(slab_ref, w_ref, out_ref, taps_ref, natural_ref):
-    slab = slab_ref[...].astype(F32)
-    own = slab.shape[0] - 2
+def input_kernel(taps_ref, w_ref, out_ref, natural_ref):
+    own = out_ref.shape[1]
     size = own * 128
-    clear_rim(taps_ref, False)
-    fill_taps(taps_ref, slab[:, :, :8], slab[:, :, 8:])
+    first_plane = lax.axis_index("sp") * own
     total = jnp.zeros((size, LANES), F32)
     for i in range(3):
         for j in range(3):
@@ -465,7 +459,7 @@
             weights = across(
                 [w_ref[(first - k) * LANES : (first - k + 1) * LANES, :] for k in range(3)]
             )
-            cells = taps_ref[1 + i : 1 + i + own, j : j + 8].reshape(size, 3 * LANES)
+            cells = taps_ref[pl.ds(first_plane + i, own), j : j + 8].reshape(size, 3 * LANES)
             total += against(cells, weights)
     total = total.reshape(own, 8, 2, 8, LANES)
     for parity in range(2):
@@ -522,14 +516,13 @@
     taps = ((10, 10, 16, 3 * LANES), BF16)
     given = ((4, HALF, LANES), BF16)
     down = ((8 * SHARE - conv_count, LANES), F32)
-    early_mine, first, rest, slab, grad_taps, down_rows = run(
+    early_mine, first, rest, grad_taps, down_rows = run(
         backward_kernel,
         (other_up, *saved, w_down, w_up),
         [
             given,
             ((2 * EARLY, HALF, LANES), BF16),
             ((8 - 2 * EARLY, HALF, LANES), BF16),
-            ((6, 8, 16, LANES), BF16),
             taps,
             down,
         ],
@@ -551,9 +544,9 @@
     )
     (grad_input,) = run(
         input_kernel,
-        (slab, w_conv),
+        (grad_taps, w_conv),
         [(inputs.shape, BF16)],
-        [((8, 10, 16, 3 * LANES), BF16), natural],
+        [natural],
         10**9,
     )
 

time: 33.3 us -> 33.3 us (level)
  no operation moved by 1% of the time
where the time goes in v7:
time: 33.3 us; the launch traced here: 33.1 us
  waiting for transfers between devices  11.8 us (35%)
  starting transfers between devices  11.4 us (34%)
  Pallas kernels  6.28 us (19%)
  local copies, waits for them, and re-layouts  2.1 us (6%)
  other arithmetic  0.83 us (2%)
  between operations  0.73 us (2%)
    ppermute x6, waiting for transfers between devices, swap_dp(): return lax.ppermute(value, 'dp', [(i, i ^ masks[i % 2]) for i in range(16)])  8.63 us
    ppermute x6, starting transfers between devices, swap_dp(): return lax.ppermute(value, 'dp', [(i, i ^ masks[i % 2]) for i in range(16)])  6.84 us
    pallas_call x7, Pallas kernels, run(): pl.pallas_call(body, out_shape=tuple((jax.ShapeDtypeStruct(shape, kind) f...  6.28 us
    ppermute x3, starting transfers between devices, swap_x(): return lax.ppermute(value, 'sp', [(0, 1), (1, 0)])  4.61 us
    ppermute x3, waiting for transfers between devices, swap_x(): return lax.ppermute(value, 'sp', [(0, 1), (1, 0)])  3.12 us
    unnamed x12, local copies, waits for them, and re-layouts  2.09 us
    reshape x1, other arithmetic, per_device_pairs(): grad_share = jnp.concatenate(lows + highs).reshape(-1)  0.71 us
  transfers between devices with their start and end apart: 9, of which 8 were waited for; matrix products, arithmetic and copies ran while one was open for 0% of the time, Pallas kernels for 14%

profile of v7, /device:TPU:0, one launch (start us, length us, event | category | flops | bytes accessed | tf_op | source)
XLA Modules:
  0.0 33.1 jit_solution(5753024413914714170)
XLA Ops:
  0.6 3.0 %collective-permute-start.1 = (bf16[2,4,8,8,128]{4,3,2,1,0:T(8,128)(2,1)}, bf16[2,4,8,8,128]{4,3,2,1,0:T(8,128)(2,1)S(1)}, u32[]{:S(2)}, u32[]{:S(2)}) collective-permute-start(bf16[2,4,8,8,128]{4,3,2,1,0:T(8,128)(2,1)} %in_ref.1), channel_id=1, source_target_pairs={{0,16},{16,0},{1,17},{17,1},{2,18},{18,2},{3,19},{19,3},{4,20},{20... | collective-permute-start | bytes 393224 | tf_op jit(solution)/shard_map/ppermute | solution.py:141
  3.6 0.1 collective-permute-start
  3.7 1.2 %copy-done = bf16[3456,128]{1,0:T(8,128)(2,1)S(1)} copy-done((bf16[3456,128]{1,0:T(8,128)(2,1)S(1)}, bf16[3456,128]{1,0:T(8,128)(2,1)}, u32[]{:S(2)}) %copy-start) | copy-done | bytes 884760
  4.9 0.9 %copy-done.4 = bf16[2,4,8,8,128]{4,3,2,1,0:T(8,128)(2,1)S(1)} copy-done((bf16[2,4,8,8,128]{4,3,2,1,0:T(8,128)(2,1)S(1)}, bf16[2,4,8,8,128]{4,3,2,1,0:T(8,128)(2,1)}, u32[]{:S(2)}) %copy-start.4) | copy-done | bytes 131096
  5.8 0.8 %shard_map.68 = (f32[6,128,128]{2,1,0:T(8,128)S(1)}, bf16[128,512]{1,0:T(8,128)(2,1)S(1)}) custom-call(bf16[2,4,8,8,128]{4,3,2,1,0:T(8,128)(2,1)S(1)} %copy-done.4, bf16[3456,128]{1,0:T(8,128)(2,1)S(1)} %copy-done), custom_call_target="tpu_custom_call" | custom-call | flops 1000000000 | bytes 2097152 | tf_op jit(solution)/shard_map/pallas_call | solution.py:472
  6.6 1.6 %collective-permute-done.1.in_ref = bf16[2,4,8,8,128]{4,3,2,1,0:T(8,128)(2,1)S(1)} collective-permute-done((bf16[2,4,8,8,128]{4,3,2,1,0:T(8,128)(2,1)}, bf16[2,4,8,8,128]{4,3,2,1,0:T(8,128)(2,1)S(1)}, u32[]{:S(2)}, u32[]{:S(2)}) %collective-permute-start.1) | collective-permute-done | bytes 131104 | tf_op jit(solution)/shard_map/ppermute | solution.py:141
  8.2 0.0 copy-done.1
  8.2 0.0 copy-done.2
  8.2 0.0 copy-done.5
  8.2 1.4 %shard_map.69 = (f32[4,2,4,2,2,8,128]{6,5,4,3,2,1,0:T(8,128)S(1)}, bf16[2,128,512]{2,1,0:T(8,128)(2,1)S(1)}, bf16[1024,128]{1,0:T(8,128)(2,1)S(1)}, bf16[256,128...) custom-call(bf16[2,4,8,8,128]{4,3,2,1,0:T(8,128)(2,1)S(1)} %collective-permute-, ...), custom_call_target="tpu_custom_call" | custom-call | flops 1000000000 | bytes 2097152 | tf_op jit(solution)/shard_map/pallas_call | solution.py:472
  9.6 0.6 %collective-permute-done.up_ref = bf16[2,4,8,8,128]{4,3,2,1,0:T(8,128)(2,1)S(1)} collective-permute-done((bf16[2,4,8,8,128]{4,3,2,1,0:T(8,128)(2,1)}, bf16[2,4,8,8,128]{4,3,2,1,0:T(8,128)(2,1)S(1)}, u32[]{:S(2)}, u32[]{:S(2)}) %collective-permute-start) | collective-permute-done | bytes 131104 | tf_op jit(solution)/shard_map/ppermute | solution.py:141
  10.2 1.7 %shard_map.70 = (bf16[4,240,128]{2,1,0:T(8,128)(2,1)S(1)}, bf16[4,240,128]{2,1,0:T(8,128)(2,1)S(1)}, bf16[4,240,128]{2,1,0:T(8,128)(2,1)S(1)}, bf16[10,10,16,384]{3,2,1,0:T(8,128)(2,1)S(1)}, f32[320,128]{1,0:T(8,128)S(1)}) custom-call(bf16[2,4,8,8,128]{4,3,2,1,0:T(8,128)(2,1)S(1)} %collective-permute-done.up_ref, ...), custom_call_target="tpu_custom_call" | custom-call | flops 1000000000 | bytes 2097152 | tf_op jit(solution)/shard_map/pallas_call | solution.py:472
  11.8 0.1 collective-permute-start.3
  11.9 0.5 %collective-permute-start.2 = (bf16[4,240,128]{2,1,0:T(8,128)(2,1)S(1)}, bf16[4,240,128]{2,1,0:T(8,128)(2,1)S(1)}, u32[]{:S(2)}, u32[]{:S(2)}) collective-permute-start(bf16[4,240,128]{2,1,0:T(8,128)(2,1)S(1)} %get-tuple-element.32), channel_id=1, source_target_pairs={{0,1},{1,0},{2,3},{3,2},{4,5},{5,4},{6,7},{7,6},{8,9},{9,8},{10,11... | collective-permute-start | bytes 737288 | tf_op jit(solution)/shard_map/ppermute | solution.py:146
  12.4 0.5 %shard_map.72.late_ref = bf16[4,240,128]{2,1,0:T(8,128)(2,1)S(1)} custom-call(bf16[10,10,16,384]{3,2,1,0:T(8,128)(2,1)S(1)} %get-tuple-element.29.taps_ref, bf16[2,128,512]{2,1,0:T(8,128)(2,1)S(1)} %get-tuple-element.23.turned_ref, f32[320,128]{1,0:T(8,128)S(1)} %get-tuple-element.30.down_ref), custom_call_target="tpu_custom_call" | custom-call | flops 1000000000 | bytes 2097152 | tf_op jit(solution)/shard_map/pallas_call | solution.py:472
  12.9 0.5 %collective-permute-done.3.passed_ref = bf16[4,240,128]{2,1,0:T(8,128)(2,1)S(1)} collective-permute-done((bf16[4,240,128]{2,1,0:T(8,128)(2,1)S(1)}, bf16[4,240,128]{2,1,0:T(8,128)(2,1)S(1)}, u32[]{:S(2)}, u32[]{:S(2)}) %collective-permute-start.3) | collective-permute-done | bytes 245792 | tf_op jit(solution)/shard_map/ppermute | solution.py:146
  13.4 0.1 shard_map.74
  13.5 1.8 %collective-permute-start.4 = (bf16[2,240,128]{2,1,0:T(8,128)(2,1)S(1)}, bf16[2,240,128]{2,1,0:T(8,128)(2,1)S(1)}, u32[]{:S(2)}, u32[]{:S(2)}) collective-permute-start(bf16[2,240,128]{2,1,0:T(8,128)(2,1)S(1)} %get-tuple-element.35), channel_id=1, source_target_pairs={{0,2},{1,7},{2,0},{3,5},{4,6},{5,3},{6,4},{7,1},{8,10},{9,15},{10,... | collective-permute-start | bytes 368648 | tf_op jit(solution)/shard_map/ppermute | solution.py:146
  15.3 1.6 %collective-permute-start.5 = (bf16[2,240,128]{2,1,0:T(8,128)(2,1)S(1)}, bf16[2,240,128]{2,1,0:T(8,128)(2,1)S(1)}, u32[]{:S(2)}, u32[]{:S(2)}) collective-permute-start(bf16[2,240,128]{2,1,0:T(8,128)(2,1)S(1)} %get-tuple-element.36), channel_id=1, source_target_pairs={{0,4},{1,3},{2,6},{3,1},{4,0},{5,7},{6,2},{7,5},{8,12},{9,11},{10,... | collective-permute-start | bytes 368648 | tf_op jit(solution)/shard_map/ppermute | solution.py:146
  16.9 0.0 collective-permute-done.2.passed_ref
  16.9 0.1 shard_map.73
  17.0 0.2 collective-permute-start.6
  17.2 3.5 %collective-permute-done.4 = bf16[2,240,128]{2,1,0:T(8,128)(2,1)S(1)} collective-permute-done((bf16[2,240,128]{2,1,0:T(8,128)(2,1)S(1)}, bf16[2,240,128]{2,1,0:T(8,128)(2,1)S(1)}, u32[]{:S(2)}, u32[]{:S(2)}) %collective-permute-start.4) | collective-permute-done | bytes 122912 | tf_op jit(solution)/shard_map/ppermute | solution.py:146
  20.6 0.6 %collective-permute-done.5 = bf16[2,240,128]{2,1,0:T(8,128)(2,1)S(1)} collective-permute-done((bf16[2,240,128]{2,1,0:T(8,128)(2,1)S(1)}, bf16[2,240,128]{2,1,0:T(8,128)(2,1)S(1)}, u32[]{:S(2)}, u32[]{:S(2)}) %collective-permute-start.5) | collective-permute-done | bytes 122912 | tf_op jit(solution)/shard_map/ppermute | solution.py:146
  21.2 1.6 %collective-permute-done.6 = bf16[2,240,128]{2,1,0:T(8,128)(2,1)S(1)} collective-permute-done((bf16[2,240,128]{2,1,0:T(8,128)(2,1)S(1)}, bf16[2,240,128]{2,1,0:T(8,128)(2,1)S(1)}, u32[]{:S(2)}, u32[]{:S(2)}) %collective-permute-start.6) | collective-permute-done | bytes 122912 | tf_op jit(solution)/shard_map/ppermute | solution.py:146
  22.8 0.1 convert_add_fusion
  22.9 2.7 %collective-permute-start.7 = (bf16[240,128]{1,0:T(8,128)(2,1)S(1)}, bf16[240,128]{1,0:T(8,128)(2,1)S(1)}, u32[]{:S(2)}, u32[]{:S(2)}) collective-permute-start(bf16[240,128]{1,0:T(8,128)(2,1)S(1)} %fusion.1), channel_id=1, source_target_pairs={{0,8},{1,9},{2,10},{3,11},{4,12},{5,13},{6,14},{7,15},{8,0},{9,1},... | collective-permute-start | bytes 184328 | tf_op jit(solution)/shard_map/ppermute | solution.py:146
  25.5 2.5 %collective-permute-done.7 = bf16[240,128]{1,0:T(8,128)(2,1)S(1)} collective-permute-done((bf16[240,128]{1,0:T(8,128)(2,1)S(1)}, bf16[240,128]{1,0:T(8,128)(2,1)S(1)}, u32[]{:S(2)}, u32[]{:S(2)}) %collective-permute-start.7) | collective-permute-done | bytes 61472 | tf_op jit(solution)/shard_map/ppermute | solution.py:146
  28.1 1.5 %collective-permute-start.8 = (bf16[240,128]{1,0:T(8,128)(2,1)S(1)}, bf16[240,128]{1,0:T(8,128)(2,1)S(1)}, u32[]{:S(2)}, u32[]{:S(2)}) collective-permute-start(bf16[240,128]{1,0:T(8,128)(2,1)S(1)} %fusion), channel_id=1, source_target_pairs={{0,16},{16,0},{1,17},{17,1},{2,18},{18,2},{3,19},{19,3},{4,20},{20... | collective-permute-start | bytes 184328 | tf_op jit(solution)/shard_map/ppermute | solution.py:141
  29.6 1.8 %shard_map.71 = bf16[2,4,8,8,128]{4,3,2,1,0:T(8,128)(2,1)} custom-call(bf16[10,10,16,384]{3,2,1,0:T(8,128)(2,1)S(1)} %get-tuple-element.29.taps_ref, bf16[3456,128]{1,0:T(8,128)(2,1)S(1)} %copy-done.1), custom_call_target="tpu_custom_call" | custom-call | flops 1000000000 | bytes 2097152 | tf_op jit(solution)/shard_map/pallas_call | solution.py:472
  31.4 1.0 %collective-permute-done.8 = bf16[240,128]{1,0:T(8,128)(2,1)S(1)} collective-permute-done((bf16[240,128]{1,0:T(8,128)(2,1)S(1)}, bf16[240,128]{1,0:T(8,128)(2,1)S(1)}, u32[]{:S(2)}, u32[]{:S(2)}) %collective-permute-start.8) | collective-permute-done | bytes 61472 | tf_op jit(solution)/shard_map/ppermute | solution.py:141
  32.4 0.7 %maximum_bitcast_fusion = f32[60416]{0:T(1024)} fusion(f32[232,128]{1,0:T(8,128)S(1)} %convert_multiply_fusion.1, f32[240,128]{1,0:T(8,128)S(1)} %convert_multiply_fusion), kind=kLoop, calls=%fused_computation.1 | loop fusion | flops 60416 | bytes 483328 | tf_op jit(solution)/shard_map/reshape | solution.py:572
  (11 shorter events, 0.1 us)
Async XLA Ops:
  0.6 7.5 %collective-permute-start.1 = (bf16[2,4,8,8,128]{4,3,2,1,0:T(8,128)(2,1)}, bf16[2,4,8,8,128]{4,3,2,1,0:T(8,128)(2,1)S(1)}, u32[]{:S(2)}, u32[]{:S(2)}) collective-permute-start(bf16[2,4,8,8,128]{4,3,2,1,0:T(8,128)(2,1)} %in_ref.1), channel_id=1, source_target_pairs={{0,16},{16,0},{1,17},{17,1},{2,18},{18,2},{3,19},{19,3},{4,20},{20... | collective-permute-start | bytes 393224 | tf_op jit(solution)/shard_map/ppermute | solution.py:141
  3.6 6.5 %collective-permute-start = (bf16[2,4,8,8,128]{4,3,2,1,0:T(8,128)(2,1)}, bf16[2,4,8,8,128]{4,3,2,1,0:T(8,128)(2,1)S(1)}, u32[]{:S(2)}, u32[]{:S(2)}) collective-permute-start(bf16[2,4,8,8,128]{4,3,2,1,0:T(8,128)(2,1)} %up_ref.1), channel_id=1, source_target_pairs={{0,16},{16,0},{1,17},{17,1},{2,18},{18,2},{3,19},{19,3},{4,20},{20... | collective-permute-start | bytes 393224 | tf_op jit(solution)/shard_map/ppermute | solution.py:141
  3.7 1.2 %copy-start = (bf16[3456,128]{1,0:T(8,128)(2,1)S(1)}, bf16[3456,128]{1,0:T(8,128)(2,1)}, u32[]{:S(2)}) copy-start(bf16[3456,128]{1,0:T(8,128)(2,1)} %w_ref.5) | copy-start | bytes 2654212
  4.9 0.9 %copy-start.4 = (bf16[2,4,8,8,128]{4,3,2,1,0:T(8,128)(2,1)S(1)}, bf16[2,4,8,8,128]{4,3,2,1,0:T(8,128)(2,1)}, u32[]{:S(2)}) copy-start(bf16[2,4,8,8,128]{4,3,2,1,0:T(8,128)(2,1)} %in_ref.1) | copy-start | bytes 393220
  5.8 2.4 %copy-start.1 = (bf16[3456,128]{1,0:T(8,128)(2,1)S(1)}, bf16[3456,128]{1,0:T(8,128)(2,1)}, u32[]{:S(2)}) copy-start(bf16[3456,128]{1,0:T(8,128)(2,1)} %w_ref.5) | copy-start | bytes 2654212
  5.8 2.4 %copy-start.2 = (bf16[1024,256]{1,0:T(8,128)(2,1)S(1)}, bf16[1024,256]{1,0:T(8,128)(2,1)}, u32[]{:S(2)}) copy-start(bf16[1024,256]{1,0:T(8,128)(2,1)} %w_down_ref.3) | copy-start | bytes 1572868
  5.8 2.4 %copy-start.3 = (bf16[2048,128]{1,0:T(8,128)(2,1)S(1)}, bf16[2048,128]{1,0:T(8,128)(2,1)}, u32[]{:S(2)}) copy-start(bf16[2048,128]{1,0:T(8,128)(2,1)} %w_up_ref.3) | copy-start | bytes 1572868
  5.8 2.4 %copy-start.5 = (bf16[2,4,8,8,128]{4,3,2,1,0:T(8,128)(2,1)S(1)}, bf16[2,4,8,8,128]{4,3,2,1,0:T(8,128)(2,1)}, u32[]{:S(2)}) copy-start(bf16[2,4,8,8,128]{4,3,2,1,0:T(8,128)(2,1)} %up_ref.1) | copy-start | bytes 393220
  11.8 1.6 %collective-permute-start.3 = (bf16[4,240,128]{2,1,0:T(8,128)(2,1)S(1)}, bf16[4,240,128]{2,1,0:T(8,128)(2,1)S(1)}, u32[]{:S(2)}, u32[]{:S(2)}) collective-permute-start(bf16[4,240,128]{2,1,0:T(8,128)(2,1)S(1)} %get-tuple-element.34), channel_id=1, source_target_pairs={{0,1},{1,0},{2,3},{3,2},{4,5},{5,4},{6,7},{7,6},{8,9},{9,8},{10,11... | collective-permute-start | bytes 737288 | tf_op jit(solution)/shard_map/ppermute | solution.py:146
  11.9 5.0 %collective-permute-start.2 = (bf16[4,240,128]{2,1,0:T(8,128)(2,1)S(1)}, bf16[4,240,128]{2,1,0:T(8,128)(2,1)S(1)}, u32[]{:S(2)}, u32[]{:S(2)}) collective-permute-start(bf16[4,240,128]{2,1,0:T(8,128)(2,1)S(1)} %get-tuple-element.32), channel_id=1, source_target_pairs={{0,1},{1,0},{2,3},{3,2},{4,5},{5,4},{6,7},{7,6},{8,9},{9,8},{10,11... | collective-permute-start | bytes 737288 | tf_op jit(solution)/shard_map/ppermute | solution.py:146
  13.5 7.2 %collective-permute-start.4 = (bf16[2,240,128]{2,1,0:T(8,128)(2,1)S(1)}, bf16[2,240,128]{2,1,0:T(8,128)(2,1)S(1)}, u32[]{:S(2)}, u32[]{:S(2)}) collective-permute-start(bf16[2,240,128]{2,1,0:T(8,128)(2,1)S(1)} %get-tuple-element.35), channel_id=1, source_target_pairs={{0,2},{1,7},{2,0},{3,5},{4,6},{5,3},{6,4},{7,1},{8,10},{9,15},{10,... | collective-permute-start | bytes 368648 | tf_op jit(solution)/shard_map/ppermute | solution.py:146
  15.3 5.9 %collective-permute-start.5 = (bf16[2,240,128]{2,1,0:T(8,128)(2,1)S(1)}, bf16[2,240,128]{2,1,0:T(8,128)(2,1)S(1)}, u32[]{:S(2)}, u32[]{:S(2)}) collective-permute-start(bf16[2,240,128]{2,1,0:T(8,128)(2,1)S(1)} %get-tuple-element.36), channel_id=1, source_target_pairs={{0,4},{1,3},{2,6},{3,1},{4,0},{5,7},{6,2},{7,5},{8,12},{9,11},{10,... | collective-permute-start | bytes 368648 | tf_op jit(solution)/shard_map/ppermute | solution.py:146
  17.0 5.8 %collective-permute-start.6 = (bf16[2,240,128]{2,1,0:T(8,128)(2,1)S(1)}, bf16[2,240,128]{2,1,0:T(8,128)(2,1)S(1)}, u32[]{:S(2)}, u32[]{:S(2)}) collective-permute-start(bf16[2,240,128]{2,1,0:T(8,128)(2,1)S(1)} %get-tuple-element.37), channel_id=1, source_target_pairs={{0,6},{1,5},{2,4},{3,7},{4,2},{5,1},{6,0},{7,3},{8,14},{9,13},{10,... | collective-permute-start | bytes 368648 | tf_op jit(solution)/shard_map/ppermute | solution.py:146
  22.9 5.2 %collective-permute-start.7 = (bf16[240,128]{1,0:T(8,128)(2,1)S(1)}, bf16[240,128]{1,0:T(8,128)(2,1)S(1)}, u32[]{:S(2)}, u32[]{:S(2)}) collective-permute-start(bf16[240,128]{1,0:T(8,128)(2,1)S(1)} %fusion.1), channel_id=1, source_target_pairs={{0,8},{1,9},{2,10},{3,11},{4,12},{5,13},{6,14},{7,15},{8,0},{9,1},... | collective-permute-start | bytes 184328 | tf_op jit(solution)/shard_map/ppermute | solution.py:146
  28.1 4.3 %collective-permute-start.8 = (bf16[240,128]{1,0:T(8,128)(2,1)S(1)}, bf16[240,128]{1,0:T(8,128)(2,1)S(1)}, u32[]{:S(2)}, u32[]{:S(2)}) collective-permute-start(bf16[240,128]{1,0:T(8,128)(2,1)S(1)} %fusion), channel_id=1, source_target_pairs={{0,16},{16,0},{1,17},{17,1},{2,18},{18,2},{3,19},{19,3},{4,20},{20... | collective-permute-start | bytes 184328 | tf_op jit(solution)/shard_map/ppermute | solution.py:141
